TPU v7x, 512 devices: a whole 4x8x8 slice. The times are simulated.
512 devices in a mesh: prov: 32 (over z_lo, y), month: 2 (over core), bin: 8 (over x, z_hi).
Axes of the slice: x: 4, y: 8, z: 8 (z_hi: 2, z_lo: 4; z = z_hi * 4 + z_lo), core: 2. Of those that a mesh axis runs over, the one named last changes fastest.
Arguments:
- tile_values: bfloat16 [4096, 128, 16, 128], P(('prov', 'month', 'bin')), may hold values from -6 to 6
- prov_block: int32 [4096], P(('prov', 'month', 'bin')), may hold values from 0 to 15
- month_block: int32 [4096], P(('prov', 'month', 'bin')), may hold values from 0 to 7
- factor_b: bfloat16 [256, 64], P(('prov', 'month')), may hold values from -0.375 to 0.375
- factor_c: bfloat16 [1024, 64], P(('prov', 'bin')), may hold values from -0.1875 to 0.1875
Outputs:
- factor_a: float32 [65536, 64], P(('prov', 'month', 'bin'))
- new_c: float32 [1024, 64], P(('bin', 'prov', 'month'))
All inputs are finite; a program needn't handle non-finite values.
Results may differ from a plain program's by a relative error of at most 0.00053.
Values may be sent and summed in bfloat16 or wider, within the bound.
No kernel may reach another device: no remote copies, remote signals or barrier semaphores. Data moves between devices by JAX's collectives and lax.ppermute only.
A program may use at most 64 MiB of HBM per device.

v0:
```python
import jax
import jax.numpy as jnp
from jax import lax
from jax.sharding import PartitionSpec as P

MB_DEV = 8
PB_DEV = 16


epsilon = 1e-06


def gram_of(factor_rows):
    return jnp.dot(
        factor_rows.T,
        factor_rows,
        precision=lax.Precision.HIGHEST,
        preferred_element_type=jnp.float32,
    )


def solve_gram(gram_matrix, right_rows):
    lower_factor = lax.linalg.cholesky(gram_matrix)
    half_solved = lax.linalg.triangular_solve(
        lower_factor, right_rows, left_side=False, lower=True, transpose_a=True
    )
    return lax.linalg.triangular_solve(
        lower_factor, half_solved, left_side=False, lower=True, transpose_a=False
    )


def shards(tile_values, prov_block, month_block, factor_b, factor_c):
    whole_b = lax.all_gather(factor_b, ("prov", "month"), axis=0, tiled=True)
    whole_c = lax.all_gather(factor_c, ("prov", "bin"), axis=0, tiled=True)
    factor_rank = factor_b.shape[1]
    tile_i = tile_values.shape[1]
    tile_j = tile_values.shape[2]
    tile_k = tile_values.shape[3]
    slab_rows = PB_DEV * tile_i
    float_b = whole_b.astype(jnp.float32)
    gram_b = gram_of(float_b)
    gram_c = gram_of(whole_c.astype(jnp.float32))
    month_index = lax.axis_index("month")
    bin_index = lax.axis_index("bin")
    slab_b = lax.dynamic_slice_in_dim(float_b, month_index * (MB_DEV * tile_j), MB_DEV * tile_j, 0)
    slab_b = slab_b.reshape(MB_DEV, tile_j, factor_rank)
    slab_c = lax.dynamic_slice_in_dim(whole_c, bin_index * tile_k, tile_k, 0)
    picked_b = jnp.take(slab_b, month_block, axis=0)
    partial_y = jnp.einsum("tijc,cr->tijr", tile_values, slab_c, preferred_element_type=jnp.float32)
    contrib = jnp.sum(partial_y * picked_b[:, None, :, :], axis=2)
    selector = (prov_block[:, None] == jnp.arange(PB_DEV, dtype=jnp.int32)[None, :]).astype(
        jnp.float32
    )
    partial_a = jnp.einsum("tp,tir->pir", selector, contrib, precision=lax.Precision.HIGHEST)
    partial_a = partial_a.reshape(slab_rows, factor_rank)
    gram_solve = gram_b * gram_c
    own_sum = lax.psum_scatter(partial_a, ("month", "bin"), scatter_dimension=0, tiled=True)
    factor_a = solve_gram(gram_solve, own_sum)
    squares = lax.psum(jnp.sum(factor_a * factor_a, axis=0), ("prov", "month", "bin"))
    col_scale = jnp.sqrt(squares + epsilon)
    gram_a = lax.psum(gram_of(factor_a / col_scale), ("prov", "month", "bin"))
    slab_a = lax.all_gather(
        (factor_a / col_scale).astype(jnp.bfloat16), ("month", "bin"), axis=0, tiled=True
    )
    picked_a = jnp.take(slab_a.reshape(PB_DEV, tile_i, factor_rank), prov_block, axis=0)
    partial_w = jnp.einsum(
        "tijc,tir->tjcr", tile_values, picked_a, preferred_element_type=jnp.float32
    )
    partial_c = jnp.sum(partial_w * picked_b[:, :, None, :], axis=(0, 1))
    own_c = lax.psum_scatter(partial_c, ("prov", "month"), scatter_dimension=0, tiled=True)
    new_c = solve_gram(gram_a * gram_b, own_c)
    return (factor_a, new_c)


def solution(mesh):
    in_specs = (
        P(("prov", "month", "bin"), None, None, None),
        P(("prov", "month", "bin")),
        P(("prov", "month", "bin")),
        P(("prov", "month"), None),
        P(("prov", "bin"), None),
    )
    out_specs = (P(("prov", "month", "bin"), None), P(("bin", "prov", "month"), None))
    return jax.shard_map(shards, mesh=mesh, in_specs=in_specs, out_specs=out_specs, check_vma=False)
```

profile of v0, /device:TPU:1, one launch (start us, length us, event | category | flops | bytes accessed | tf_op | source)
XLA Modules:
  0.0 1553.2 jit_solution(235201649275844337)
XLA Ops:
  7.2 0.7 compare_and_fusion.1
  7.9 0.7 compare_select_fusion.1
  8.6 84.1 %all-gather.1 = bf16[64,4,64]{2,1,0:T(4,128)(2,1)S(1)} all-gather(bf16[1,4,64]{2,1,0:T(4,128)(2,1)} %bitcast.77), channel_id=1, replica_groups=mesh['prov'=32,'month'=2,'bin'=8] {'prov','month'}, dimensions={0}, use_global_device_ids=true | all-gather | bytes 33280 | tf_op jit(solution)/shard_map/all_gather | solution.py:33
  92.7 682.7 %all-gather = bf16[256,4,64]{2,1,0:T(4,128)(2,1)S(1)} all-gather(bf16[1,4,64]{2,1,0:T(4,128)(2,1)} %bitcast.78), channel_id=1, replica_groups=mesh['prov'=32,'month'=2,'bin'=8] {'prov','bin'}, dimensions={0}, use_global_device_ids=true | all-gather | bytes 131584 | tf_op jit(solution)/shard_map/all_gather | solution.py:34
  776.0 3.8 fusion.1
  780.4 1.0 copy.75
  781.9 5.8 custom-call.16
  787.8 0.6 compare_reduce_fusion.1
  788.4 0.7 fusion.16
  789.1 4.9 custom-call.13
  794.0 1.3 dynamic-slice
  795.9 226.9 %reduce-scatter.2.cloned.1.call-done = f32[128,64]{0,1:T(8,128)} async-done(((f32[2048,64]{0,1:T(8,128)}), f32[128,64]{0,1:T(8,128)}) %reduce-scatter.2.cloned.1.call-update) | async-done | bytes 32784 | tf_op jit(solution)/shard_map/reduce_scatter | solution.py:57
  1022.8 1.0 fusion.26
  1024.1 97.7 %psum.14 = f32[64]{0:T(128)S(1)} all-reduce(f32[64]{0:T(128)S(1)} %get-tuple-element.3), channel_id=1, replica_groups=mesh['prov'=32,'month'=2,'bin'=8] {'prov','month','bin'}, use_global_device_ids=true, to_apply=%region_5.7 | all-reduce | flops 64 | bytes 512 | tf_op jit(solution)/shard_map/psum | solution.py:59
  1122.2 93.6 %psum.15 = f32[64,64]{0,1:T(8,128)S(1)} all-reduce(f32[64,64]{0,1:T(8,128)S(1)} %fusion.30), channel_id=1, replica_groups=mesh['prov'=32,'month'=2,'bin'=8] {'prov','month','bin'}, use_global_device_ids=true, to_apply=%region_8.10 | all-reduce | flops 4096 | bytes 32768 | tf_op jit(solution)/shard_map/psum | solution.py:61
  1215.9 5.8 custom-call.17
  1221.8 0.6 compare_reduce_fusion
  1222.5 0.7 fusion.17
  1223.1 4.9 custom-call.14
  1228.0 49.8 %all_gather.11 = bf16[2048,64]{0,1:T(8,128)(2,1)S(1)} all-gather(bf16[128,64]{0,1:T(8,128)(2,1)S(1)} %fusion.31), channel_id=1, replica_groups=mesh['prov'=32,'month'=2,'bin'=8] {'month','bin'}, dimensions={0}, use_global_device_ids=true | all-gather | bytes 278528 | tf_op jit(solution)/shard_map/all_gather | solution.py:62
  1277.9 0.6 gather_fusion.1
  1278.4 4.1 fusion
  1282.7 262.8 %all-reduce = f32[128,64]{1,0:T(8,128)S(1)} all-reduce(f32[128,64]{1,0:T(8,128)S(1)} %copy.51), channel_id=3, replica_groups=mesh['prov'=32,'month'=2,'bin'=8] {'prov','month'}, use_global_device_ids=true, to_apply=%region_7.9.clone | all-reduce | flops 8192 | bytes 65536
  1545.6 0.7 fusion.19
  (30 shorter events, 2.8 us)
Async XLA Ops:
  7.2 772.6 %copy-start.1 = (s32[8]{0:T(128)S(1)}, s32[8]{0:T(128)}, u32[]{:S(2)}) copy-start(s32[8]{0:T(128)} %param.7) | copy-start | bytes 100
  7.2 1015.7 %reduce-scatter.2.cloned.1.call-start = ((), (), s32[]{:S(2)}) async-start(), calls=%async_computation.1 | async-start | bytes 557056 | tf_op jit(solution)/shard_map/reduce_scatter | solution.py:57
  1024.1 258.5 %copy-start = (f32[128,64]{0,1:T(8,128)}, f32[128,64]{0,1:T(8,128)S(1)}, u32[]{:S(2)}) copy-start(f32[128,64]{0,1:T(8,128)S(1)} %get-tuple-element.4) | copy-start | bytes 98308
Sparse Core Ops, SparseCore 0:
  781.4 241.3 reduce-scatter.1
where the time goes:
time: 1560 us; the launch traced here: 1550 us
  blocking collectives  1270 us (81%)
  waiting for transfers between devices  227 us (15%)
  other arithmetic  25.7 us (2%)
    all_gather x1, blocking collectives, shards(): whole_c = lax.all_gather(factor_c, ('prov', 'bin'), axis=0, tiled=True)  683 us
    unnamed x1, blocking collectives  263 us
    reduce_scatter x1, waiting for transfers between devices, shards(): lax.psum_scatter(partial_a, ('month', 'bin'), scatter_dimension=0, tiled=...  227 us
    psum x1, blocking collectives, shards(): lax.psum(jnp.sum(factor_a * factor_a, axis=0), ('prov', 'month', 'bin'))  97.7 us
    psum x1, blocking collectives, shards(): gram_a = lax.psum(gram_of(factor_a / col_scale), ('prov', 'month', 'bin'))  93.6 us
    all_gather x1, blocking collectives, shards(): whole_b = lax.all_gather(factor_b, ('prov', 'month'), axis=0, tiled=True)  84.1 us
    all_gather x1, blocking collectives, shards(): lax.all_gather((factor_a / col_scale).astype(jnp.bfloat16), ('month', 'bi...  49.8 us
  transfers between devices with their start and end apart: 1, of which 1 were waited for; matrix products, arithmetic and copies ran while one was open for 1% of the time, Pallas kernels for 0%

commit v1 on v0

v1 whole, which is shorter than its diff:
```python
import jax
import jax.numpy as jnp
from jax import lax
from jax.sharding import PartitionSpec as P

MB_DEV = 8
PB_DEV = 16
epsilon = 1e-06
HIGH = lax.Precision.HIGHEST


def dot32(a, b, dims):
    return lax.dot_general(a, b, (dims, ((), ())), precision=HIGH, preferred_element_type=jnp.float32)


def inverse_factor(gram_matrix):
    lower = lax.linalg.cholesky(gram_matrix)
    eye = jnp.eye(gram_matrix.shape[0], dtype=jnp.float32)
    return lax.linalg.triangular_solve(lower, eye, left_side=True, lower=True)


def apply_inverse(rows, inv_factor):
    half = dot32(rows, inv_factor, ((1,), (1,)))
    return dot32(half, inv_factor, ((1,), (0,)))


def shards(tile_values, prov_block, month_block, factor_b, factor_c):
    tiles, tile_i, tile_j, tile_k = tile_values.shape
    rank = factor_b.shape[1]
    n_prov = lax.axis_size("prov")
    n_month = lax.axis_size("month")
    n_bin = lax.axis_size("bin")
    month = lax.axis_index("month")
    bin_at = lax.axis_index("bin")

    n_all = n_prov * n_month * n_bin
    c_rows = factor_c.shape[0] // n_month
    b_rep = n_bin // factor_b.shape[0]
    own_c_rows = lax.dynamic_slice_in_dim(factor_c, month * c_rows, c_rows, 0).reshape(1, c_rows * rank)
    own_b_row = lax.dynamic_slice_in_dim(factor_b, bin_at // b_rep, 1, 0)
    own_b_row = jnp.concatenate([own_b_row] * c_rows, axis=1)
    chunk = jnp.concatenate([own_c_rows, own_b_row], axis=0)
    sent = jnp.broadcast_to(chunk[None], (n_all,) + chunk.shape)
    got = lax.all_to_all(sent, ("prov", "bin", "month"), 0, 0, tiled=True)
    pairs_c = got[:, 0, :]
    whole_c = pairs_c.reshape(n_all * c_rows, rank)
    whole_b = got[:, 1, :rank].reshape(n_prov, factor_b.shape[0], b_rep, n_month, rank)[:, :, 0]
    whole_b = whole_b.transpose(0, 2, 1, 3).reshape(-1, rank)

    slab_c = lax.dynamic_slice_in_dim(whole_c, bin_at * tile_k, tile_k, 0)
    slab_b = lax.dynamic_slice_in_dim(whole_b, month * (MB_DEV * tile_j), MB_DEV * tile_j, 0)
    slab_b = slab_b.astype(jnp.float32).reshape(MB_DEV, tile_j, rank)
    picked_b = jnp.take(slab_b, month_block, axis=0)

    partial_y = jnp.einsum("tijc,cr->tijr", tile_values, slab_c, preferred_element_type=jnp.float32)
    contrib = jnp.sum(partial_y * picked_b[:, None, :, :], axis=2)
    selector = (prov_block[:, None] == jnp.arange(PB_DEV, dtype=jnp.int32)[None, :]).astype(jnp.float32)
    partial_a = jnp.einsum("tp,tir->pir", selector, contrib, precision=HIGH)

    pair_a = lax.all_to_all(partial_a.reshape(n_month, n_bin, tile_i, rank), "month", 0, 0, tiled=True)
    pair_a = jnp.sum(pair_a, axis=0)
    own_a = lax.all_to_all(pair_a, "bin", 0, 0, tiled=True)
    own_a = jnp.sum(own_a, axis=0)

    float_b = whole_b.astype(jnp.float32)
    float_c = whole_c.astype(jnp.float32)
    gram_b = dot32(float_b, float_b, ((0,), (0,)))
    gram_c = dot32(float_c, float_c, ((0,), (0,)))
    factor_a = apply_inverse(own_a, inverse_factor(gram_b * gram_c))

    slab_a = lax.all_to_all(
        jnp.broadcast_to(factor_a[None], (n_month * n_bin,) + factor_a.shape), ("month", "bin"), 0, 0, tiled=True
    )
    flat_a = slab_a.reshape(-1, rank)
    slab_gram = dot32(flat_a, flat_a, ((0,), (0,)))
    slab_gram = jnp.concatenate([slab_gram[: rank // 2], slab_gram[rank // 2 :]], axis=1)
    grams = lax.all_to_all(jnp.broadcast_to(slab_gram[None], (n_prov,) + slab_gram.shape), "prov", 0, 0, tiled=True)
    gram = jnp.sum(grams, axis=0)
    gram = jnp.concatenate([gram[:, :rank], gram[:, rank:]], axis=0)
    scale = jnp.sqrt(jnp.diagonal(gram) + epsilon)
    gram_a = gram / scale[:, None] / scale[None, :]

    high = slab_a.astype(jnp.bfloat16)
    low = (slab_a - high.astype(jnp.float32)).astype(jnp.bfloat16)
    both = jnp.concatenate([high, low], axis=2)
    picked_a = jnp.take(both, prov_block, axis=0)
    partial_w = jnp.einsum("tijc,tir->tjcr", tile_values, picked_a, preferred_element_type=jnp.float32)
    twice_b = jnp.concatenate([picked_b, picked_b], axis=2)
    partial_c = jnp.sum(partial_w * twice_b[:, :, None, :], axis=(0, 1))
    partial_c = partial_c[:, :rank] + partial_c[:, rank:]
    out_rows = tile_k // (n_prov * n_month)
    own_c = lax.all_to_all(
        partial_c.reshape(n_prov * n_month, 1, out_rows * rank), ("prov", "month"), 0, 0, tiled=True
    )
    own_c = jnp.sum(own_c, axis=0).reshape(out_rows, rank) / scale[None, :]
    new_c = apply_inverse(own_c, inverse_factor(gram_a * gram_b))
    return (factor_a, new_c)


def solution(mesh):
    in_specs = (
        P(("prov", "month", "bin"), None, None, None),
        P(("prov", "month", "bin")),
        P(("prov", "month", "bin")),
        P(("prov", "month"), None),
        P(("prov", "bin"), None),
    )
    out_specs = (P(("prov", "month", "bin"), None), P(("bin", "prov", "month"), None))
    return jax.shard_map(shards, mesh=mesh, in_specs=in_specs, out_specs=out_specs, check_vma=False)
```

time: 1560 us -> 160 us (0.10)
  blocking collectives: 1270 us -> 4.38 us
  waiting for transfers between devices: 227 us -> 57.5 us
  starting transfers between devices: 0.04 us -> 47.1 us
    all_gather x3 -> x0, blocking collectives: 817 us -> none  [the longest x1 683 us: shards(): whole_c = lax.all_gather(factor_c, ('prov', 'bin'), axis=0, tiled=True)]
    unnamed x1 -> x0, blocking collectives: 263 us -> none
    reduce_scatter x1 -> x0, waiting for transfers between devices: 227 us -> none  [shards(): lax.psum_scatter(partial_a, ('month', 'bin'), scatter_dimension=0, tiled=...]
    psum x2 -> x0, blocking collectives: 191 us -> none  [the longest x1 97.7 us: shards(): lax.psum(jnp.sum(factor_a * factor_a, axis=0), ('prov', 'month', 'bin'))]
    all_to_all x0 -> x5, waiting for transfers between devices: none -> 57.5 us  [the longest x1 16 us: shards(): got = lax.all_to_all(sent, ('prov', 'bin', 'month'), 0, 0, tiled=True)]
    all_to_all x0 -> x5, starting transfers between devices: none -> 47.1 us  [the longest x1 22.2 us: shards(): got = lax.all_to_all(sent, ('prov', 'bin', 'month'), 0, 0, tiled=True)]
  transfers between devices with their start and end apart: 1 -> 5, of which waited for: 1 -> 5; matrix products, arithmetic and copies ran while one was open for 1% -> 5% of each run, Pallas kernels for 0% -> 0%
where the time goes in v1:
time: 160 us; the launch traced here: 157 us
  waiting for transfers between devices  57.5 us (36%)
  starting transfers between devices  47.1 us (29%)
  other arithmetic  27 us (17%)
  matrix products  11.8 us (7%)
  local copies, waits for them, and re-layouts  8.57 us (5%)
  blocking collectives  4.38 us (3%)
    all_to_all x1, starting transfers between devices, shards(): got = lax.all_to_all(sent, ('prov', 'bin', 'month'), 0, 0, tiled=True)  22.2 us
    all_to_all x1, waiting for transfers between devices, shards(): got = lax.all_to_all(sent, ('prov', 'bin', 'month'), 0, 0, tiled=True)  16 us
    all_to_all x1, waiting for transfers between devices, shards(): lax.all_to_all(jnp.broadcast_to(slab_gram[None], (n_prov,) + slab_gram.sh...  14.9 us
    another operation x6, other arithmetic, inverse_factor(): lower = lax.linalg.cholesky(gram_matrix)  13 us
    all_to_all x1, waiting for transfers between devices, shards(): lax.all_to_all(jnp.broadcast_to(factor_a[None], (n_month * n_bin,) + fact...  12.6 us
    all_to_all x1, starting transfers between devices, shards(): lax.all_to_all(partial_c.reshape(n_prov * n_month, 1, out_rows * rank), (...  12.2 us
    another operation x4, other arithmetic, inverse_factor(): return lax.linalg.triangular_solve(lower, eye, left_side=True, lower=True)  11.1 us
    all_to_all x1, waiting for transfers between devices, shards(): lax.all_to_all(partial_c.reshape(n_prov * n_month, 1, out_rows * rank), (...  9.51 us
  transfers between devices with their start and end apart: 5, of which 5 were waited for; matrix products, arithmetic and copies ran while one was open for 5% of the time, Pallas kernels for 0%

profile of v1, /device:TPU:1, one launch (start us, length us, event | category | flops | bytes accessed | tf_op | source)
XLA Modules:
  0.0 157.4 jit_solution(8568359042062327848)
XLA Ops:
  2.2 0.8 broadcast_in_dim.34
  3.0 22.2 %all-to-all-start = ((bf16[512,2,128]{2,1,0:T(2,128)(2,1)}), bf16[512,2,128]{2,1,0:T(2,128)(2,1)S(1)}, u32[]{:S(2)}, u32[]{:S(2)}) async-start(bf16[512,2,128]{2,1,0:T(2,128)(2,1)} %broadcast_in_dim.34), calls=%async_computation | async-start | bytes 524288 | tf_op jit(solution)/shard_map/all_to_all | solution.py:44
  26.5 16.0 %all-to-all-done = bf16[512,2,128]{2,1,0:T(2,128)(2,1)S(1)} async-done(((bf16[512,2,128]{2,1,0:T(2,128)(2,1)}), bf16[512,2,128]{2,1,0:T(2,128)(2,1)S(1)}, u32[]{:S(2)}, u32[]{:S(2)}) %all-to-all-start) | async-done | bytes 262176 | tf_op jit(solution)/shard_map/all_to_all | solution.py:44
  43.2 0.7 slice_reduce_fusion
  44.4 5.8 %custom-call.10 = f32[64,64]{1,0:T(8,128)S(1)} custom-call(f32[64,64]{1,0:T(8,128)S(1)} %fusion.27), custom_call_target="Cholesky" | custom-call | tf_op jit(solution)/shard_map/cholesky/custom-call.1 | solution.py:17
  51.0 3.8 %fusion.1 = f32[8,128,64]{1,2,0:T(8,128)S(1)} fusion(f32[8,16,64]{2,1,0:T(8,128)S(1)} %broadcast_select_fusion, bf16[8,128,16,128]{3,2,1,0:T(8,128)(2,1)} %param.8, bf16[1024,64]{1,0:T(8,128)(2,1)S(1)} %reshape_squeeze.6, s32[]{:T(128)S(6)} %select_n.51), kind=kOutput, calls=%fused_computation.6 | convolution fusion | flops 270467072 | bytes 4554756 | tf_op jit(solution)/shard_map/tijc,cr->tijr/dot_general | solution.py:55
  55.4 4.4 %all_to_all.30 = f32[2,8,128,64]{2,3,1,0:T(8,128)S(1)} all-to-all(f32[2,8,128,64]{2,3,1,0:T(8,128)S(1)} %copy.58), channel_id=1, replica_groups=mesh['prov'=32,'month'=2,'bin'=8] {'month'}, dimensions={0} | all-to-all | bytes 1048576 | tf_op jit(solution)/shard_map/all_to_all | solution.py:60
  59.8 0.7 reduce_sum.55
  60.5 3.4 %all-to-all-start.2 = ((f32[8,128,64]{1,2,0:T(8,128)}), f32[8,128,64]{1,2,0:T(8,128)S(1)}, u32[]{:S(2)}, u32[]{:S(2)}) async-start(f32[8,128,64]{1,2,0:T(8,128)} %reduce_sum.55), calls=%async_computation.2 | async-start | bytes 524288 | tf_op jit(solution)/shard_map/all_to_all | solution.py:62
  65.2 4.9 %custom-call.11 = f32[1,64,64]{1,2,0:T(8,128)S(1)} custom-call(f32[1,64,64]{2,1,0:T(8,128)S(1)} %fusion.21), custom_call_target="InvertDiagBlocksLowerTriangular" | custom-call | tf_op jit(solution)/shard_map/triangular_solve/custom-call.0 | solution.py:19
  70.3 4.5 %all-to-all-done.2 = f32[8,128,64]{1,2,0:T(8,128)S(1)} async-done(((f32[8,128,64]{1,2,0:T(8,128)}), f32[8,128,64]{1,2,0:T(8,128)S(1)}, u32[]{:S(2)}, u32[]{:S(2)}) %all-to-all-start.2) | async-done | bytes 262176 | tf_op jit(solution)/shard_map/all_to_all | solution.py:62
  75.3 0.8 broadcast_in_dim.58
  76.2 5.5 %all-to-all-start.3 = ((f32[16,128,64]{1,2,0:T(8,128)}), f32[16,128,64]{1,2,0:T(8,128)S(1)}, u32[]{:S(2)}, u32[]{:S(2)}) async-start(f32[16,128,64]{1,2,0:T(8,128)} %broadcast_in_dim.58), calls=%async_computation.3 | async-start | bytes 1048576 | tf_op jit(solution)/shard_map/all_to_all | solution.py:71
  81.8 12.6 %all-to-all-done.3 = f32[16,128,64]{1,2,0:T(8,128)S(1)} async-done(((f32[16,128,64]{1,2,0:T(8,128)}), f32[16,128,64]{1,2,0:T(8,128)S(1)}, u32[]{:S(2)}, u32[]{:S(2)}) %all-to-all-start.3) | async-done | bytes 524320 | tf_op jit(solution)/shard_map/all_to_all | solution.py:71
  95.1 4.7 %fusion = f32[128,128]{0,1:T(8,128)S(1)} fusion(f32[8,16,128]{2,1,0:T(8,128)S(1)} %pad_maximum_fusion.1, bf16[8,128,16,128]{3,2,1,0:T(8,128)(2,1)} %param.8, bf16[8,128,128]{1,2,0:T(8,128)(2,1)S(1)} %gather_fusion.1, pred[8]{0:T(512)(128)(4,1)S(1)} %compare_and_fusion), kind=kOutput, calls=%fused_computation.4 | convolution fusion | flops 541179904 | bytes 4587528 | tf_op jit(solution)/shard_map/tijc,tir->tjcr/dot_general | solution.py:87
  101.2 12.2 %all-to-all-start.4 = ((f32[64,1,128]{2,1,0:T(1,128)}), f32[64,1,128]{2,1,0:T(1,128)S(1)}, u32[]{:S(2)}, u32[]{:S(2)}) async-start(f32[64,1,128]{2,1,0:T(1,128)} %bitcast.20), calls=%async_computation.4 | async-start | bytes 65536 | tf_op jit(solution)/shard_map/all_to_all | solution.py:92
  113.4 9.5 %all-to-all-done.4 = f32[64,1,128]{2,1,0:T(1,128)S(1)} async-done(((f32[64,1,128]{2,1,0:T(1,128)}), f32[64,1,128]{2,1,0:T(1,128)S(1)}, u32[]{:S(2)}, u32[]{:S(2)}) %all-to-all-start.4) | async-done | bytes 32800 | tf_op jit(solution)/shard_map/all_to_all | solution.py:92
  123.0 0.8 broadcast_in_dim.61
  123.8 3.9 %all-to-all-start.5 = ((f32[32,32,128]{2,1,0:T(8,128)}), f32[32,32,128]{2,1,0:T(8,128)S(1)}, u32[]{:S(2)}, u32[]{:S(2)}) async-start(f32[32,32,128]{2,1,0:T(8,128)} %broadcast_in_dim.61), calls=%async_computation.5 | async-start | bytes 1048576 | tf_op jit(solution)/shard_map/all_to_all | solution.py:77
  127.9 14.9 %all-to-all-done.5 = f32[32,32,128]{2,1,0:T(8,128)S(1)} async-done(((f32[32,32,128]{2,1,0:T(8,128)}), f32[32,32,128]{2,1,0:T(8,128)S(1)}, u32[]{:S(2)}, u32[]{:S(2)}) %all-to-all-start.5) | async-done | bytes 524320 | tf_op jit(solution)/shard_map/all_to_all | solution.py:77
  143.1 0.8 gather_fusion.2
  144.1 5.8 %custom-call.12 = f32[64,64]{1,0:T(8,128)S(1)} custom-call(f32[64,64]{1,0:T(8,128)S(1)} %fusion.25), custom_call_target="Cholesky" | custom-call | tf_op jit(solution)/shard_map/cholesky/custom-call.1 | solution.py:17
  151.3 4.9 %custom-call.13 = f32[1,64,64]{1,2,0:T(8,128)S(1)} custom-call(f32[1,64,64]{2,1,0:T(8,128)S(1)} %fusion.22), custom_call_target="InvertDiagBlocksLowerTriangular" | custom-call | tf_op jit(solution)/shard_map/triangular_solve/custom-call.0 | solution.py:19
  156.6 0.7 fusion.42
  (67 shorter events, 11.8 us)
Async XLA Ops:
  0.6 0.7 copy-start
  3.0 39.5 %all-to-all-start = ((bf16[512,2,128]{2,1,0:T(2,128)(2,1)}), bf16[512,2,128]{2,1,0:T(2,128)(2,1)S(1)}, u32[]{:S(2)}, u32[]{:S(2)}) async-start(bf16[512,2,128]{2,1,0:T(2,128)(2,1)} %broadcast_in_dim.34), calls=%async_computation | async-start | bytes 524288 | tf_op jit(solution)/shard_map/all_to_all | solution.py:44
  43.1 11.7 %copy-start.2 = (s32[8]{0:T(128)S(1)}, s32[8]{0:T(128)}, u32[]{:S(2)}) copy-start(s32[8]{0:T(128)} %param.9) | copy-start | bytes 100
  60.5 14.4 %all-to-all-start.2 = ((f32[8,128,64]{1,2,0:T(8,128)}), f32[8,128,64]{1,2,0:T(8,128)S(1)}, u32[]{:S(2)}, u32[]{:S(2)}) async-start(f32[8,128,64]{1,2,0:T(8,128)} %reduce_sum.55), calls=%async_computation.2 | async-start | bytes 524288 | tf_op jit(solution)/shard_map/all_to_all | solution.py:62
  75.3 24.5 %copy-start.1 = (f32[128,64]{0,1:T(8,128)}, f32[128,64]{0,1:T(8,128)S(1)}, u32[]{:S(2)}) copy-start(f32[128,64]{0,1:T(8,128)S(1)} %fusion.41) | copy-start | bytes 98308
  76.2 18.2 %all-to-all-start.3 = ((f32[16,128,64]{1,2,0:T(8,128)}), f32[16,128,64]{1,2,0:T(8,128)S(1)}, u32[]{:S(2)}, u32[]{:S(2)}) async-start(f32[16,128,64]{1,2,0:T(8,128)} %broadcast_in_dim.58), calls=%async_computation.3 | async-start | bytes 1048576 | tf_op jit(solution)/shard_map/all_to_all | solution.py:71
  101.2 21.7 %all-to-all-start.4 = ((f32[64,1,128]{2,1,0:T(1,128)}), f32[64,1,128]{2,1,0:T(1,128)S(1)}, u32[]{:S(2)}, u32[]{:S(2)}) async-start(f32[64,1,128]{2,1,0:T(1,128)} %bitcast.20), calls=%async_computation.4 | async-start | bytes 65536 | tf_op jit(solution)/shard_map/all_to_all | solution.py:92
  123.8 18.9 %all-to-all-start.5 = ((f32[32,32,128]{2,1,0:T(8,128)}), f32[32,32,128]{2,1,0:T(8,128)S(1)}, u32[]{:S(2)}, u32[]{:S(2)}) async-start(f32[32,32,128]{2,1,0:T(8,128)} %broadcast_in_dim.61), calls=%async_computation.5 | async-start | bytes 1048576 | tf_op jit(solution)/shard_map/all_to_all | solution.py:77

commit v2 on v1

v2 whole, which is shorter than its diff:
```python
import jax
import jax.numpy as jnp
from jax import lax
from jax.experimental import pallas as pl
from jax.experimental.pallas import tpu as pltpu
from jax.sharding import PartitionSpec as P

MB_DEV = 8
PB_DEV = 16
epsilon = 1e-06
HIGH = lax.Precision.HIGHEST


def dot32(a, b, dims, precision=HIGH):
    return lax.dot_general(a, b, (dims, ((), ())), precision=precision, preferred_element_type=jnp.float32)


def spd_inverse(a):
    n = a.shape[0]
    lane = lax.broadcasted_iota(jnp.int32, a.shape, 1)
    sub = lax.broadcasted_iota(jnp.int32, a.shape, 0)
    lane_row = lax.broadcasted_iota(jnp.int32, (1, n), 1)
    for k in range(n):
        col = a[:, k : k + 1]
        inv = 1.0 / a[k : k + 1, k : k + 1]
        row = jnp.where(lane_row == k, inv, a[k : k + 1, :] * inv)
        rest = jnp.where(lane == k, 0.0, a) - col * row
        a = jnp.where(sub == k, row, rest)
    return a


def first_inverse_kernel(b_ref, pairs_ref, inv_ref, gram_b_ref):
    rank = b_ref.shape[1]
    b = b_ref[...]
    gram_b = dot32(b, b, ((0,), (0,)), None)
    z = pairs_ref[...]
    twin = dot32(z, z, ((0,), (0,)), None)
    gram_c = twin[:rank, :rank] + twin[rank:, rank:]
    gram_b_ref[...] = gram_b
    inv_ref[...] = spd_inverse(gram_b * gram_c)


def last_kernel(got_ref, gram_b_ref, out_ref):
    rank = gram_b_ref.shape[0]
    rows = jnp.sum(got_ref[:, 0, :], axis=0, keepdims=True)
    own = jnp.concatenate([rows[:, :rank], rows[:, rank:]], axis=0)
    gram = got_ref[:, 1, :rank]
    lane = lax.broadcasted_iota(jnp.int32, gram.shape, 1)
    sub = lax.broadcasted_iota(jnp.int32, gram.shape, 0)
    diag = jnp.where(lane == sub, gram, 0.0)
    scale_row = jnp.sqrt(jnp.sum(diag, axis=0, keepdims=True) + epsilon)
    scale_col = jnp.sqrt(jnp.sum(diag, axis=1, keepdims=True) + epsilon)
    system = gram / scale_col / scale_row * gram_b_ref[...]
    out_ref[...] = dot32(own / scale_row, spd_inverse(system), ((1,), (0,)))


def pick(blocks, index):
    return blocks.at[index].get(mode="promise_in_bounds")


def shards(tile_values, prov_block, month_block, factor_b, factor_c):
    tiles, tile_i, tile_j, tile_k = tile_values.shape
    rank = factor_b.shape[1]
    n_prov = lax.axis_size("prov")
    n_month = lax.axis_size("month")
    n_bin = lax.axis_size("bin")
    month = lax.axis_index("month")
    bin_at = lax.axis_index("bin")

    n_all = n_prov * n_month * n_bin
    c_rows = factor_c.shape[0] // n_month
    b_rep = n_bin // factor_b.shape[0]
    own_c_rows = lax.dynamic_slice_in_dim(factor_c, month * c_rows, c_rows, 0).reshape(1, c_rows * rank)
    own_b_row = lax.dynamic_slice_in_dim(factor_b, bin_at // b_rep, 1, 0)
    own_b_row = jnp.concatenate([own_b_row] * c_rows, axis=1)
    chunk = jnp.concatenate([own_c_rows, own_b_row], axis=0)
    sent = jnp.broadcast_to(chunk[None], (n_all,) + chunk.shape)
    got = lax.all_to_all(sent, ("prov", "bin", "month"), 0, 0, tiled=True)
    pairs_c = got[:, 0, :]
    whole_b = got[:, 1, :rank].reshape(n_prov, factor_b.shape[0], b_rep, n_month, rank)[:, :, 0]
    whole_b = whole_b.transpose(0, 2, 1, 3).reshape(-1, rank)

    slab_pairs = lax.dynamic_slice_in_dim(pairs_c, bin_at * (tile_k // c_rows), tile_k // c_rows, 0)
    slab_c = slab_pairs.reshape(tile_k, rank)
    slab_b = lax.dynamic_slice_in_dim(whole_b, month * (MB_DEV * tile_j), MB_DEV * tile_j, 0)
    slab_b = slab_b.astype(jnp.float32).reshape(MB_DEV, tile_j, rank)
    picked_b = pick(slab_b, month_block)

    partial_y = jnp.einsum("tijc,cr->tijr", tile_values, slab_c, preferred_element_type=jnp.float32)
    contrib = jnp.sum(partial_y * picked_b[:, None, :, :], axis=2)
    selector = (prov_block[:, None] == jnp.arange(PB_DEV, dtype=jnp.int32)[None, :]).astype(jnp.float32)
    partial_a = jnp.einsum("tp,tir->pir", selector, contrib, precision=HIGH)

    pair_a = lax.all_to_all(partial_a.reshape(n_month, n_bin, tile_i, rank), "month", 0, 0, tiled=True)
    pair_a = jnp.sum(pair_a, axis=0)
    whole_b, pairs_c, pair_a = lax.optimization_barrier((whole_b, pairs_c, pair_a))
    own_a = lax.all_to_all(pair_a, "bin", 0, 0, tiled=True)

    square = jax.ShapeDtypeStruct((rank, rank), jnp.float32)
    inverse, gram_b = pl.pallas_call(
        first_inverse_kernel,
        out_shape=(square, square),
        cost_estimate=pl.CostEstimate(flops=20000000, bytes_accessed=200000, transcendentals=0),
        name="first_inverse",
    )(whole_b, pairs_c)
    own_a = jnp.sum(own_a, axis=0)
    factor_a = dot32(own_a, inverse, ((1,), (0,)))

    half_a = lax.all_to_all(jnp.broadcast_to(factor_a[None], (n_bin,) + factor_a.shape), "bin", 0, 0, tiled=True)
    flat_a = half_a.reshape(-1, rank)
    half_gram = dot32(flat_a, flat_a, ((0,), (0,)))
    gram_rows = lax.all_to_all(half_gram.reshape(rank, 1, rank), ("prov", "month"), 0, 0, tiled=True)

    other_a = lax.ppermute(half_a, "month", [(i, n_month - 1 - i) for i in range(n_month)])

    def split(values):
        high = lax.reduce_precision(values, 8, 7)
        return jnp.concatenate([high, values - high], axis=2).astype(jnp.bfloat16)

    both = jnp.concatenate([split(half_a), split(other_a)], axis=0)
    picked_a = pick(both, prov_block ^ (month * n_bin))
    partial_w = jnp.einsum("tijc,tir->tjcr", tile_values, picked_a, preferred_element_type=jnp.float32)
    twice_b = jnp.concatenate([picked_b, picked_b], axis=2)
    partial_c = jnp.sum(partial_w * twice_b[:, :, None, :], axis=(0, 1))
    partial_c = partial_c[:, :rank] + partial_c[:, rank:]

    gram_rows, partial_c = lax.optimization_barrier((gram_rows, partial_c))
    gram_row = jnp.sum(gram_rows, axis=0)
    n_out = n_prov * n_month
    out_rows = tile_k // n_out
    sent_c = partial_c.reshape(n_out, 1, out_rows * rank)
    sent_row = jnp.broadcast_to(jnp.concatenate([gram_row] * out_rows, axis=1)[None], sent_c.shape)
    last = lax.all_to_all(jnp.concatenate([sent_c, sent_row], axis=1), ("prov", "month"), 0, 0, tiled=True)
    new_c = pl.pallas_call(
        last_kernel, out_shape=jax.ShapeDtypeStruct((out_rows, rank), jnp.float32), name="last_solve"
    )(last, gram_b)
    return (factor_a, new_c)


def solution(mesh):
    in_specs = (
        P(("prov", "month", "bin"), None, None, None),
        P(("prov", "month", "bin")),
        P(("prov", "month", "bin")),
        P(("prov", "month"), None),
        P(("prov", "bin"), None),
    )
    out_specs = (P(("prov", "month", "bin"), None), P(("bin", "prov", "month"), None))
    return jax.shard_map(shards, mesh=mesh, in_specs=in_specs, out_specs=out_specs, check_vma=False)
```

time: 160 us -> 131 us (0.82); the launches traced: 157 us -> 131 us
  other arithmetic: 27 us -> 1.28 us
  waiting for transfers between devices: 57.5 us -> 35.1 us
  blocking collectives: 4.38 us -> 20.2 us
  Pallas kernels: 0 us -> 14.5 us
  starting transfers between devices: 47.1 us -> 42.1 us
  local copies, waits for them, and re-layouts: 8.57 us -> 6.23 us
    another operation x10 -> x2, other arithmetic: 24.1 us -> 0.11 us  [the longest x6 13 us: inverse_factor(): lower = lax.linalg.cholesky(gram_matrix)]
    all_to_all x3 -> x2, waiting for transfers between devices: 36.9 us -> 14.7 us  [the longest x1 10 us: shards(): lax.all_to_all(jnp.broadcast_to(factor_a[None], (n_bin,) + factor_a.shape...]
    all_to_all x0 -> x1, blocking collectives: none -> 15.9 us  [shards(): lax.all_to_all(jnp.concatenate([sent_c, sent_row], axis=1), ('prov', 'mon...]
    pallas_call x0 -> x2, Pallas kernels: none -> 14.5 us  [the longest x1 7.36 us: shards(): pl.pallas_call(first_inverse_kernel, out_shape=(square, square), cost_est...]
    all_to_all x3 -> x2, starting transfers between devices: 21.5 us -> 12.6 us  [the longest x1 7.18 us: shards(): lax.all_to_all(half_gram.reshape(rank, 1, rank), ('prov', 'month'), 0, 0,...]
    ppermute x0 -> x1, starting transfers between devices: none -> 4 us  [shards(): lax.ppermute(half_a, 'month', [(i, n_month - 1 - i) for i in range(n_mont...]
  transfers between devices with their start and end apart: 5 -> 5, of which waited for: 5 -> 4; matrix products, arithmetic and copies ran while one was open for 5% -> 5% of each run, Pallas kernels for 0% -> 6%
where the time goes in v2:
time: 131 us
  starting transfers between devices  42.1 us (32%)
  waiting for transfers between devices  35.1 us (27%)
  blocking collectives  20.2 us (15%)
  Pallas kernels  14.5 us (11%)
  matrix products  10.3 us (8%)
  local copies, waits for them, and re-layouts  6.23 us (5%)
    all_to_all x1, starting transfers between devices, shards(): got = lax.all_to_all(sent, ('prov', 'bin', 'month'), 0, 0, tiled=True)  22.2 us
    all_to_all x1, waiting for transfers between devices, shards(): got = lax.all_to_all(sent, ('prov', 'bin', 'month'), 0, 0, tiled=True)  16.7 us
    all_to_all x1, blocking collectives, shards(): lax.all_to_all(jnp.concatenate([sent_c, sent_row], axis=1), ('prov', 'mon...  15.9 us
    all_to_all x1, waiting for transfers between devices, shards(): lax.all_to_all(jnp.broadcast_to(factor_a[None], (n_bin,) + factor_a.shape...  10 us
    pallas_call x1, Pallas kernels, shards(): pl.pallas_call(first_inverse_kernel, out_shape=(square, square), cost_est...  7.36 us
    all_to_all x1, starting transfers between devices, shards(): lax.all_to_all(half_gram.reshape(rank, 1, rank), ('prov', 'month'), 0, 0,...  7.18 us
    pallas_call x1, Pallas kernels, shards(): pl.pallas_call(last_kernel, out_shape=jax.ShapeDtypeStruct((out_rows, ran...  7.15 us
    all_to_all x1, starting transfers between devices, shards(): lax.all_to_all(jnp.broadcast_to(factor_a[None], (n_bin,) + factor_a.shape...  5.39 us
  transfers between devices with their start and end apart: 5, of which 4 were waited for; matrix products, arithmetic and copies ran while one was open for 5% of the time, Pallas kernels for 6%

profile of v2, /device:TPU:1, one launch (start us, length us, event | category | flops | bytes accessed | tf_op | source)
XLA Modules:
  0.0 130.7 jit_solution(72860743128605169)
XLA Ops:
  0.7 0.7 copy-done
  1.4 0.7 constant_dynamic-slice_fusion.2
  2.2 0.8 broadcast_in_dim.12
  3.0 22.2 %all-to-all-start = ((bf16[512,2,128]{2,1,0:T(2,128)(2,1)}), bf16[512,2,128]{2,1,0:T(2,128)(2,1)S(1)}, u32[]{:S(2)}, u32[]{:S(2)}) async-start(bf16[512,2,128]{2,1,0:T(2,128)(2,1)} %broadcast_in_dim.12), calls=%async_computation | async-start | bytes 524288 | tf_op jit(solution)/shard_map/all_to_all | solution.py:78
  25.2 0.7 compare_select_fusion.1
  25.9 16.7 %all-to-all-done = bf16[512,2,128]{2,1,0:T(2,128)(2,1)S(1)} async-done(((bf16[512,2,128]{2,1,0:T(2,128)(2,1)}), bf16[512,2,128]{2,1,0:T(2,128)(2,1)S(1)}, u32[]{:S(2)}, u32[]{:S(2)}) %all-to-all-start) | async-done | bytes 262176 | tf_op jit(solution)/shard_map/all_to_all | solution.py:78
  42.6 0.7 copy.63
  44.4 3.8 %fusion.1 = f32[8,128,64]{1,2,0:T(8,128)S(1)} fusion(f32[8,16,64]{2,1,0:T(8,128)S(1)} %gather_fusion, bf16[8,128,16,128]{3,2,1,0:T(8,128)(2,1)} %param.5, bf16[128,64]{1,0:T(8,128)(2,1)S(1)} %reshape.54), kind=kOutput, calls=%fused_computation.5 | convolution fusion | flops 270467072 | bytes 4505600 | tf_op jit(solution)/shard_map/tijc,cr->tijr/dot_general | solution.py:89
  48.7 4.3 %all_to_all.30 = f32[2,8,128,64]{2,1,3,0:T(8,128)S(1)} all-to-all(f32[2,8,128,64]{2,1,3,0:T(8,128)S(1)} %fusion.13), channel_id=1, replica_groups=mesh['prov'=32,'month'=2,'bin'=8] {'month'}, dimensions={0} | all-to-all | bytes 1048576 | tf_op jit(solution)/shard_map/all_to_all | solution.py:94
  53.0 0.7 copy.39
  53.8 3.4 %all-to-all-start.2 = ((f32[8,128,64]{1,2,0:T(8,128)}), f32[8,128,64]{1,2,0:T(8,128)S(1)}, u32[]{:S(2)}, u32[]{:S(2)}) async-start(f32[8,128,64]{1,2,0:T(8,128)} %copy.39), calls=%async_computation.2 | async-start | bytes 524288 | tf_op jit(solution)/shard_map/all_to_all | solution.py:97
  57.2 7.4 %first_inverse.1 = (f32[64,64]{1,0:T(8,128)}, f32[64,64]{1,0:T(8,128)}) custom-call(bf16[256,64]{1,0:T(8,128)(2,1)} %bitcast.54, bf16[512,128]{1,0:T(8,128)(2,1)} %bitcast.52), custom_call_target="tpu_custom_call" | custom-call | flops 20000000 | bytes 200000 | tf_op jit(solution)/shard_map/first_inverse/pallas_call | solution.py:100
  64.6 3.6 %all-to-all-done.2 = f32[8,128,64]{1,2,0:T(8,128)S(1)} async-done(((f32[8,128,64]{1,2,0:T(8,128)}), f32[8,128,64]{1,2,0:T(8,128)S(1)}, u32[]{:S(2)}, u32[]{:S(2)}) %all-to-all-start.2) | async-done | bytes 262176 | tf_op jit(solution)/shard_map/all_to_all | solution.py:97
  68.2 1.0 fusion.21
  69.2 0.7 broadcast_in_dim.14
  69.9 5.4 %all-to-all-start.3 = ((f32[8,128,64]{1,2,0:T(8,128)}), f32[8,128,64]{1,2,0:T(8,128)S(1)}, u32[]{:S(2)}, u32[]{:S(2)}) async-start(f32[8,128,64]{1,2,0:T(8,128)} %broadcast_in_dim.14), calls=%async_computation.3 | async-start | bytes 524288 | tf_op jit(solution)/shard_map/all_to_all | solution.py:109
  75.4 10.0 %all-to-all-done.3 = f32[8,128,64]{1,2,0:T(8,128)S(1)} async-done(((f32[8,128,64]{1,2,0:T(8,128)}), f32[8,128,64]{1,2,0:T(8,128)S(1)}, u32[]{:S(2)}, u32[]{:S(2)}) %all-to-all-start.3) | async-done | bytes 262176 | tf_op jit(solution)/shard_map/all_to_all | solution.py:109
  85.4 4.0 %collective-permute-start = (f32[8,128,64]{1,2,0:T(8,128)S(1)}, f32[8,128,64]{1,2,0:T(8,128)S(1)}, u32[]{:S(2)}, u32[]{:S(2)}) collective-permute-start(f32[8,128,64]{1,2,0:T(8,128)S(1)} %all-to-all-done.3), channel_id=1, source_target_pairs={{0,8},{8,0},{1,9},{9,1},{2,10},{10,2},{3,11},{11,3},{4,12},{12,4},... | collective-permute-start | bytes 786440 | tf_op jit(solution)/shard_map/ppermute | solution.py:114
  89.4 1.0 fusion.22
  90.4 7.2 %all-to-all-start.4 = ((f32[64,1,64]{2,1,0:T(1,128)}), f32[64,1,64]{2,1,0:T(1,128)S(1)}, u32[]{:S(2)}, u32[]{:S(2)}) async-start(f32[64,1,64]{2,1,0:T(1,128)} %bitcast.13), calls=%async_computation.4 | async-start | bytes 65536 | tf_op jit(solution)/shard_map/all_to_all | solution.py:112
  98.4 4.1 %fusion = f32[128,128]{0,1:T(8,128)S(1)} fusion(f32[8,16,128]{2,1,0:T(8,128)S(1)} %pad_maximum_fusion, bf16[8,128,16,128]{3,2,1,0:T(8,128)(2,1)} %param.5, bf16[8,128,128]{1,2,0:T(8,128)(2,1)S(1)} %gather_fusion.1), kind=kOutput, calls=%fused_computation.3 | convolution fusion | flops 541048832 | bytes 4587520 | tf_op jit(solution)/shard_map/tijc,tir->tjcr/dot_general | solution.py:122
  102.5 4.7 %all-to-all-done.4 = f32[64,1,64]{2,1,0:T(1,128)S(1)} async-done(((f32[64,1,64]{2,1,0:T(1,128)}), f32[64,1,64]{2,1,0:T(1,128)S(1)}, u32[]{:S(2)}, u32[]{:S(2)}) %all-to-all-start.4) | async-done | bytes 16416 | tf_op jit(solution)/shard_map/all_to_all | solution.py:112
  107.6 15.9 %all_to_all.31.got_ref = f32[64,2,128]{2,1,0:T(2,128)} all-to-all(f32[64,2,128]{2,1,0:T(2,128)S(1)} %pad_maximum_fusion.1), channel_id=1, replica_groups=mesh['prov'=32,'month'=2,'bin'=8] {'prov','month'}, dimensions={0} | all-to-all | bytes 131072 | tf_op jit(solution)/shard_map/all_to_all | solution.py:133
  123.5 7.2 %last_solve.1 = f32[2,64]{1,0:T(2,128)} custom-call(f32[64,2,128]{2,1,0:T(2,128)} %all_to_all.31.got_ref, f32[64,64]{1,0:T(8,128)} %get-tuple-element.15.gram_b_ref), custom_call_target="tpu_custom_call" | custom-call | tf_op jit(solution)/shard_map/last_solve/pallas_call | solution.py:134
  (40 shorter events, 3.0 us)
Async XLA Ops:
  0.6 0.7 copy-start
  3.0 39.6 %all-to-all-start = ((bf16[512,2,128]{2,1,0:T(2,128)(2,1)}), bf16[512,2,128]{2,1,0:T(2,128)(2,1)S(1)}, u32[]{:S(2)}, u32[]{:S(2)}) async-start(bf16[512,2,128]{2,1,0:T(2,128)(2,1)} %broadcast_in_dim.12), calls=%async_computation | async-start | bytes 524288 | tf_op jit(solution)/shard_map/all_to_all | solution.py:78
  42.6 5.6 %copy-start.3 = (s32[8]{0:T(128)S(1)}, s32[8]{0:T(128)}, u32[]{:S(2)}) copy-start(s32[8]{0:T(128)} %param.6) | copy-start | bytes 100
  43.7 9.3 %copy-start.1 = (bf16[32,2,4,64]{3,2,1,0:T(4,128)(2,1)}, bf16[32,2,4,64]{3,2,1,0:T(4,128)(2,1)S(1)}, u32[]{:S(2)}) copy-start(bf16[32,2,4,64]{3,2,1,0:T(4,128)(2,1)S(1)} %copy.34) | copy-start | bytes 98308
  53.8 14.4 %all-to-all-start.2 = ((f32[8,128,64]{1,2,0:T(8,128)}), f32[8,128,64]{1,2,0:T(8,128)S(1)}, u32[]{:S(2)}, u32[]{:S(2)}) async-start(f32[8,128,64]{1,2,0:T(8,128)} %copy.39), calls=%async_computation.2 | async-start | bytes 524288 | tf_op jit(solution)/shard_map/all_to_all | solution.py:97
  69.2 33.3 %copy-start.2 = (f32[128,64]{0,1:T(8,128)}, f32[128,64]{0,1:T(8,128)S(1)}, u32[]{:S(2)}) copy-start(f32[128,64]{0,1:T(8,128)S(1)} %fusion.21) | copy-start | bytes 98308
  69.9 15.5 %all-to-all-start.3 = ((f32[8,128,64]{1,2,0:T(8,128)}), f32[8,128,64]{1,2,0:T(8,128)S(1)}, u32[]{:S(2)}, u32[]{:S(2)}) async-start(f32[8,128,64]{1,2,0:T(8,128)} %broadcast_in_dim.14), calls=%async_computation.3 | async-start | bytes 524288 | tf_op jit(solution)/shard_map/all_to_all | solution.py:109
  85.4 12.2 %collective-permute-start = (f32[8,128,64]{1,2,0:T(8,128)S(1)}, f32[8,128,64]{1,2,0:T(8,128)S(1)}, u32[]{:S(2)}, u32[]{:S(2)}) collective-permute-start(f32[8,128,64]{1,2,0:T(8,128)S(1)} %all-to-all-done.3), channel_id=1, source_target_pairs={{0,8},{8,0},{1,9},{9,1},{2,10},{10,2},{3,11},{11,3},{4,12},{12,4},... | collective-permute-start | bytes 786440 | tf_op jit(solution)/shard_map/ppermute | solution.py:114
  90.4 16.8 %all-to-all-start.4 = ((f32[64,1,64]{2,1,0:T(1,128)}), f32[64,1,64]{2,1,0:T(1,128)S(1)}, u32[]{:S(2)}, u32[]{:S(2)}) async-start(f32[64,1,64]{2,1,0:T(1,128)} %bitcast.13), calls=%async_computation.4 | async-start | bytes 65536 | tf_op jit(solution)/shard_map/all_to_all | solution.py:112

commit v3 on v2

v3 whole, which is shorter than its diff:
```python
import jax
import jax.numpy as jnp
from jax import lax
from jax.experimental import pallas as pl
from jax.experimental.pallas import tpu as pltpu
from jax.sharding import PartitionSpec as P

MB_DEV = 8
PB_DEV = 16
epsilon = 1e-06
HIGH = lax.Precision.HIGHEST
SMALL = pltpu.CompilerParams(vmem_limit_bytes=8 * 1024 * 1024)
PROV = ("zl", "y")
BIN = ("x", "zh")
GRAM = ("zl", "month")


def dot32(a, b, dims, precision=HIGH):
    return lax.dot_general(a, b, (dims, ((), ())), precision=precision, preferred_element_type=jnp.float32)


def diagonals(a):
    lane = lax.broadcasted_iota(jnp.int32, a.shape, 1)
    sub = lax.broadcasted_iota(jnp.int32, a.shape, 0)
    diag = jnp.where(lane == sub, a, 0.0)
    return jnp.sum(diag, axis=0, keepdims=True), jnp.sum(diag, axis=1, keepdims=True)


def spd_inverse(a):
    n = a.shape[0]
    in_row, in_col = diagonals(a)
    in_row, in_col = lax.rsqrt(in_row), lax.rsqrt(in_col)
    a = a * in_col * in_row
    lane = lax.broadcasted_iota(jnp.int32, a.shape, 1)
    sub = lax.broadcasted_iota(jnp.int32, a.shape, 0)
    lane_row = lax.broadcasted_iota(jnp.int32, (1, n), 1)
    for k in range(0, n, 2):
        col0 = jnp.broadcast_to(a[:, k : k + 1], a.shape)
        col1 = jnp.broadcast_to(a[:, k + 1 : k + 2], a.shape)
        p, q, s = col0[k : k + 1], col1[k : k + 1], col1[k + 1 : k + 2]
        inv = 1.0 / (p * s - q * q)
        p, q, s = p * inv, q * inv, s * inv
        row0, row1 = a[k : k + 1], a[k + 1 : k + 2]
        first, second = lane_row == k, lane_row == k + 1
        new0 = jnp.where(first, s, jnp.where(second, -q, s * row0 - q * row1))
        new1 = jnp.where(first, -q, jnp.where(second, p, p * row1 - q * row0))
        rest = jnp.where((lane == k) | (lane == k + 1), 0.0, a) - col0 * new0 - col1 * new1
        a = jnp.where(sub == k, new0, jnp.where(sub == k + 1, new1, rest))
    return a * in_col * in_row


def first_inverse_kernel(b_ref, pairs_ref, inv_ref, gram_b_ref):
    rank = b_ref.shape[1]
    b = b_ref[...]
    gram_b = dot32(b, b, ((0,), (0,)), None)
    z = pairs_ref[...]
    twin = dot32(z, z, ((0,), (0,)), None)
    gram_c = twin[:rank, :rank] + twin[rank:, rank:]
    gram_b_ref[...] = gram_b
    inv_ref[...] = spd_inverse(gram_b * gram_c)


def gram_kernel(a_ref, out_ref):
    rank = a_ref.shape[1]
    gram = dot32(a_ref[0], a_ref[0], ((1,), (1,)))
    for block in range(1, a_ref.shape[0]):
        gram = gram + dot32(a_ref[block], a_ref[block], ((1,), (1,)))
    groups = out_ref.shape[0]
    for j in range(rank // groups):
        out_ref[:, j * rank : (j + 1) * rank] = gram[j * groups : (j + 1) * groups]


def last_kernel(got_ref, gram_b_ref, out_ref):
    rank = gram_b_ref.shape[0]
    width = got_ref.shape[1]
    lead = out_ref.shape[0] * rank
    groups = rank * rank // (width - lead)
    got = got_ref[...]
    rows = jnp.sum(got[:, :lead], axis=0, keepdims=True)
    own = jnp.concatenate([rows[:, j * rank : (j + 1) * rank] for j in range(out_ref.shape[0])], axis=0)
    folded = got[:groups, lead:]
    for part in range(1, got.shape[0] // groups):
        folded = folded + got[part * groups : (part + 1) * groups, lead:]
    gram = jnp.concatenate([folded[:, j * rank : (j + 1) * rank] for j in range(rank // groups)], axis=0)
    square_row, square_col = diagonals(gram)
    scale_row = jnp.sqrt(square_row + epsilon)
    scale_col = jnp.sqrt(square_col + epsilon)
    system = gram / scale_col / scale_row * gram_b_ref[...]
    out_ref[...] = dot32(own / scale_row, spd_inverse(system), ((1,), (0,)))


def pick(blocks, index):
    return blocks.at[index].get(mode="promise_in_bounds")


def shards(tile_values, prov_block, month_block, factor_b, factor_c):
    tiles, tile_i, tile_j, tile_k = tile_values.shape
    rank = factor_b.shape[1]
    n_prov = lax.axis_size(PROV)
    n_month = lax.axis_size("month")
    n_bin = lax.axis_size(BIN)
    month = lax.axis_index("month")
    bin_at = lax.axis_index(BIN)

    n_all = n_prov * n_month * n_bin
    c_rows = factor_c.shape[0] // n_month
    b_rep = n_bin // factor_b.shape[0]
    own_c_rows = lax.dynamic_slice_in_dim(factor_c, month * c_rows, c_rows, 0).reshape(1, c_rows * rank)
    own_b_row = lax.dynamic_slice_in_dim(factor_b, bin_at // b_rep, 1, 0)
    own_b_row = jnp.concatenate([own_b_row] * c_rows, axis=1)
    chunk = jnp.concatenate([own_c_rows, own_b_row], axis=0)
    sent = jnp.broadcast_to(chunk[None], (n_all,) + chunk.shape)
    got = lax.all_to_all(sent, PROV + BIN + ("month",), 0, 0, tiled=True)
    pairs_c = got[:, 0, :]
    whole_b = got[:, 1, :rank].reshape(n_prov, factor_b.shape[0], b_rep, n_month, rank)[:, :, 0]
    whole_b = whole_b.transpose(0, 2, 1, 3).reshape(-1, rank)

    slab_pairs = lax.dynamic_slice_in_dim(pairs_c, bin_at * (tile_k // c_rows), tile_k // c_rows, 0)
    slab_c = slab_pairs.reshape(tile_k, rank)
    slab_b = lax.dynamic_slice_in_dim(whole_b, month * (MB_DEV * tile_j), MB_DEV * tile_j, 0)
    slab_b = slab_b.astype(jnp.float32).reshape(MB_DEV, tile_j, rank)
    picked_b = pick(slab_b, month_block)

    partial_y = jnp.einsum("tijc,cr->tijr", tile_values, slab_c, preferred_element_type=jnp.float32)
    contrib = jnp.sum(partial_y * picked_b[:, None, :, :], axis=2)
    selector = (prov_block[:, None] == jnp.arange(PB_DEV, dtype=jnp.int32)[None, :]).astype(jnp.float32)
    partial_a = jnp.einsum("tp,tir->pir", selector, contrib, precision=HIGH)

    pair_a = lax.all_to_all(partial_a.reshape(n_month, n_bin, tile_i, rank), "month", 0, 0, tiled=True)
    pair_a = jnp.sum(pair_a, axis=0)
    whole_b, pairs_c, pair_a = lax.optimization_barrier((whole_b, pairs_c, pair_a))
    own_a = lax.all_to_all(pair_a, BIN, 0, 0, tiled=True)

    square = jax.ShapeDtypeStruct((rank, rank), jnp.float32)
    inverse, gram_b = pl.pallas_call(
        first_inverse_kernel,
        out_shape=(square, square),
        cost_estimate=pl.CostEstimate(flops=20000000, bytes_accessed=200000, transcendentals=0),
        name="first_inverse",
        compiler_params=SMALL,
    )(whole_b, pairs_c)
    own_a = jnp.sum(own_a, axis=0)
    factor_a = dot32(own_a, inverse, ((1,), (0,)))

    half_a = lax.all_to_all(jnp.broadcast_to(factor_a[None], (n_bin,) + factor_a.shape), BIN, 0, 0, tiled=True)
    n_gram = lax.axis_size(GRAM)
    half_gram = pl.pallas_call(
        gram_kernel, out_shape=jax.ShapeDtypeStruct((n_gram, rank * rank // n_gram), jnp.float32), name="half_gram", compiler_params=SMALL
    )(half_a.transpose(0, 2, 1))
    gram_rows = lax.all_to_all(half_gram[:, None, :], GRAM, 0, 0, tiled=True)

    other_a = lax.ppermute(half_a, "month", [(i, n_month - 1 - i) for i in range(n_month)])

    def split(values):
        high = lax.reduce_precision(values, 8, 7)
        return jnp.concatenate([high, values - high], axis=2).astype(jnp.bfloat16)

    both = jnp.concatenate([split(half_a), split(other_a)], axis=0)
    picked_a = pick(both, prov_block ^ (month * n_bin))
    partial_w = jnp.einsum("tijc,tir->tjcr", tile_values, picked_a, preferred_element_type=jnp.float32)
    twice_b = jnp.concatenate([picked_b, picked_b], axis=2)
    partial_c = jnp.sum(partial_w * twice_b[:, :, None, :], axis=(0, 1))
    partial_c = partial_c[:, :rank] + partial_c[:, rank:]

    gram_rows, partial_c = lax.optimization_barrier((gram_rows, partial_c))
    gram_row = jnp.sum(gram_rows, axis=0, keepdims=True)
    n_out = n_prov * n_month
    out_rows = tile_k // n_out
    n_y = lax.axis_size("y")
    sent_c = partial_c.reshape(n_prov // n_y, n_y, n_month, out_rows * rank).transpose(1, 0, 2, 3)
    sent_c = sent_c.reshape(n_out, 1, out_rows * rank)
    sent_row = jnp.broadcast_to(gram_row, (n_out,) + gram_row.shape[1:])
    last = lax.all_to_all(jnp.concatenate([sent_c, sent_row], axis=2), ("y",) + GRAM, 0, 0, tiled=True)
    new_c = pl.pallas_call(
        last_kernel, out_shape=jax.ShapeDtypeStruct((out_rows, rank), jnp.float32), name="last_solve", compiler_params=SMALL
    )(last.reshape(n_out, -1), gram_b)
    return (factor_a, new_c)


def solution(mesh):
    prov, month, bins = mesh.devices.shape
    shape = (prov // 8, 8, month, bins // 2, 2)
    mesh = jax.sharding.Mesh(mesh.devices.reshape(shape), ("zl", "y", "month", "x", "zh"))
    everywhere = PROV + ("month",) + BIN
    in_specs = (
        P(everywhere, None, None, None),
        P(everywhere),
        P(everywhere),
        P(PROV + ("month",), None),
        P(PROV + BIN, None),
    )
    out_specs = (P(everywhere, None), P(BIN + PROV + ("month",), None))
    return jax.shard_map(shards, mesh=mesh, in_specs=in_specs, out_specs=out_specs, check_vma=False)
```

time: 131 us -> 121 us (0.924)
  Pallas kernels: 14.5 us -> 8.75 us
  starting transfers between devices: 42.1 us -> 39.8 us
  matrix products: 10.3 us -> 8.59 us
  blocking collectives: 20.2 us -> 21.6 us
    pallas_call x1, Pallas kernels: 7.36 us -> 3.83 us  [shards(): pl.pallas_call(first_inverse_kernel, out_shape=(square, square), cost_est...]
    pallas_call x1, Pallas kernels: 7.15 us -> 4.33 us  [shards(): pl.pallas_call(last_kernel, out_shape=jax.ShapeDtypeStruct((out_rows, ran...]
    all_to_all x1, starting transfers between devices: 5.39 us -> 3.41 us  [shards(): lax.all_to_all(jnp.broadcast_to(factor_a[None], (n_bin,) + factor_a.shape...]
    dot_general x2 -> x1, matrix products: 1.96 us -> 0.24 us  [dot32(): lax.dot_general(a, b, (dims, ((), ())), precision=precision, preferred_el...]
    all_to_all x1, blocking collectives: 15.9 us -> 17.2 us  [shards(): lax.all_to_all(jnp.concatenate([sent_c, sent_row], axis=2), ('y',) + GRAM...]
  transfers between devices with their start and end apart: 5 -> 5, of which waited for: 4 -> 3; matrix products, arithmetic and copies ran while one was open for 5% -> 5% of each run, Pallas kernels for 6% -> 4%
where the time goes in v3:
time: 121 us
  starting transfers between devices  39.8 us (33%)
  waiting for transfers between devices  33.8 us (28%)
  blocking collectives  21.6 us (18%)
  Pallas kernels  8.75 us (7%)
  matrix products  8.59 us (7%)
  local copies, waits for them, and re-layouts  6.24 us (5%)
    all_to_all x1, starting transfers between devices, shards(): got = lax.all_to_all(sent, PROV + BIN + ('month',), 0, 0, tiled=True)  22.2 us
    all_to_all x1, blocking collectives, shards(): lax.all_to_all(jnp.concatenate([sent_c, sent_row], axis=2), ('y',) + GRAM...  17.2 us
    all_to_all x1, waiting for transfers between devices, shards(): got = lax.all_to_all(sent, PROV + BIN + ('month',), 0, 0, tiled=True)  16.7 us
    all_to_all x1, waiting for transfers between devices, shards(): lax.all_to_all(jnp.broadcast_to(factor_a[None], (n_bin,) + factor_a.shape...  9.95 us
    all_to_all x1, waiting for transfers between devices, shards(): own_a = lax.all_to_all(pair_a, BIN, 0, 0, tiled=True)  7.1 us
    all_to_all x1, starting transfers between devices, shards(): gram_rows = lax.all_to_all(half_gram[:, None, :], GRAM, 0, 0, tiled=True)  6.45 us
    ppermute x1, starting transfers between devices, shards(): lax.ppermute(half_a, 'month', [(i, n_month - 1 - i) for i in range(n_mont...  4.4 us
    pallas_call x1, Pallas kernels, shards(): pl.pallas_call(last_kernel, out_shape=jax.ShapeDtypeStruct((out_rows, ran...  4.33 us
  transfers between devices with their start and end apart: 5, of which 3 were waited for; matrix products, arithmetic and copies ran while one was open for 5% of the time, Pallas kernels for 4%

profile of v3, /device:TPU:1, one launch (start us, length us, event | category | flops | bytes accessed | tf_op | source)
XLA Modules:
  0.0 120.9 jit_solution(10673300998816818739)
XLA Ops:
  0.7 0.6 copy-done
  1.4 0.7 constant_dynamic-slice_fusion.2
  2.2 0.8 broadcast_in_dim.12
  3.0 22.2 %all-to-all-start = ((bf16[512,2,128]{2,1,0:T(2,128)(2,1)}), bf16[512,2,128]{2,1,0:T(2,128)(2,1)S(1)}, u32[]{:S(2)}, u32[]{:S(2)}) async-start(bf16[512,2,128]{2,1,0:T(2,128)(2,1)} %broadcast_in_dim.12), calls=%async_computation | async-start | bytes 524288 | tf_op jit(solution)/shard_map/all_to_all | solution.py:113
  25.2 0.7 compare_select_fusion.1
  25.9 16.7 %all-to-all-done = bf16[512,2,128]{2,1,0:T(2,128)(2,1)S(1)} async-done(((bf16[512,2,128]{2,1,0:T(2,128)(2,1)}), bf16[512,2,128]{2,1,0:T(2,128)(2,1)S(1)}, u32[]{:S(2)}, u32[]{:S(2)}) %all-to-all-start) | async-done | bytes 262176 | tf_op jit(solution)/shard_map/all_to_all | solution.py:113
  43.2 0.6 gather_fusion
  43.7 3.8 %fusion.1 = f32[8,128,64]{1,2,0:T(8,128)S(1)} fusion(f32[8,16,64]{2,1,0:T(8,128)S(1)} %gather_fusion, bf16[8,128,16,128]{3,2,1,0:T(8,128)(2,1)} %param.5, bf16[128,64]{1,0:T(8,128)(2,1)S(1)} %reshape.57), kind=kOutput, calls=%fused_computation.5 | convolution fusion | flops 270467072 | bytes 4505600 | tf_op jit(solution)/shard_map/tijc,cr->tijr/dot_general | solution.py:124
  48.0 4.3 %all_to_all.30 = f32[2,8,128,64]{2,1,3,0:T(8,128)S(1)} all-to-all(f32[2,8,128,64]{2,1,3,0:T(8,128)S(1)} %fusion.13), channel_id=1, replica_groups=mesh['zl'=4,'y'=8,'month'=2,'x'=4,'zh'=2] {'month'}, dimensions={0} | all-to-all | bytes 1048576 | tf_op jit(solution)/shard_map/all_to_all | solution.py:129
  52.4 0.7 copy.39
  53.1 3.4 %all-to-all-start.2 = ((f32[8,128,64]{1,2,0:T(8,128)}), f32[8,128,64]{1,2,0:T(8,128)S(1)}, u32[]{:S(2)}, u32[]{:S(2)}) async-start(f32[8,128,64]{1,2,0:T(8,128)} %copy.39), calls=%async_computation.2 | async-start | bytes 524288 | tf_op jit(solution)/shard_map/all_to_all | solution.py:132
  56.6 3.8 %first_inverse.1 = (f32[64,64]{1,0:T(8,128)S(1)}, f32[64,64]{1,0:T(8,128)S(1)}) custom-call(bf16[256,64]{1,0:T(8,128)(2,1)S(1)} %bitcast.53, bf16[512,128]{1,0:T(8,128)(2,1)S(1)} %bitcast.51), custom_call_target="tpu_custom_call" | custom-call | flops 20000000 | bytes 200000 | tf_op jit(solution)/shard_map/first_inverse/pallas_call | solution.py:135
  60.4 7.1 %all-to-all-done.2 = f32[8,128,64]{1,2,0:T(8,128)S(1)} async-done(((f32[8,128,64]{1,2,0:T(8,128)}), f32[8,128,64]{1,2,0:T(8,128)S(1)}, u32[]{:S(2)}, u32[]{:S(2)}) %all-to-all-start.2) | async-done | bytes 262176 | tf_op jit(solution)/shard_map/all_to_all | solution.py:132
  67.8 0.7 broadcast_in_dim.14
  68.5 3.4 %all-to-all-start.3 = ((f32[8,128,64]{1,2,0:T(8,128)}), f32[8,128,64]{1,2,0:T(8,128)S(1)}, u32[]{:S(2)}, u32[]{:S(2)}) async-start(f32[8,128,64]{1,2,0:T(8,128)} %broadcast_in_dim.14), calls=%async_computation.3 | async-start | bytes 524288 | tf_op jit(solution)/shard_map/all_to_all | solution.py:145
  71.9 9.9 %all-to-all-done.3 = f32[8,128,64]{1,2,0:T(8,128)S(1)} async-done(((f32[8,128,64]{1,2,0:T(8,128)}), f32[8,128,64]{1,2,0:T(8,128)S(1)}, u32[]{:S(2)}, u32[]{:S(2)}) %all-to-all-start.3) | async-done | bytes 262176 | tf_op jit(solution)/shard_map/all_to_all | solution.py:145
  81.9 4.4 %collective-permute-start = (f32[8,128,64]{1,2,0:T(8,128)S(1)}, f32[8,128,64]{1,2,0:T(8,128)S(1)}, u32[]{:S(2)}, u32[]{:S(2)}) collective-permute-start(f32[8,128,64]{1,2,0:T(8,128)S(1)} %all-to-all-done.3), channel_id=1, source_target_pairs={{0,8},{8,0},{1,9},{9,1},{2,10},{10,2},{3,11},{11,3},{4,12},{12,4},... | collective-permute-start | bytes 786440 | tf_op jit(solution)/shard_map/ppermute | solution.py:152
  86.4 0.6 half_gram.1
  87.0 0.6 copy.40
  87.6 6.4 %all-to-all-start.4 = ((f32[8,1,512]{2,1,0:T(1,128)}), f32[8,1,512]{2,1,0:T(1,128)S(1)}, u32[]{:S(2)}, u32[]{:S(2)}) async-start(f32[8,1,512]{2,1,0:T(1,128)} %copy.40), calls=%async_computation.4 | async-start | bytes 32768 | tf_op jit(solution)/shard_map/all_to_all | solution.py:150
  94.2 0.6 gather_fusion.1
  94.8 4.1 %fusion = f32[128,128]{0,1:T(8,128)S(1)} fusion(f32[8,16,128]{2,1,0:T(8,128)S(1)} %pad_maximum_fusion.1, bf16[8,128,16,128]{3,2,1,0:T(8,128)(2,1)} %param.5, bf16[8,128,128]{1,2,0:T(8,128)(2,1)S(1)} %gather_fusion.1), kind=kOutput, calls=%fused_computation.3 | convolution fusion | flops 541048832 | bytes 4587520 | tf_op jit(solution)/shard_map/tijc,tir->tjcr/dot_general | solution.py:160
  99.3 17.2 %all_to_all.31 = f32[64,1,640]{2,1,0:T(1,128)S(1)} all-to-all(f32[64,1,640]{2,1,0:T(1,128)S(1)} %pad_maximum_fusion), channel_id=1, replica_groups=mesh['zl'=4,'y'=8,'month'=2,'x'=4,'zh'=2] {'y','zl','month'}, dimensions={0} | all-to-all | bytes 327680 | tf_op jit(solution)/shard_map/all_to_all | solution.py:173
  116.6 4.3 %last_solve.1 = f32[2,64]{1,0:T(2,128)} custom-call(f32[64,640]{1,0:T(8,128)S(1)} %bitcast.50, f32[64,64]{1,0:T(8,128)S(1)} %get-tuple-element.15.gram_b_ref), custom_call_target="tpu_custom_call" | custom-call | tf_op jit(solution)/shard_map/last_solve/pallas_call | solution.py:174
  (40 shorter events, 2.1 us)
Async XLA Ops:
  0.6 0.7 copy-start
  3.0 39.6 %all-to-all-start = ((bf16[512,2,128]{2,1,0:T(2,128)(2,1)}), bf16[512,2,128]{2,1,0:T(2,128)(2,1)S(1)}, u32[]{:S(2)}, u32[]{:S(2)}) async-start(bf16[512,2,128]{2,1,0:T(2,128)(2,1)} %broadcast_in_dim.12), calls=%async_computation | async-start | bytes 524288 | tf_op jit(solution)/shard_map/all_to_all | solution.py:113
  42.6 5.0 %copy-start.2 = (s32[8]{0:T(128)S(1)}, s32[8]{0:T(128)}, u32[]{:S(2)}) copy-start(s32[8]{0:T(128)} %param.6) | copy-start | bytes 100
  53.1 14.4 %all-to-all-start.2 = ((f32[8,128,64]{1,2,0:T(8,128)}), f32[8,128,64]{1,2,0:T(8,128)S(1)}, u32[]{:S(2)}, u32[]{:S(2)}) async-start(f32[8,128,64]{1,2,0:T(8,128)} %copy.39), calls=%async_computation.2 | async-start | bytes 524288 | tf_op jit(solution)/shard_map/all_to_all | solution.py:132
  67.8 31.2 %copy-start.1 = (f32[128,64]{0,1:T(8,128)}, f32[128,64]{0,1:T(8,128)S(1)}, u32[]{:S(2)}) copy-start(f32[128,64]{0,1:T(8,128)S(1)} %fusion.21) | copy-start | bytes 98308
  68.5 13.4 %all-to-all-start.3 = ((f32[8,128,64]{1,2,0:T(8,128)}), f32[8,128,64]{1,2,0:T(8,128)S(1)}, u32[]{:S(2)}, u32[]{:S(2)}) async-start(f32[8,128,64]{1,2,0:T(8,128)} %broadcast_in_dim.14), calls=%async_computation.3 | async-start | bytes 524288 | tf_op jit(solution)/shard_map/all_to_all | solution.py:145
  81.9 12.2 %collective-permute-start = (f32[8,128,64]{1,2,0:T(8,128)S(1)}, f32[8,128,64]{1,2,0:T(8,128)S(1)}, u32[]{:S(2)}, u32[]{:S(2)}) collective-permute-start(f32[8,128,64]{1,2,0:T(8,128)S(1)} %all-to-all-done.3), channel_id=1, source_target_pairs={{0,8},{8,0},{1,9},{9,1},{2,10},{10,2},{3,11},{11,3},{4,12},{12,4},... | collective-permute-start | bytes 786440 | tf_op jit(solution)/shard_map/ppermute | solution.py:152
  87.6 11.4 %all-to-all-start.4 = ((f32[8,1,512]{2,1,0:T(1,128)}), f32[8,1,512]{2,1,0:T(1,128)S(1)}, u32[]{:S(2)}, u32[]{:S(2)}) async-start(f32[8,1,512]{2,1,0:T(1,128)} %copy.40), calls=%async_computation.4 | async-start | bytes 32768 | tf_op jit(solution)/shard_map/all_to_all | solution.py:150

commit v4 on v3

--- a/solution.py
+++ b/solution.py
@@ -10,6 +10,7 @@
 epsilon = 1e-06
 HIGH = lax.Precision.HIGHEST
 SMALL = pltpu.CompilerParams(vmem_limit_bytes=8 * 1024 * 1024)
+LARGE = pltpu.CompilerParams(vmem_limit_bytes=52 * 1024 * 1024)
 PROV = ("zl", "y")
 BIN = ("x", "zh")
 GRAM = ("zl", "month")
@@ -50,8 +51,8 @@
 
 
 def first_inverse_kernel(b_ref, pairs_ref, inv_ref, gram_b_ref):
-    rank = b_ref.shape[1]
-    b = b_ref[...]
+    rank = inv_ref.shape[0]
+    b = b_ref[:, :rank]
     gram_b = dot32(b, b, ((0,), (0,)), None)
     z = pairs_ref[...]
     twin = dot32(z, z, ((0,), (0,)), None)
@@ -60,14 +61,79 @@
     inv_ref[...] = spd_inverse(gram_b * gram_c)
 
 
+def tile_copies(tiles_ref, held, sems):
+    copies = [pltpu.make_async_copy(tiles_ref.at[t], held.at[t], sems.at[t]) for t in range(held.shape[0])]
+    for copy in copies:
+        copy.start()
+    return copies
+
+
+def both_halves(held, t):
+    _, tile_i, tile_j, tile_k = held.shape
+    half = tile_i // 2
+    upper = held[t, :half].reshape(half * tile_j, tile_k)
+    lower = held[t, half:].reshape(half * tile_j, tile_k)
+    return jnp.concatenate([upper, lower], axis=1)
+
+
+def first_product_kernel(prov_ref, month_ref, tiles_ref, c_ref, b_ref, out_ref, held, sems):
+    copies = tile_copies(tiles_ref, held, sems)
+    out_ref[...] = jnp.zeros_like(out_ref)
+    c = c_ref[...]
+    zero = jnp.zeros_like(c)
+    twice_c = jnp.concatenate([jnp.concatenate([c, zero], axis=1), jnp.concatenate([zero, c], axis=1)], axis=0)
+    half, tile_j = held.shape[1] // 2, held.shape[2]
+    for t in range(held.shape[0]):
+        copies[t].wait()
+        product = dot32(both_halves(held, t), twice_c, ((1,), (0,)), None)
+        product = product.reshape(half, tile_j, -1) * b_ref[month_ref[t]][None]
+        out_ref[prov_ref[t]] += jnp.sum(product, axis=1)
+
+
+def solve_kernel(got_ref, inv_ref, out_ref, own_ref):
+    rank = inv_ref.shape[0]
+    total = got_ref[0]
+    for source in range(1, got_ref.shape[0]):
+        total = total + got_ref[source]
+    inv = inv_ref[...]
+    upper = dot32(total[:, :rank], inv, ((1,), (0,)))
+    lower = dot32(total[:, rank:], inv, ((1,), (0,)))
+    solved = jnp.concatenate([upper, lower], axis=1)
+    for target in range(out_ref.shape[0]):
+        out_ref[target] = solved
+    own_ref[: upper.shape[0]] = upper
+    own_ref[upper.shape[0] :] = lower
+
+
 def gram_kernel(a_ref, out_ref):
-    rank = a_ref.shape[1]
-    gram = dot32(a_ref[0], a_ref[0], ((1,), (1,)))
-    for block in range(1, a_ref.shape[0]):
-        gram = gram + dot32(a_ref[block], a_ref[block], ((1,), (1,)))
+    rank = a_ref.shape[2] // 2
+    rows = a_ref[...].reshape(-1, 2 * rank)
+    twin = dot32(rows, rows, ((0,), (0,)))
+    gram = twin[:rank, :rank] + twin[rank:, rank:]
     groups = out_ref.shape[0]
     for j in range(rank // groups):
         out_ref[:, j * rank : (j + 1) * rank] = gram[j * groups : (j + 1) * groups]
+
+
+def last_product_kernel(at_ref, month_ref, tiles_ref, a_ref, other_ref, b_ref, out_ref, held, sems, turned):
+    copies = tile_copies(tiles_ref, held, sems)
+    blocks, half, lanes = a_ref.shape
+    rank, tile_j, tile_k = lanes // 2, held.shape[2], held.shape[3]
+    total = None
+    for t in range(held.shape[0]):
+        at = at_ref[t]
+        a = jnp.where(at < blocks, a_ref[at % blocks], other_ref[at % blocks])
+        joint = (a[:, None, :] * b_ref[month_ref[t]][None]).reshape(half * tile_j, lanes)
+        high = joint.astype(jnp.bfloat16)
+        low = (joint - high.astype(jnp.float32)).astype(jnp.bfloat16)
+        copies[t].wait()
+        part = dot32(jnp.concatenate([high, low], axis=1), both_halves(held, t), ((0,), (0,)), None)
+        total = part if total is None else total + part
+    parts = [total[k * rank : (k + 1) * rank, (k % 2) * tile_k : (k % 2 + 1) * tile_k] for k in range(4)]
+    turned[...] = (parts[0] + parts[1] + parts[2] + parts[3]).T
+    out_rows = lanes // rank
+    for row in range(out_rows):
+        out_ref[:, row * rank : (row + 1) * rank] = turned[pl.ds(row, tile_k // out_rows, stride=out_rows), :]
 
 
 def last_kernel(got_ref, gram_b_ref, out_ref):
@@ -78,19 +144,19 @@
     got = got_ref[...]
     rows = jnp.sum(got[:, :lead], axis=0, keepdims=True)
     own = jnp.concatenate([rows[:, j * rank : (j + 1) * rank] for j in range(out_ref.shape[0])], axis=0)
-    folded = got[:groups, lead:]
-    for part in range(1, got.shape[0] // groups):
-        folded = folded + got[part * groups : (part + 1) * groups, lead:]
+    n_zl = groups // 2
+    per = got.shape[0] // n_zl
+    folded = []
+    for zl in range(n_zl):
+        part = jnp.sum(got[zl * per : (zl + 1) * per, lead:].reshape(per // 8, 8, width - lead), axis=0)
+        folded.append((part[0:2] + part[2:4]) + (part[4:6] + part[6:8]))
+    folded = jnp.concatenate(folded, axis=0)
     gram = jnp.concatenate([folded[:, j * rank : (j + 1) * rank] for j in range(rank // groups)], axis=0)
     square_row, square_col = diagonals(gram)
     scale_row = jnp.sqrt(square_row + epsilon)
     scale_col = jnp.sqrt(square_col + epsilon)
     system = gram / scale_col / scale_row * gram_b_ref[...]
     out_ref[...] = dot32(own / scale_row, spd_inverse(system), ((1,), (0,)))
-
-
-def pick(blocks, index):
-    return blocks.at[index].get(mode="promise_in_bounds")
 
 
 def shards(tile_values, prov_block, month_block, factor_b, factor_c):
@@ -112,23 +178,30 @@
     sent = jnp.broadcast_to(chunk[None], (n_all,) + chunk.shape)
     got = lax.all_to_all(sent, PROV + BIN + ("month",), 0, 0, tiled=True)
     pairs_c = got[:, 0, :]
-    whole_b = got[:, 1, :rank].reshape(n_prov, factor_b.shape[0], b_rep, n_month, rank)[:, :, 0]
-    whole_b = whole_b.transpose(0, 2, 1, 3).reshape(-1, rank)
+    twice_b = got[:, 1, :].reshape(n_prov, factor_b.shape[0], b_rep, n_month, c_rows * rank)[:, :, 0]
+    twice_b = twice_b.transpose(0, 2, 1, 3).reshape(-1, c_rows * rank)
 
     slab_pairs = lax.dynamic_slice_in_dim(pairs_c, bin_at * (tile_k // c_rows), tile_k // c_rows, 0)
     slab_c = slab_pairs.reshape(tile_k, rank)
-    slab_b = lax.dynamic_slice_in_dim(whole_b, month * (MB_DEV * tile_j), MB_DEV * tile_j, 0)
-    slab_b = slab_b.astype(jnp.float32).reshape(MB_DEV, tile_j, rank)
-    picked_b = pick(slab_b, month_block)
-
-    partial_y = jnp.einsum("tijc,cr->tijr", tile_values, slab_c, preferred_element_type=jnp.float32)
-    contrib = jnp.sum(partial_y * picked_b[:, None, :, :], axis=2)
-    selector = (prov_block[:, None] == jnp.arange(PB_DEV, dtype=jnp.int32)[None, :]).astype(jnp.float32)
-    partial_a = jnp.einsum("tp,tir->pir", selector, contrib, precision=HIGH)
-
-    pair_a = lax.all_to_all(partial_a.reshape(n_month, n_bin, tile_i, rank), "month", 0, 0, tiled=True)
+    slab_b = lax.dynamic_slice_in_dim(twice_b, month * (MB_DEV * tile_j), MB_DEV * tile_j, 0)
+    slab_b = slab_b.astype(jnp.float32).reshape(MB_DEV, tile_j, c_rows * rank)
+
+    smem, vmem, hbm = (pl.BlockSpec(memory_space=space) for space in (pltpu.SMEM, pltpu.VMEM, pl.ANY))
+    tile_scratch = [pltpu.VMEM(tile_values.shape, tile_values.dtype), pltpu.SemaphoreType.DMA((tiles,))]
+    half = tile_i // 2
+    partial_a = pl.pallas_call(
+        first_product_kernel,
+        out_shape=jax.ShapeDtypeStruct((PB_DEV, half, 2 * rank), jnp.float32),
+        in_specs=[smem, smem, hbm, vmem, vmem],
+        out_specs=vmem,
+        scratch_shapes=tile_scratch,
+        compiler_params=LARGE,
+        name="first_product",
+    )(prov_block, month_block, tile_values, slab_c, slab_b)
+
+    pair_a = lax.all_to_all(partial_a.reshape(n_month, n_bin, half, 2 * rank), "month", 0, 0, tiled=True)
     pair_a = jnp.sum(pair_a, axis=0)
-    whole_b, pairs_c, pair_a = lax.optimization_barrier((whole_b, pairs_c, pair_a))
+    twice_b, pairs_c, pair_a = lax.optimization_barrier((twice_b, pairs_c, pair_a))
     own_a = lax.all_to_all(pair_a, BIN, 0, 0, tiled=True)
 
     square = jax.ShapeDtypeStruct((rank, rank), jnp.float32)
@@ -138,41 +211,51 @@
         cost_estimate=pl.CostEstimate(flops=20000000, bytes_accessed=200000, transcendentals=0),
         name="first_inverse",
         compiler_params=SMALL,
-    )(whole_b, pairs_c)
-    own_a = jnp.sum(own_a, axis=0)
-    factor_a = dot32(own_a, inverse, ((1,), (0,)))
-
-    half_a = lax.all_to_all(jnp.broadcast_to(factor_a[None], (n_bin,) + factor_a.shape), BIN, 0, 0, tiled=True)
+    )(twice_b, pairs_c)
+    spread, factor_a = pl.pallas_call(
+        solve_kernel,
+        out_shape=(
+            jax.ShapeDtypeStruct(own_a.shape, jnp.float32),
+            jax.ShapeDtypeStruct((tile_i, rank), jnp.float32),
+        ),
+        compiler_params=SMALL,
+        name="solve_first",
+    )(own_a, inverse)
+
+    half_a = lax.all_to_all(spread, BIN, 0, 0, tiled=True)
     n_gram = lax.axis_size(GRAM)
     half_gram = pl.pallas_call(
-        gram_kernel, out_shape=jax.ShapeDtypeStruct((n_gram, rank * rank // n_gram), jnp.float32), name="half_gram", compiler_params=SMALL
-    )(half_a.transpose(0, 2, 1))
+        gram_kernel,
+        out_shape=jax.ShapeDtypeStruct((n_gram, rank * rank // n_gram), jnp.float32),
+        compiler_params=SMALL,
+        name="half_gram",
+    )(half_a)
     gram_rows = lax.all_to_all(half_gram[:, None, :], GRAM, 0, 0, tiled=True)
 
     other_a = lax.ppermute(half_a, "month", [(i, n_month - 1 - i) for i in range(n_month)])
 
-    def split(values):
-        high = lax.reduce_precision(values, 8, 7)
-        return jnp.concatenate([high, values - high], axis=2).astype(jnp.bfloat16)
-
-    both = jnp.concatenate([split(half_a), split(other_a)], axis=0)
-    picked_a = pick(both, prov_block ^ (month * n_bin))
-    partial_w = jnp.einsum("tijc,tir->tjcr", tile_values, picked_a, preferred_element_type=jnp.float32)
-    twice_b = jnp.concatenate([picked_b, picked_b], axis=2)
-    partial_c = jnp.sum(partial_w * twice_b[:, :, None, :], axis=(0, 1))
-    partial_c = partial_c[:, :rank] + partial_c[:, rank:]
+    n_out = n_prov * n_month
+    out_rows = tile_k // n_out
+    partial_c = pl.pallas_call(
+        last_product_kernel,
+        out_shape=jax.ShapeDtypeStruct((n_out, out_rows * rank), jnp.float32),
+        in_specs=[smem, smem, hbm, vmem, vmem, vmem],
+        out_specs=vmem,
+        scratch_shapes=tile_scratch + [pltpu.VMEM((tile_k, rank), jnp.float32)],
+        compiler_params=LARGE,
+        name="last_product",
+    )(prov_block ^ (month * n_bin), month_block, tile_values, half_a, other_a, slab_b)
 
     gram_rows, partial_c = lax.optimization_barrier((gram_rows, partial_c))
     gram_row = jnp.sum(gram_rows, axis=0, keepdims=True)
-    n_out = n_prov * n_month
-    out_rows = tile_k // n_out
-    n_y = lax.axis_size("y")
-    sent_c = partial_c.reshape(n_prov // n_y, n_y, n_month, out_rows * rank).transpose(1, 0, 2, 3)
-    sent_c = sent_c.reshape(n_out, 1, out_rows * rank)
     sent_row = jnp.broadcast_to(gram_row, (n_out,) + gram_row.shape[1:])
-    last = lax.all_to_all(jnp.concatenate([sent_c, sent_row], axis=2), ("y",) + GRAM, 0, 0, tiled=True)
+    last = jnp.concatenate([partial_c[:, None, :], sent_row], axis=2)
+    last = lax.all_to_all(last, PROV + ("month",), 0, 0, tiled=True)
     new_c = pl.pallas_call(
-        last_kernel, out_shape=jax.ShapeDtypeStruct((out_rows, rank), jnp.float32), name="last_solve", compiler_params=SMALL
+        last_kernel,
+        out_shape=jax.ShapeDtypeStruct((out_rows, rank), jnp.float32),
+        compiler_params=SMALL,
+        name="last_solve",
     )(last.reshape(n_out, -1), gram_b)
     return (factor_a, new_c)
 

time: 121 us -> 122 us (level)
  Pallas kernels: 8.75 us -> 19.7 us
  matrix products: 8.59 us -> 0 us
  blocking collectives: 21.6 us -> 16.8 us
  starting transfers between devices: 39.8 us -> 42.6 us
    pallas_call x0 -> x3, Pallas kernels: none -> 11 us  [the longest x1 5.57 us: shards(): pl.pallas_call(last_product_kernel, out_shape=jax.ShapeDtypeStruct((n_out...]
    dot_general x4 -> x0, matrix products: 8.59 us -> none  [the longest x1 4.09 us: shards(): jnp.einsum('tijc,tir->tjcr', tile_values, picked_a, preferred_element_typ...]
    all_to_all x2, blocking collectives: 21.6 us -> 16.8 us  [the longest x1 12.5 us: shards(): half_a = lax.all_to_all(spread, BIN, 0, 0, tiled=True)]
    all_to_all x1, starting transfers between devices: 3.41 us -> 6.2 us  [shards(): last = lax.all_to_all(last, PROV + ('month',), 0, 0, tiled=True)]
    unnamed x10 -> x15, local copies, waits for them, and re-layouts: 0.74 us -> 2.74 us
  transfers between devices with their start and end apart: 5 -> 5, of which waited for: 3 -> 3; matrix products, arithmetic and copies ran while one was open for 5% -> 1% of each run, Pallas kernels for 4% -> 8%
where the time goes in v4:
time: 122 us; the launch traced here: 121 us
  starting transfers between devices  42.6 us (35%)
  waiting for transfers between devices  34.1 us (28%)
  Pallas kernels  19.7 us (16%)
  blocking collectives  16.8 us (14%)
  local copies, waits for them, and re-layouts  5.54 us (5%)
  other arithmetic  1.62 us (1%)
    all_to_all x1, starting transfers between devices, shards(): got = lax.all_to_all(sent, PROV + BIN + ('month',), 0, 0, tiled=True)  22.2 us
    all_to_all x1, waiting for transfers between devices, shards(): got = lax.all_to_all(sent, PROV + BIN + ('month',), 0, 0, tiled=True)  17.4 us
    all_to_all x1, blocking collectives, shards(): half_a = lax.all_to_all(spread, BIN, 0, 0, tiled=True)  12.5 us
    all_to_all x1, waiting for transfers between devices, shards(): last = lax.all_to_all(last, PROV + ('month',), 0, 0, tiled=True)  9.52 us
    all_to_all x1, waiting for transfers between devices, shards(): own_a = lax.all_to_all(pair_a, BIN, 0, 0, tiled=True)  7.15 us
    all_to_all x1, starting transfers between devices, shards(): gram_rows = lax.all_to_all(half_gram[:, None, :], GRAM, 0, 0, tiled=True)  6.45 us
    all_to_all x1, starting transfers between devices, shards(): last = lax.all_to_all(last, PROV + ('month',), 0, 0, tiled=True)  6.2 us
    pallas_call x1, Pallas kernels, shards(): pl.pallas_call(last_product_kernel, out_shape=jax.ShapeDtypeStruct((n_out...  5.57 us
  transfers between devices with their start and end apart: 5, of which 3 were waited for; matrix products, arithmetic and copies ran while one was open for 1% of the time, Pallas kernels for 8%

profile of v4, /device:TPU:1, one launch (start us, length us, event | category | flops | bytes accessed | tf_op | source)
XLA Modules:
  0.0 121.1 jit_solution(5736641021293704741)
XLA Ops:
  0.7 0.6 copy-done
  1.4 0.7 constant_dynamic-slice_fusion.2
  2.2 0.8 broadcast_in_dim.8
  3.0 22.2 %all-to-all-start = ((bf16[512,2,128]{2,1,0:T(2,128)(2,1)}), bf16[512,2,128]{2,1,0:T(2,128)(2,1)S(1)}, u32[]{:S(2)}, u32[]{:S(2)}) async-start(bf16[512,2,128]{2,1,0:T(2,128)(2,1)} %broadcast_in_dim.8), calls=%async_computation | async-start | bytes 524288 | tf_op jit(solution)/shard_map/all_to_all | solution.py:179
  25.2 17.4 %all-to-all-done = bf16[512,2,128]{2,1,0:T(2,128)(2,1)S(1)} async-done(((bf16[512,2,128]{2,1,0:T(2,128)(2,1)}), bf16[512,2,128]{2,1,0:T(2,128)(2,1)S(1)}, u32[]{:S(2)}, u32[]{:S(2)}) %all-to-all-start) | async-done | bytes 262176 | tf_op jit(solution)/shard_map/all_to_all | solution.py:179
  43.3 0.7 copy-done.1
  43.9 0.7 copy-done.3
  44.6 5.1 %first_product.1 = f32[16,64,128]{2,1,0:T(8,128)S(1)} custom-call(s32[8]{0:T(128)S(1)} %copy-done.3, s32[8]{0:T(128)S(1)} %copy-done.1, bf16[8,128,16,128]{3,2,1,0:T(8,128)(2,1)} %tiles_ref.3, bf16[128,64]{1,0:T(8,128)(2,1)S(1)} %reshape.34.c_ref, f32[8,16,128]{2,1,0:T(8,128)S(1)} %convert.1.b_ref), custom_call_target="tpu_custom_call" | custom-call | tf_op jit(solution)/shard_map/first_product/pallas_call | solution.py:192
  49.7 4.3 %all_to_all.30 = f32[2,8,64,128]{3,2,1,0:T(8,128)S(1)} all-to-all(f32[2,8,64,128]{3,2,1,0:T(8,128)S(1)} %bitcast.21), channel_id=1, replica_groups=mesh['zl'=4,'y'=8,'month'=2,'x'=4,'zh'=2] {'month'}, dimensions={0} | all-to-all | bytes 1048576 | tf_op jit(solution)/shard_map/all_to_all | solution.py:202
  54.0 0.7 reduce_sum.18
  54.7 3.4 %all-to-all-start.2 = ((f32[8,64,128]{2,1,0:T(8,128)}), f32[8,64,128]{2,1,0:T(8,128)S(1)}, u32[]{:S(2)}, u32[]{:S(2)}) async-start(f32[8,64,128]{2,1,0:T(8,128)} %reduce_sum.18), calls=%async_computation.2 | async-start | bytes 524288 | tf_op jit(solution)/shard_map/all_to_all | solution.py:205
  58.2 3.8 %first_inverse.1 = (f32[64,64]{1,0:T(8,128)S(1)}, f32[64,64]{1,0:T(8,128)S(1)}) custom-call(bf16[256,128]{1,0:T(8,128)(2,1)S(1)} %bitcast.25, bf16[512,128]{1,0:T(8,128)(2,1)S(1)} %bitcast.23), custom_call_target="tpu_custom_call" | custom-call | flops 20000000 | bytes 200000 | tf_op jit(solution)/shard_map/first_inverse/pallas_call | solution.py:208
  62.0 7.1 %all-to-all-done.2.got_ref = f32[8,64,128]{2,1,0:T(8,128)S(1)} async-done(((f32[8,64,128]{2,1,0:T(8,128)}), f32[8,64,128]{2,1,0:T(8,128)S(1)}, u32[]{:S(2)}, u32[]{:S(2)}) %all-to-all-start.2) | async-done | bytes 262176 | tf_op jit(solution)/shard_map/all_to_all | solution.py:205
  69.5 12.5 %all_to_all.31.a_ref = f32[8,64,128]{2,1,0:T(8,128)S(1)} all-to-all(f32[8,64,128]{2,1,0:T(8,128)S(1)} %get-tuple-element.16), channel_id=1, replica_groups=mesh['zl'=4,'y'=8,'month'=2,'x'=4,'zh'=2] {'x','zh'}, dimensions={0} | all-to-all | bytes 524288 | tf_op jit(solution)/shard_map/all_to_all | solution.py:225
  81.9 4.3 %collective-permute-start = (f32[8,64,128]{2,1,0:T(8,128)S(1)}, f32[8,64,128]{2,1,0:T(8,128)S(1)}, u32[]{:S(2)}, u32[]{:S(2)}) collective-permute-start(f32[8,64,128]{2,1,0:T(8,128)S(1)} %all_to_all.31.a_ref), channel_id=1, source_target_pairs={{0,8},{8,0},{1,9},{9,1},{2,10},{10,2},{3,11},{11,3},{4,12},{12,4},... | collective-permute-start | bytes 786440 | tf_op jit(solution)/shard_map/ppermute | solution.py:235
  86.3 0.6 half_gram.1
  86.8 0.6 copy.19
  87.5 6.5 %all-to-all-start.4 = ((f32[8,1,512]{2,1,0:T(1,128)}), f32[8,1,512]{2,1,0:T(1,128)S(1)}, u32[]{:S(2)}, u32[]{:S(2)}) async-start(f32[8,1,512]{2,1,0:T(1,128)} %copy.19), calls=%async_computation.4 | async-start | bytes 32768 | tf_op jit(solution)/shard_map/all_to_all | solution.py:233
  93.9 5.6 %last_product.1 = f32[64,128]{1,0:T(8,128)S(1)} custom-call(s32[8]{0:T(128)S(1)} %broadcast_xor_fusion.at_ref, s32[8]{0:T(128)S(1)} %copy-done.2, bf16[8,128,16,128]{3,2,1,0:T(8,128)(2,1)} %tiles_ref.3, f32[8,64,128]{2,1,0:T(8,128)S(1)} %all_to_all.31.a_ref, f32[8,64,128]{2,1,0:T(8,128)S(1)} %collective-permute-done.other_ref, f32[8,16,128]{2,1,0:T(8,128)S(1)} %convert.1.b_ref), custom_call_target="tpu_custom_call" | custom-call | tf_op jit(solution)/shard_map/last_product/pallas_call | solution.py:239
  99.6 0.8 pad_maximum_fusion
  100.3 6.2 %all-to-all-start.5 = ((f32[64,1,640]{2,1,0:T(1,128)}), f32[64,1,640]{2,1,0:T(1,128)S(1)}, u32[]{:S(2)}, u32[]{:S(2)}) async-start(f32[64,1,640]{2,1,0:T(1,128)} %pad_maximum_fusion), calls=%async_computation.5 | async-start | bytes 327680 | tf_op jit(solution)/shard_map/all_to_all | solution.py:253
  106.5 0.7 copy.21
  107.2 9.5 %all-to-all-done.5 = f32[64,1,640]{2,1,0:T(1,128)S(1)} async-done(((f32[64,1,640]{2,1,0:T(1,128)}), f32[64,1,640]{2,1,0:T(1,128)S(1)}, u32[]{:S(2)}, u32[]{:S(2)}) %all-to-all-start.5) | async-done | bytes 163872 | tf_op jit(solution)/shard_map/all_to_all | solution.py:253
  116.8 4.3 %last_solve.1 = f32[2,64]{1,0:T(2,128)} custom-call(f32[64,640]{1,0:T(8,128)S(1)} %bitcast.22, f32[64,64]{1,0:T(8,128)S(1)} %get-tuple-element.19.gram_b_ref), custom_call_target="tpu_custom_call" | custom-call | tf_op jit(solution)/shard_map/last_solve/pallas_call | solution.py:254
  (27 shorter events, 1.2 us)
Async XLA Ops:
  0.6 0.7 copy-start
  3.0 39.6 %all-to-all-start = ((bf16[512,2,128]{2,1,0:T(2,128)(2,1)}), bf16[512,2,128]{2,1,0:T(2,128)(2,1)S(1)}, u32[]{:S(2)}, u32[]{:S(2)}) async-start(bf16[512,2,128]{2,1,0:T(2,128)(2,1)} %broadcast_in_dim.8), calls=%async_computation | async-start | bytes 524288 | tf_op jit(solution)/shard_map/all_to_all | solution.py:179
  43.3 0.7 copy-start.1
  43.9 0.7 copy-start.3
  44.6 49.4 %copy-start.4 = (s32[8]{0:T(128)S(1)}, s32[8]{0:T(128)}, u32[]{:S(2)}) copy-start(s32[8]{0:T(128)} %prov_ref.1) | copy-start | bytes 100
  44.6 49.4 %copy-start.2 = (s32[8]{0:T(128)S(1)}, s32[8]{0:T(128)}, u32[]{:S(2)}) copy-start(s32[8]{0:T(128)} %month_ref.3) | copy-start | bytes 100
  54.7 14.4 %all-to-all-start.2 = ((f32[8,64,128]{2,1,0:T(8,128)}), f32[8,64,128]{2,1,0:T(8,128)S(1)}, u32[]{:S(2)}, u32[]{:S(2)}) async-start(f32[8,64,128]{2,1,0:T(8,128)} %reduce_sum.18), calls=%async_computation.2 | async-start | bytes 524288 | tf_op jit(solution)/shard_map/all_to_all | solution.py:205
  81.9 12.0 %collective-permute-start = (f32[8,64,128]{2,1,0:T(8,128)S(1)}, f32[8,64,128]{2,1,0:T(8,128)S(1)}, u32[]{:S(2)}, u32[]{:S(2)}) collective-permute-start(f32[8,64,128]{2,1,0:T(8,128)S(1)} %all_to_all.31.a_ref), channel_id=1, source_target_pairs={{0,8},{8,0},{1,9},{9,1},{2,10},{10,2},{3,11},{11,3},{4,12},{12,4},... | collective-permute-start | bytes 786440 | tf_op jit(solution)/shard_map/ppermute | solution.py:235
  87.5 12.1 %all-to-all-start.4 = ((f32[8,1,512]{2,1,0:T(1,128)}), f32[8,1,512]{2,1,0:T(1,128)S(1)}, u32[]{:S(2)}, u32[]{:S(2)}) async-start(f32[8,1,512]{2,1,0:T(1,128)} %copy.19), calls=%async_computation.4 | async-start | bytes 32768 | tf_op jit(solution)/shard_map/all_to_all | solution.py:233
  100.3 16.4 %all-to-all-start.5 = ((f32[64,1,640]{2,1,0:T(1,128)}), f32[64,1,640]{2,1,0:T(1,128)S(1)}, u32[]{:S(2)}, u32[]{:S(2)}) async-start(f32[64,1,640]{2,1,0:T(1,128)} %pad_maximum_fusion), calls=%async_computation.5 | async-start | bytes 327680 | tf_op jit(solution)/shard_map/all_to_all | solution.py:253

commit v5 on v4

--- a/solution.py
+++ b/solution.py
@@ -6,11 +6,12 @@
 from jax.sharding import PartitionSpec as P
 
 MB_DEV = 8
+KEPT = 5
 PB_DEV = 16
 epsilon = 1e-06
 HIGH = lax.Precision.HIGHEST
 SMALL = pltpu.CompilerParams(vmem_limit_bytes=8 * 1024 * 1024)
-LARGE = pltpu.CompilerParams(vmem_limit_bytes=52 * 1024 * 1024)
+LARGE = pltpu.CompilerParams(vmem_limit_bytes=50 * 1024 * 1024)
 PROV = ("zl", "y")
 BIN = ("x", "zh")
 GRAM = ("zl", "month")
@@ -61,33 +62,44 @@
     inv_ref[...] = spd_inverse(gram_b * gram_c)
 
 
-def tile_copies(tiles_ref, held, sems):
-    copies = [pltpu.make_async_copy(tiles_ref.at[t], held.at[t], sems.at[t]) for t in range(held.shape[0])]
+def keep_kernel(tiles_ref, kept_ref, sem):
+    copy = pltpu.make_async_copy(tiles_ref.at[pl.ds(0, kept_ref.shape[0])], kept_ref, sem)
+    copy.start()
+    copy.wait()
+
+
+def tile_copies(tiles_ref, late, sems):
+    kept = tiles_ref.shape[0] - late.shape[0]
+    copies = [pltpu.make_async_copy(tiles_ref.at[kept + t], late.at[t], sems.at[t]) for t in range(late.shape[0])]
     for copy in copies:
         copy.start()
-    return copies
-
-
-def both_halves(held, t):
-    _, tile_i, tile_j, tile_k = held.shape
-    half = tile_i // 2
-    upper = held[t, :half].reshape(half * tile_j, tile_k)
-    lower = held[t, half:].reshape(half * tile_j, tile_k)
+    return [None] * kept + copies
+
+
+def both_halves(kept_ref, late, t, start, size):
+    kept, tile_i, tile_j, tile_k = kept_ref.shape
+    tile, at = (kept_ref, t) if t < kept else (late, t - kept)
+    upper = tile[at, start : start + size].reshape(size * tile_j, tile_k)
+    lower = tile[at, tile_i // 2 + start : tile_i // 2 + start + size].reshape(size * tile_j, tile_k)
     return jnp.concatenate([upper, lower], axis=1)
 
 
-def first_product_kernel(prov_ref, month_ref, tiles_ref, c_ref, b_ref, out_ref, held, sems):
-    copies = tile_copies(tiles_ref, held, sems)
+def first_product_kernel(prov_ref, month_ref, tiles_ref, kept_ref, c_ref, b_ref, out_ref, late, sems):
+    copies = tile_copies(tiles_ref, late, sems)
     out_ref[...] = jnp.zeros_like(out_ref)
     c = c_ref[...]
     zero = jnp.zeros_like(c)
     twice_c = jnp.concatenate([jnp.concatenate([c, zero], axis=1), jnp.concatenate([zero, c], axis=1)], axis=0)
-    half, tile_j = held.shape[1] // 2, held.shape[2]
-    for t in range(held.shape[0]):
-        copies[t].wait()
-        product = dot32(both_halves(held, t), twice_c, ((1,), (0,)), None)
-        product = product.reshape(half, tile_j, -1) * b_ref[month_ref[t]][None]
-        out_ref[prov_ref[t]] += jnp.sum(product, axis=1)
+    half, tile_j = tiles_ref.shape[1] // 2, tiles_ref.shape[2]
+    size = half // 4
+    for t, copy in enumerate(copies):
+        if copy is not None:
+            copy.wait()
+        b = b_ref[month_ref[t]][None]
+        for start in range(0, half, size):
+            product = dot32(both_halves(kept_ref, late, t, start, size), twice_c, ((1,), (0,)), None)
+            product = product.reshape(size, tile_j, -1) * b
+            out_ref[prov_ref[t], start : start + size] += jnp.sum(product, axis=1)
 
 
 def solve_kernel(got_ref, inv_ref, out_ref, own_ref):
@@ -115,20 +127,26 @@
         out_ref[:, j * rank : (j + 1) * rank] = gram[j * groups : (j + 1) * groups]
 
 
-def last_product_kernel(at_ref, month_ref, tiles_ref, a_ref, other_ref, b_ref, out_ref, held, sems, turned):
-    copies = tile_copies(tiles_ref, held, sems)
+def last_product_kernel(at_ref, month_ref, tiles_ref, kept_ref, a_ref, other_ref, b_ref, out_ref, late, sems, turned):
+    copies = tile_copies(tiles_ref, late, sems)
     blocks, half, lanes = a_ref.shape
-    rank, tile_j, tile_k = lanes // 2, held.shape[2], held.shape[3]
+    rank, tile_j, tile_k = lanes // 2, tiles_ref.shape[2], tiles_ref.shape[3]
+    size = half // 4
     total = None
-    for t in range(held.shape[0]):
+    for t, copy in enumerate(copies):
+        if copy is not None:
+            copy.wait()
         at = at_ref[t]
-        a = jnp.where(at < blocks, a_ref[at % blocks], other_ref[at % blocks])
-        joint = (a[:, None, :] * b_ref[month_ref[t]][None]).reshape(half * tile_j, lanes)
-        high = joint.astype(jnp.bfloat16)
-        low = (joint - high.astype(jnp.float32)).astype(jnp.bfloat16)
-        copies[t].wait()
-        part = dot32(jnp.concatenate([high, low], axis=1), both_halves(held, t), ((0,), (0,)), None)
-        total = part if total is None else total + part
+        b = b_ref[month_ref[t]][None]
+        for start in range(0, half, size):
+            rows = pl.ds(start, size)
+            a = jnp.where(at < blocks, a_ref[at % blocks, rows], other_ref[at % blocks, rows])
+            joint = (a[:, None, :] * b).reshape(size * tile_j, lanes).T
+            high = joint.astype(jnp.bfloat16)
+            low = (joint - high.astype(jnp.float32)).astype(jnp.bfloat16)
+            both = jnp.concatenate([high, low], axis=0)
+            part = dot32(both, both_halves(kept_ref, late, t, start, size), ((1,), (0,)), None)
+            total = part if total is None else total + part
     parts = [total[k * rank : (k + 1) * rank, (k % 2) * tile_k : (k % 2 + 1) * tile_k] for k in range(4)]
     turned[...] = (parts[0] + parts[1] + parts[2] + parts[3]).T
     out_rows = lanes // rank
@@ -187,17 +205,32 @@
     slab_b = slab_b.astype(jnp.float32).reshape(MB_DEV, tile_j, c_rows * rank)
 
     smem, vmem, hbm = (pl.BlockSpec(memory_space=space) for space in (pltpu.SMEM, pltpu.VMEM, pl.ANY))
-    tile_scratch = [pltpu.VMEM(tile_values.shape, tile_values.dtype), pltpu.SemaphoreType.DMA((tiles,))]
+    kept = pl.pallas_call(
+        keep_kernel,
+        out_shape=jax.ShapeDtypeStruct((KEPT,) + tile_values.shape[1:], tile_values.dtype),
+        in_specs=[hbm],
+        out_specs=vmem,
+        scratch_shapes=[pltpu.SemaphoreType.DMA],
+        compiler_params=LARGE,
+        name="keep_tiles",
+    )(tile_values)
+    late = tiles - KEPT
+    tile_scratch = [
+        pltpu.VMEM((late,) + tile_values.shape[1:], tile_values.dtype),
+        pltpu.SemaphoreType.DMA((late,)),
+    ]
     half = tile_i // 2
+    prov_at = jnp.clip(prov_block, 0, PB_DEV - 1)
+    month_at = jnp.clip(month_block, 0, MB_DEV - 1)
     partial_a = pl.pallas_call(
         first_product_kernel,
         out_shape=jax.ShapeDtypeStruct((PB_DEV, half, 2 * rank), jnp.float32),
-        in_specs=[smem, smem, hbm, vmem, vmem],
+        in_specs=[smem, smem, hbm, vmem, vmem, vmem],
         out_specs=vmem,
         scratch_shapes=tile_scratch,
         compiler_params=LARGE,
         name="first_product",
-    )(prov_block, month_block, tile_values, slab_c, slab_b)
+    )(prov_at, month_at, tile_values, kept, slab_c, slab_b)
 
     pair_a = lax.all_to_all(partial_a.reshape(n_month, n_bin, half, 2 * rank), "month", 0, 0, tiled=True)
     pair_a = jnp.sum(pair_a, axis=0)
@@ -239,12 +272,12 @@
     partial_c = pl.pallas_call(
         last_product_kernel,
         out_shape=jax.ShapeDtypeStruct((n_out, out_rows * rank), jnp.float32),
-        in_specs=[smem, smem, hbm, vmem, vmem, vmem],
+        in_specs=[smem, smem, hbm, vmem, vmem, vmem, vmem],
         out_specs=vmem,
         scratch_shapes=tile_scratch + [pltpu.VMEM((tile_k, rank), jnp.float32)],
         compiler_params=LARGE,
         name="last_product",
-    )(prov_block ^ (month * n_bin), month_block, tile_values, half_a, other_a, slab_b)
+    )(prov_at ^ (month * n_bin), month_at, tile_values, kept, half_a, other_a, slab_b)
 
     gram_rows, partial_c = lax.optimization_barrier((gram_rows, partial_c))
     gram_row = jnp.sum(gram_rows, axis=0, keepdims=True)

time: 122 us -> 117 us (0.959)
  Pallas kernels: 19.7 us -> 17.9 us
  local copies, waits for them, and re-layouts: 5.54 us -> 4.22 us
    pallas_call x1, Pallas kernels: 5.09 us -> 3.23 us  [shards(): pl.pallas_call(first_product_kernel, out_shape=jax.ShapeDtypeStruct((PB_D...]
    all_to_all x1, waiting for transfers between devices: 17.4 us -> 15.6 us  [shards(): got = lax.all_to_all(sent, PROV + BIN + ('month',), 0, 0, tiled=True)]
    pallas_call x0 -> x1, Pallas kernels: none -> 1.75 us  [shards(): pl.pallas_call(keep_kernel, out_shape=jax.ShapeDtypeStruct((KEPT,) + tile...]
    pallas_call x1, Pallas kernels: 5.57 us -> 3.84 us  [shards(): pl.pallas_call(last_product_kernel, out_shape=jax.ShapeDtypeStruct((n_out...]
    unnamed x15 -> x11, local copies, waits for them, and re-layouts: 2.74 us -> 1.42 us
  transfers between devices with their start and end apart: 5 -> 5, of which waited for: 3 -> 4; matrix products, arithmetic and copies ran while one was open for 1% -> 1% of each run, Pallas kernels for 8% -> 9%
where the time goes in v5:
time: 117 us; the launch traced here: 116 us
  starting transfers between devices  41.5 us (35%)
  waiting for transfers between devices  33.3 us (28%)
  Pallas kernels  17.9 us (15%)
  blocking collectives  16.8 us (14%)
  local copies, waits for them, and re-layouts  4.22 us (4%)
  other arithmetic  1.62 us (1%)
    all_to_all x1, starting transfers between devices, shards(): got = lax.all_to_all(sent, PROV + BIN + ('month',), 0, 0, tiled=True)  22.2 us
    all_to_all x1, waiting for transfers between devices, shards(): got = lax.all_to_all(sent, PROV + BIN + ('month',), 0, 0, tiled=True)  15.6 us
    all_to_all x1, blocking collectives, shards(): half_a = lax.all_to_all(spread, BIN, 0, 0, tiled=True)  12.5 us
    all_to_all x1, waiting for transfers between devices, shards(): last = lax.all_to_all(last, PROV + ('month',), 0, 0, tiled=True)  9.52 us
    all_to_all x1, waiting for transfers between devices, shards(): own_a = lax.all_to_all(pair_a, BIN, 0, 0, tiled=True)  7.15 us
    all_to_all x1, starting transfers between devices, shards(): gram_rows = lax.all_to_all(half_gram[:, None, :], GRAM, 0, 0, tiled=True)  6.46 us
    all_to_all x1, starting transfers between devices, shards(): last = lax.all_to_all(last, PROV + ('month',), 0, 0, tiled=True)  5.11 us
    all_to_all x1, blocking collectives, shards(): lax.all_to_all(partial_a.reshape(n_month, n_bin, half, 2 * rank), 'month'...  4.38 us
  transfers between devices with their start and end apart: 5, of which 4 were waited for; matrix products, arithmetic and copies ran while one was open for 1% of the time, Pallas kernels for 9%

profile of v5, /device:TPU:1, one launch (start us, length us, event | category | flops | bytes accessed | tf_op | source)
XLA Modules:
  0.0 116.2 jit_solution(6147064401046444369)
XLA Ops:
  0.7 0.6 copy-done
  1.4 0.7 constant_dynamic-slice_fusion.2
  2.2 0.8 broadcast_in_dim.8
  3.0 22.2 %all-to-all-start = ((bf16[512,2,128]{2,1,0:T(2,128)(2,1)}), bf16[512,2,128]{2,1,0:T(2,128)(2,1)S(1)}, u32[]{:S(2)}, u32[]{:S(2)}) async-start(bf16[512,2,128]{2,1,0:T(2,128)(2,1)} %broadcast_in_dim.8), calls=%async_computation | async-start | bytes 524288 | tf_op jit(solution)/shard_map/all_to_all | solution.py:197
  25.2 1.8 %keep_tiles.1.kept_ref = bf16[5,128,16,128]{3,2,1,0:T(8,128)(2,1)S(1)} custom-call(bf16[8,128,16,128]{3,2,1,0:T(8,128)(2,1)} %tiles_ref.5), custom_call_target="tpu_custom_call" | custom-call | tf_op jit(solution)/shard_map/keep_tiles/pallas_call | solution.py:208
  27.0 15.6 %all-to-all-done = bf16[512,2,128]{2,1,0:T(2,128)(2,1)S(1)} async-done(((bf16[512,2,128]{2,1,0:T(2,128)(2,1)}), bf16[512,2,128]{2,1,0:T(2,128)(2,1)S(1)}, u32[]{:S(2)}, u32[]{:S(2)}) %all-to-all-start) | async-done | bytes 262176 | tf_op jit(solution)/shard_map/all_to_all | solution.py:197
  43.2 3.2 %first_product.1 = f32[16,64,128]{2,1,0:T(8,128)S(1)} custom-call(s32[8]{0:T(128)S(1)} %get-tuple-element.31.prov_ref, s32[8]{0:T(128)S(1)} %get-tuple-element.32.month_ref, bf16[8,128,16,128]{3,2,1,0:T(8,128)(2,1)} %tiles_ref.5, bf16[5,128,16,128]{3,2,1,0:T(8,128)(2,1)S(1)} %keep_tiles.1.kept_ref, bf16[128,64]{1,0:T(8,128)(2,1)S(1)} %reshape.34.c_ref, ...), custom_call_target="tpu_custom_call" | custom-call | tf_op jit(solution)/shard_map/first_product/pallas_call | solution.py:225
  46.5 4.4 %all_to_all.30 = f32[2,8,64,128]{3,2,1,0:T(8,128)S(1)} all-to-all(f32[2,8,64,128]{3,2,1,0:T(8,128)S(1)} %bitcast.21), channel_id=1, replica_groups=mesh['zl'=4,'y'=8,'month'=2,'x'=4,'zh'=2] {'month'}, dimensions={0} | all-to-all | bytes 1048576 | tf_op jit(solution)/shard_map/all_to_all | solution.py:235
  50.9 0.7 reduce_sum.18
  51.6 3.4 %all-to-all-start.2 = ((f32[8,64,128]{2,1,0:T(8,128)}), f32[8,64,128]{2,1,0:T(8,128)S(1)}, u32[]{:S(2)}, u32[]{:S(2)}) async-start(f32[8,64,128]{2,1,0:T(8,128)} %reduce_sum.18), calls=%async_computation.2 | async-start | bytes 524288 | tf_op jit(solution)/shard_map/all_to_all | solution.py:238
  55.0 3.8 %first_inverse.1 = (f32[64,64]{1,0:T(8,128)S(1)}, f32[64,64]{1,0:T(8,128)S(1)}) custom-call(bf16[256,128]{1,0:T(8,128)(2,1)S(1)} %bitcast.25, bf16[512,128]{1,0:T(8,128)(2,1)S(1)} %bitcast.23), custom_call_target="tpu_custom_call" | custom-call | flops 20000000 | bytes 200000 | tf_op jit(solution)/shard_map/first_inverse/pallas_call | solution.py:241
  58.9 7.1 %all-to-all-done.2.got_ref = f32[8,64,128]{2,1,0:T(8,128)S(1)} async-done(((f32[8,64,128]{2,1,0:T(8,128)}), f32[8,64,128]{2,1,0:T(8,128)S(1)}, u32[]{:S(2)}, u32[]{:S(2)}) %all-to-all-start.2) | async-done | bytes 262176 | tf_op jit(solution)/shard_map/all_to_all | solution.py:238
  66.3 12.5 %all_to_all.31.a_ref = f32[8,64,128]{2,1,0:T(8,128)S(1)} all-to-all(f32[8,64,128]{2,1,0:T(8,128)S(1)} %get-tuple-element.16), channel_id=1, replica_groups=mesh['zl'=4,'y'=8,'month'=2,'x'=4,'zh'=2] {'x','zh'}, dimensions={0} | all-to-all | bytes 524288 | tf_op jit(solution)/shard_map/all_to_all | solution.py:258
  78.8 4.3 %collective-permute-start = (f32[8,64,128]{2,1,0:T(8,128)S(1)}, f32[8,64,128]{2,1,0:T(8,128)S(1)}, u32[]{:S(2)}, u32[]{:S(2)}) collective-permute-start(f32[8,64,128]{2,1,0:T(8,128)S(1)} %all_to_all.31.a_ref), channel_id=1, source_target_pairs={{0,8},{8,0},{1,9},{9,1},{2,10},{10,2},{3,11},{11,3},{4,12},{12,4},... | collective-permute-start | bytes 786440 | tf_op jit(solution)/shard_map/ppermute | solution.py:268
  83.1 0.6 half_gram.1
  83.7 0.6 copy.19
  84.3 6.5 %all-to-all-start.4 = ((f32[8,1,512]{2,1,0:T(1,128)}), f32[8,1,512]{2,1,0:T(1,128)S(1)}, u32[]{:S(2)}, u32[]{:S(2)}) async-start(f32[8,1,512]{2,1,0:T(1,128)} %copy.19), calls=%async_computation.4 | async-start | bytes 32768 | tf_op jit(solution)/shard_map/all_to_all | solution.py:266
  90.8 3.8 %last_product.1 = f32[64,128]{1,0:T(8,128)S(1)} custom-call(s32[8]{0:T(128)S(1)} %get-tuple-element.30.at_ref, s32[8]{0:T(128)S(1)} %get-tuple-element.32.month_ref, bf16[8,128,16,128]{3,2,1,0:T(8,128)(2,1)} %tiles_ref.5, bf16[5,128,16,128]{3,2,1,0:T(8,128)(2,1)S(1)} %keep_tiles.1.kept_ref, f32[8,64,128]{2,1,0:T(8,128)S(1)} %all_to_all.31.a_ref, ...), custom_call_target="tpu_custom_call" | custom-call | tf_op jit(solution)/shard_map/last_product/pallas_call | solution.py:272
  94.6 1.1 all-to-all-done.4
  95.7 0.8 pad_maximum_fusion
  96.5 5.1 %all-to-all-start.5 = ((f32[64,1,640]{2,1,0:T(1,128)}), f32[64,1,640]{2,1,0:T(1,128)S(1)}, u32[]{:S(2)}, u32[]{:S(2)}) async-start(f32[64,1,640]{2,1,0:T(1,128)} %pad_maximum_fusion), calls=%async_computation.5 | async-start | bytes 327680 | tf_op jit(solution)/shard_map/all_to_all | solution.py:286
  101.6 0.7 copy.21
  102.3 9.5 %all-to-all-done.5 = f32[64,1,640]{2,1,0:T(1,128)S(1)} async-done(((f32[64,1,640]{2,1,0:T(1,128)}), f32[64,1,640]{2,1,0:T(1,128)S(1)}, u32[]{:S(2)}, u32[]{:S(2)}) %all-to-all-start.5) | async-done | bytes 163872 | tf_op jit(solution)/shard_map/all_to_all | solution.py:286
  111.8 4.3 %last_solve.1 = f32[2,64]{1,0:T(2,128)} custom-call(f32[64,640]{1,0:T(8,128)S(1)} %bitcast.22, f32[64,64]{1,0:T(8,128)S(1)} %get-tuple-element.19.gram_b_ref), custom_call_target="tpu_custom_call" | custom-call | tf_op jit(solution)/shard_map/last_solve/pallas_call | solution.py:287
  (24 shorter events, 1.2 us)
Async XLA Ops:
  0.6 0.7 copy-start
  0.6 26.3 %copy-start.2 = (s32[8]{0:T(128)S(1)}, s32[8]{0:T(128)}, u32[]{:S(2)}) copy-start(s32[8]{0:T(128)} %param.7) | copy-start | bytes 100
  0.7 26.3 %copy-start.1 = (s32[8]{0:T(128)S(1)}, s32[8]{0:T(128)}, u32[]{:S(2)}) copy-start(s32[8]{0:T(128)} %param.6) | copy-start | bytes 100
  3.0 39.5 %all-to-all-start = ((bf16[512,2,128]{2,1,0:T(2,128)(2,1)}), bf16[512,2,128]{2,1,0:T(2,128)(2,1)S(1)}, u32[]{:S(2)}, u32[]{:S(2)}) async-start(bf16[512,2,128]{2,1,0:T(2,128)(2,1)} %broadcast_in_dim.8), calls=%async_computation | async-start | bytes 524288 | tf_op jit(solution)/shard_map/all_to_all | solution.py:197
  51.6 14.4 %all-to-all-start.2 = ((f32[8,64,128]{2,1,0:T(8,128)}), f32[8,64,128]{2,1,0:T(8,128)S(1)}, u32[]{:S(2)}, u32[]{:S(2)}) async-start(f32[8,64,128]{2,1,0:T(8,128)} %reduce_sum.18), calls=%async_computation.2 | async-start | bytes 524288 | tf_op jit(solution)/shard_map/all_to_all | solution.py:238
  78.8 12.0 %collective-permute-start = (f32[8,64,128]{2,1,0:T(8,128)S(1)}, f32[8,64,128]{2,1,0:T(8,128)S(1)}, u32[]{:S(2)}, u32[]{:S(2)}) collective-permute-start(f32[8,64,128]{2,1,0:T(8,128)S(1)} %all_to_all.31.a_ref), channel_id=1, source_target_pairs={{0,8},{8,0},{1,9},{9,1},{2,10},{10,2},{3,11},{11,3},{4,12},{12,4},... | collective-permute-start | bytes 786440 | tf_op jit(solution)/shard_map/ppermute | solution.py:268
  84.3 11.4 %all-to-all-start.4 = ((f32[8,1,512]{2,1,0:T(1,128)}), f32[8,1,512]{2,1,0:T(1,128)S(1)}, u32[]{:S(2)}, u32[]{:S(2)}) async-start(f32[8,1,512]{2,1,0:T(1,128)} %copy.19), calls=%async_computation.4 | async-start | bytes 32768 | tf_op jit(solution)/shard_map/all_to_all | solution.py:266
  96.5 15.3 %all-to-all-start.5 = ((f32[64,1,640]{2,1,0:T(1,128)}), f32[64,1,640]{2,1,0:T(1,128)S(1)}, u32[]{:S(2)}, u32[]{:S(2)}) async-start(f32[64,1,640]{2,1,0:T(1,128)} %pad_maximum_fusion), calls=%async_computation.5 | async-start | bytes 327680 | tf_op jit(solution)/shard_map/all_to_all | solution.py:286

commit v6 on v5

--- a/solution.py
+++ b/solution.py
@@ -14,7 +14,6 @@
 LARGE = pltpu.CompilerParams(vmem_limit_bytes=50 * 1024 * 1024)
 PROV = ("zl", "y")
 BIN = ("x", "zh")
-GRAM = ("zl", "month")
 
 
 def dot32(a, b, dims, precision=HIGH):
@@ -117,21 +116,49 @@
     own_ref[upper.shape[0] :] = lower
 
 
-def gram_kernel(a_ref, out_ref):
-    rank = a_ref.shape[2] // 2
-    rows = a_ref[...].reshape(-1, 2 * rank)
-    twin = dot32(rows, rows, ((0,), (0,)))
-    gram = twin[:rank, :rank] + twin[rank:, rank:]
-    groups = out_ref.shape[0]
-    for j in range(rank // groups):
-        out_ref[:, j * rank : (j + 1) * rank] = gram[j * groups : (j + 1) * groups]
-
-
-def last_product_kernel(at_ref, month_ref, tiles_ref, kept_ref, a_ref, other_ref, b_ref, out_ref, late, sems, turned):
+def iotas(n):
+    return lax.broadcasted_iota(jnp.int32, (n, n), 0), lax.broadcasted_iota(jnp.int32, (n, n), 1)
+
+
+def pack_gram(gram, month):
+    n = gram.shape[0] // 2
+    row, column = iotas(n)
+    last = gram[n:, n:]
+    triangles = jnp.where(row >= column, gram[:n, :n], last)
+    mine = jnp.where(month == 0, gram[:n, n:], triangles)
+    per = n // 4
+    folded = jnp.concatenate([mine[k * per : (k + 1) * per] for k in range(4)], axis=1)
+    diagonal = jnp.sum(jnp.where(row == column, last, 0.0), axis=0, keepdims=True)
+    return folded, jnp.concatenate([diagonal, jnp.zeros((1, 3 * n), jnp.float32)], axis=1)
+
+
+def unpack_gram(block, triangles, diagonal):
+    n = diagonal.shape[1]
+    row, column = iotas(n)
+
+    def square(flat):
+        rows = jnp.concatenate([flat[:, k * 4 * n : (k + 1) * 4 * n] for k in range(n // 4)], axis=0)
+        return jnp.concatenate([rows[:, k * n : (k + 1) * n] for k in range(4)], axis=0)
+
+    block, triangles = square(block), square(triangles)
+    turned = triangles.T
+    first = jnp.where(row >= column, triangles, turned)
+    last = jnp.where(row < column, triangles, jnp.where(row > column, turned, diagonal))
+    return jnp.concatenate(
+        [jnp.concatenate([first, block], axis=1), jnp.concatenate([block.T, last], axis=1)], axis=0
+    )
+
+
+def last_product_kernel(at_ref, month_ref, tiles_ref, kept_ref, a_ref, other_ref, b_ref, out_ref, gram_ref, late, sems, turned):
     copies = tile_copies(tiles_ref, late, sems)
     blocks, half, lanes = a_ref.shape
     rank, tile_j, tile_k = lanes // 2, tiles_ref.shape[2], tiles_ref.shape[3]
     size = half // 4
+    own, other = (ref[...].reshape(blocks * half, lanes) for ref in (a_ref, other_ref))
+    twin = dot32(own, own, ((0,), (0,))) + dot32(other, other, ((0,), (0,)))
+    folded, diagonal = pack_gram(twin[:rank, :rank] + twin[rank:, rank:], month_ref[month_ref.shape[0] - 1])
+    gram_ref[: folded.shape[0]] = folded
+    gram_ref[folded.shape[0] :] = diagonal
     total = None
     for t, copy in enumerate(copies):
         if copy is not None:
@@ -158,18 +185,13 @@
     rank = gram_b_ref.shape[0]
     width = got_ref.shape[1]
     lead = out_ref.shape[0] * rank
-    groups = rank * rank // (width - lead)
     got = got_ref[...]
-    rows = jnp.sum(got[:, :lead], axis=0, keepdims=True)
+    total = jnp.sum(got.reshape(got.shape[0] // 8, 8, width), axis=0)
+    total = (total[0:2] + total[2:4]) + (total[4:6] + total[6:8])
+    rows = total[0:1, :lead] + total[1:2, :lead]
     own = jnp.concatenate([rows[:, j * rank : (j + 1) * rank] for j in range(out_ref.shape[0])], axis=0)
-    n_zl = groups // 2
-    per = got.shape[0] // n_zl
-    folded = []
-    for zl in range(n_zl):
-        part = jnp.sum(got[zl * per : (zl + 1) * per, lead:].reshape(per // 8, 8, width - lead), axis=0)
-        folded.append((part[0:2] + part[2:4]) + (part[4:6] + part[6:8]))
-    folded = jnp.concatenate(folded, axis=0)
-    gram = jnp.concatenate([folded[:, j * rank : (j + 1) * rank] for j in range(rank // groups)], axis=0)
+    end = lead + rank * rank // 4
+    gram = unpack_gram(total[0:1, lead:end], total[1:2, lead:end], total[1:2, end : end + rank // 2])
     square_row, square_col = diagonals(gram)
     scale_row = jnp.sqrt(square_row + epsilon)
     scale_col = jnp.sqrt(square_col + epsilon)
@@ -221,7 +243,7 @@
     ]
     half = tile_i // 2
     prov_at = jnp.clip(prov_block, 0, PB_DEV - 1)
-    month_at = jnp.clip(month_block, 0, MB_DEV - 1)
+    month_at = jnp.clip(jnp.concatenate([month_block, month[None]]), 0, MB_DEV - 1)
     partial_a = pl.pallas_call(
         first_product_kernel,
         out_shape=jax.ShapeDtypeStruct((PB_DEV, half, 2 * rank), jnp.float32),
@@ -256,33 +278,25 @@
     )(own_a, inverse)
 
     half_a = lax.all_to_all(spread, BIN, 0, 0, tiled=True)
-    n_gram = lax.axis_size(GRAM)
-    half_gram = pl.pallas_call(
-        gram_kernel,
-        out_shape=jax.ShapeDtypeStruct((n_gram, rank * rank // n_gram), jnp.float32),
-        compiler_params=SMALL,
-        name="half_gram",
-    )(half_a)
-    gram_rows = lax.all_to_all(half_gram[:, None, :], GRAM, 0, 0, tiled=True)
-
     other_a = lax.ppermute(half_a, "month", [(i, n_month - 1 - i) for i in range(n_month)])
 
     n_out = n_prov * n_month
     out_rows = tile_k // n_out
-    partial_c = pl.pallas_call(
+    partial_c, packed = pl.pallas_call(
         last_product_kernel,
-        out_shape=jax.ShapeDtypeStruct((n_out, out_rows * rank), jnp.float32),
+        out_shape=(
+            jax.ShapeDtypeStruct((n_out, out_rows * rank), jnp.float32),
+            jax.ShapeDtypeStruct((rank // 8 + 1, 2 * rank), jnp.float32),
+        ),
         in_specs=[smem, smem, hbm, vmem, vmem, vmem, vmem],
-        out_specs=vmem,
+        out_specs=(vmem, vmem),
         scratch_shapes=tile_scratch + [pltpu.VMEM((tile_k, rank), jnp.float32)],
         compiler_params=LARGE,
         name="last_product",
     )(prov_at ^ (month * n_bin), month_at, tile_values, kept, half_a, other_a, slab_b)
 
-    gram_rows, partial_c = lax.optimization_barrier((gram_rows, partial_c))
-    gram_row = jnp.sum(gram_rows, axis=0, keepdims=True)
-    sent_row = jnp.broadcast_to(gram_row, (n_out,) + gram_row.shape[1:])
-    last = jnp.concatenate([partial_c[:, None, :], sent_row], axis=2)
+    sent_gram = jnp.broadcast_to(packed.reshape(1, 1, -1), (n_out, 1, packed.size))
+    last = jnp.concatenate([partial_c[:, None, :], sent_gram], axis=2)
     last = lax.all_to_all(last, PROV + ("month",), 0, 0, tiled=True)
     new_c = pl.pallas_call(
         last_kernel,

time: 117 us -> 116 us (level)
  starting transfers between devices: 41.5 us -> 37.7 us
  waiting for transfers between devices: 33.3 us -> 36.7 us
    all_to_all x1 -> x0, starting transfers between devices: 6.46 us -> none  [shards(): gram_rows = lax.all_to_all(half_gram[:, None, :], GRAM, 0, 0, tiled=True)]
    all_to_all x1, waiting for transfers between devices: 9.52 us -> 12.9 us  [shards(): last = lax.all_to_all(last, PROV + ('month',), 0, 0, tiled=True)]
    all_to_all x1, starting transfers between devices: 5.11 us -> 7.81 us  [shards(): last = lax.all_to_all(last, PROV + ('month',), 0, 0, tiled=True)]
    pallas_call x2 -> x1, Pallas kernels: 4.39 us -> 4.39 us  [shards(): pl.pallas_call(last_product_kernel, out_shape=(jax.ShapeDtypeStruct((n_ou...]
  transfers between devices with their start and end apart: 5 -> 4, of which waited for: 4 -> 4; matrix products, arithmetic and copies ran while one was open for 1% -> 1% of each run, Pallas kernels for 9% -> 5%
where the time goes in v6:
time: 116 us; the launch traced here: 115 us
  starting transfers between devices  37.7 us (33%)
  waiting for transfers between devices  36.7 us (32%)
  Pallas kernels  18 us (16%)
  blocking collectives  16.8 us (14%)
  local copies, waits for them, and re-layouts  3.6 us (3%)
  other arithmetic  1.81 us (2%)
    all_to_all x1, starting transfers between devices, shards(): got = lax.all_to_all(sent, PROV + BIN + ('month',), 0, 0, tiled=True)  22.2 us
    all_to_all x1, waiting for transfers between devices, shards(): got = lax.all_to_all(sent, PROV + BIN + ('month',), 0, 0, tiled=True)  15.5 us
    all_to_all x1, waiting for transfers between devices, shards(): last = lax.all_to_all(last, PROV + ('month',), 0, 0, tiled=True)  12.9 us
    all_to_all x1, blocking collectives, shards(): half_a = lax.all_to_all(spread, BIN, 0, 0, tiled=True)  12.5 us
    all_to_all x1, starting transfers between devices, shards(): last = lax.all_to_all(last, PROV + ('month',), 0, 0, tiled=True)  7.81 us
    all_to_all x1, waiting for transfers between devices, shards(): own_a = lax.all_to_all(pair_a, BIN, 0, 0, tiled=True)  7.12 us
    pallas_call x1, Pallas kernels, shards(): pl.pallas_call(last_kernel, out_shape=jax.ShapeDtypeStruct((out_rows, ran...  4.48 us
    pallas_call x1, Pallas kernels, shards(): pl.pallas_call(last_product_kernel, out_shape=(jax.ShapeDtypeStruct((n_ou...  4.39 us
  transfers between devices with their start and end apart: 4, of which 4 were waited for; matrix products, arithmetic and copies ran while one was open for 1% of the time, Pallas kernels for 5%

profile of v6, /device:TPU:1, one launch (start us, length us, event | category | flops | bytes accessed | tf_op | source)
XLA Modules:
  0.0 115.4 jit_solution(6704591365544515940)
XLA Ops:
  0.7 0.6 copy-done
  1.3 0.1 reshape.31
  1.4 0.7 constant_dynamic-slice_fusion.2
  2.2 0.8 broadcast_in_dim.19
  3.0 22.2 %all-to-all-start = ((bf16[512,2,128]{2,1,0:T(2,128)(2,1)}), bf16[512,2,128]{2,1,0:T(2,128)(2,1)S(1)}, u32[]{:S(2)}, u32[]{:S(2)}) async-start(bf16[512,2,128]{2,1,0:T(2,128)(2,1)} %broadcast_in_dim.19), calls=%async_computation | async-start | bytes 524288 | tf_op jit(solution)/shard_map/all_to_all | solution.py:219
  25.2 1.8 %keep_tiles.1.kept_ref = bf16[5,128,16,128]{3,2,1,0:T(8,128)(2,1)S(1)} custom-call(bf16[8,128,16,128]{3,2,1,0:T(8,128)(2,1)} %tiles_ref.5), custom_call_target="tpu_custom_call" | custom-call | tf_op jit(solution)/shard_map/keep_tiles/pallas_call | solution.py:230
  27.0 15.5 %all-to-all-done = bf16[512,2,128]{2,1,0:T(2,128)(2,1)S(1)} async-done(((bf16[512,2,128]{2,1,0:T(2,128)(2,1)}), bf16[512,2,128]{2,1,0:T(2,128)(2,1)S(1)}, u32[]{:S(2)}, u32[]{:S(2)}) %all-to-all-start) | async-done | bytes 262176 | tf_op jit(solution)/shard_map/all_to_all | solution.py:219
  42.6 0.4 fusion
  43.3 3.2 %first_product.1 = f32[16,64,128]{2,1,0:T(8,128)S(1)} custom-call(s32[8]{0:T(128)S(1)} %get-tuple-element.31.prov_ref, s32[9]{0:T(128)S(1)} %add_clamp_fusion.month_ref, bf16[8,128,16,128]{3,2,1,0:T(8,128)(2,1)} %tiles_ref.5, bf16[5,128,16,128]{3,2,1,0:T(8,128)(2,1)S(1)} %keep_tiles.1.kept_ref, bf16[128,64]{1,0:T(8,128)(2,1)S(1)} %reshape.33.c_ref, ...), custom_call_target="tpu_custom_call" | custom-call | tf_op jit(solution)/shard_map/first_product/pallas_call | solution.py:247
  46.5 4.3 %all_to_all.25 = f32[2,8,64,128]{3,2,1,0:T(8,128)S(1)} all-to-all(f32[2,8,64,128]{3,2,1,0:T(8,128)S(1)} %bitcast.22), channel_id=1, replica_groups=mesh['zl'=4,'y'=8,'month'=2,'x'=4,'zh'=2] {'month'}, dimensions={0} | all-to-all | bytes 1048576 | tf_op jit(solution)/shard_map/all_to_all | solution.py:257
  50.8 0.7 reduce_sum.9
  51.6 3.4 %all-to-all-start.2 = ((f32[8,64,128]{2,1,0:T(8,128)}), f32[8,64,128]{2,1,0:T(8,128)S(1)}, u32[]{:S(2)}, u32[]{:S(2)}) async-start(f32[8,64,128]{2,1,0:T(8,128)} %reduce_sum.9), calls=%async_computation.2 | async-start | bytes 524288 | tf_op jit(solution)/shard_map/all_to_all | solution.py:260
  55.0 3.8 %first_inverse.1 = (f32[64,64]{1,0:T(8,128)S(1)}, f32[64,64]{1,0:T(8,128)S(1)}) custom-call(bf16[256,128]{1,0:T(8,128)(2,1)S(1)} %bitcast.26, bf16[512,128]{1,0:T(8,128)(2,1)S(1)} %bitcast.24), custom_call_target="tpu_custom_call" | custom-call | flops 20000000 | bytes 200000 | tf_op jit(solution)/shard_map/first_inverse/pallas_call | solution.py:263
  58.8 7.1 %all-to-all-done.2.got_ref = f32[8,64,128]{2,1,0:T(8,128)S(1)} async-done(((f32[8,64,128]{2,1,0:T(8,128)}), f32[8,64,128]{2,1,0:T(8,128)S(1)}, u32[]{:S(2)}, u32[]{:S(2)}) %all-to-all-start.2) | async-done | bytes 262176 | tf_op jit(solution)/shard_map/all_to_all | solution.py:260
  66.0 0.3 solve_first.1
  66.3 12.5 %all_to_all.26.a_ref = f32[8,64,128]{2,1,0:T(8,128)S(1)} all-to-all(f32[8,64,128]{2,1,0:T(8,128)S(1)} %get-tuple-element.16), channel_id=1, replica_groups=mesh['zl'=4,'y'=8,'month'=2,'x'=4,'zh'=2] {'x','zh'}, dimensions={0} | all-to-all | bytes 524288 | tf_op jit(solution)/shard_map/all_to_all | solution.py:280
  78.7 4.4 %collective-permute-start = (f32[8,64,128]{2,1,0:T(8,128)S(1)}, f32[8,64,128]{2,1,0:T(8,128)S(1)}, u32[]{:S(2)}, u32[]{:S(2)}) collective-permute-start(f32[8,64,128]{2,1,0:T(8,128)S(1)} %all_to_all.26.a_ref), channel_id=1, source_target_pairs={{0,8},{8,0},{1,9},{9,1},{2,10},{10,2},{3,11},{11,3},{4,12},{12,4},... | collective-permute-start | bytes 786440 | tf_op jit(solution)/shard_map/ppermute | solution.py:281
  83.1 1.1 collective-permute-done.other_ref
  84.2 4.4 %last_product.1 = (f32[64,128]{1,0:T(8,128)S(1)}, f32[9,128]{1,0:T(8,128)S(1)}) custom-call(s32[8]{0:T(128)S(1)} %get-tuple-element.30.at_ref, s32[9]{0:T(128)S(1)} %add_clamp_fusion.month_ref, bf16[8,128,16,128]{3,2,1,0:T(8,128)(2,1)} %tiles_ref.5, bf16[5,128,16,128]{3,2,1,0:T(8,128)(2,1)S(1)} %keep_tiles.1.kept_ref, f32[8,64,128]{2,1,0:T(8,128)S(1)} %all_to_all.26.a_ref, ...), custom_call_target="tpu_custom_call" | custom-call | tf_op jit(solution)/shard_map/last_product/pallas_call | solution.py:285
  88.7 0.9 pad_maximum_fusion
  89.6 7.8 %all-to-all-start.4 = ((f32[64,1,1280]{2,1,0:T(1,128)}), f32[64,1,1280]{2,1,0:T(1,128)S(1)}, u32[]{:S(2)}, u32[]{:S(2)}) async-start(f32[64,1,1280]{2,1,0:T(1,128)} %pad_maximum_fusion), calls=%async_computation.4 | async-start | bytes 655360 | tf_op jit(solution)/shard_map/all_to_all | solution.py:300
  97.4 0.7 copy.19
  98.1 12.9 %all-to-all-done.4 = f32[64,1,1280]{2,1,0:T(1,128)S(1)} async-done(((f32[64,1,1280]{2,1,0:T(1,128)}), f32[64,1,1280]{2,1,0:T(1,128)S(1)}, u32[]{:S(2)}, u32[]{:S(2)}) %all-to-all-start.4) | async-done | bytes 327712 | tf_op jit(solution)/shard_map/all_to_all | solution.py:300
  111.0 4.5 %last_solve.1 = f32[2,64]{1,0:T(2,128)} custom-call(f32[64,1280]{1,0:T(8,128)S(1)} %bitcast.23, f32[64,64]{1,0:T(8,128)S(1)} %get-tuple-element.19.gram_b_ref), custom_call_target="tpu_custom_call" | custom-call | tf_op jit(solution)/shard_map/last_solve/pallas_call | solution.py:301
  (20 shorter events, 0.5 us)
Async XLA Ops:
  0.6 0.7 copy-start
  0.6 26.3 %copy-start.2 = (s32[8]{0:T(128)S(1)}, s32[8]{0:T(128)}, u32[]{:S(2)}) copy-start(s32[8]{0:T(128)} %param.7) | copy-start | bytes 100
  0.7 26.4 %copy-start.1 = (s32[8]{0:T(128)S(1)}, s32[8]{0:T(128)}, u32[]{:S(2)}) copy-start(s32[8]{0:T(128)} %param.6) | copy-start | bytes 100
  3.0 39.6 %all-to-all-start = ((bf16[512,2,128]{2,1,0:T(2,128)(2,1)}), bf16[512,2,128]{2,1,0:T(2,128)(2,1)S(1)}, u32[]{:S(2)}, u32[]{:S(2)}) async-start(bf16[512,2,128]{2,1,0:T(2,128)(2,1)} %broadcast_in_dim.19), calls=%async_computation | async-start | bytes 524288 | tf_op jit(solution)/shard_map/all_to_all | solution.py:219
  51.6 14.4 %all-to-all-start.2 = ((f32[8,64,128]{2,1,0:T(8,128)}), f32[8,64,128]{2,1,0:T(8,128)S(1)}, u32[]{:S(2)}, u32[]{:S(2)}) async-start(f32[8,64,128]{2,1,0:T(8,128)} %reduce_sum.9), calls=%async_computation.2 | async-start | bytes 524288 | tf_op jit(solution)/shard_map/all_to_all | solution.py:260
  78.7 5.5 %collective-permute-start = (f32[8,64,128]{2,1,0:T(8,128)S(1)}, f32[8,64,128]{2,1,0:T(8,128)S(1)}, u32[]{:S(2)}, u32[]{:S(2)}) collective-permute-start(f32[8,64,128]{2,1,0:T(8,128)S(1)} %all_to_all.26.a_ref), channel_id=1, source_target_pairs={{0,8},{8,0},{1,9},{9,1},{2,10},{10,2},{3,11},{11,3},{4,12},{12,4},... | collective-permute-start | bytes 786440 | tf_op jit(solution)/shard_map/ppermute | solution.py:281
  89.6 21.4 %all-to-all-start.4 = ((f32[64,1,1280]{2,1,0:T(1,128)}), f32[64,1,1280]{2,1,0:T(1,128)S(1)}, u32[]{:S(2)}, u32[]{:S(2)}) async-start(f32[64,1,1280]{2,1,0:T(1,128)} %pad_maximum_fusion), calls=%async_computation.4 | async-start | bytes 655360 | tf_op jit(solution)/shard_map/all_to_all | solution.py:300

commit v7 on v6

--- a/solution.py
+++ b/solution.py
@@ -35,18 +35,40 @@
     lane = lax.broadcasted_iota(jnp.int32, a.shape, 1)
     sub = lax.broadcasted_iota(jnp.int32, a.shape, 0)
     lane_row = lax.broadcasted_iota(jnp.int32, (1, n), 1)
-    for k in range(0, n, 2):
-        col0 = jnp.broadcast_to(a[:, k : k + 1], a.shape)
-        col1 = jnp.broadcast_to(a[:, k + 1 : k + 2], a.shape)
-        p, q, s = col0[k : k + 1], col1[k : k + 1], col1[k + 1 : k + 2]
-        inv = 1.0 / (p * s - q * q)
-        p, q, s = p * inv, q * inv, s * inv
-        row0, row1 = a[k : k + 1], a[k + 1 : k + 2]
-        first, second = lane_row == k, lane_row == k + 1
-        new0 = jnp.where(first, s, jnp.where(second, -q, s * row0 - q * row1))
-        new1 = jnp.where(first, -q, jnp.where(second, p, p * row1 - q * row0))
-        rest = jnp.where((lane == k) | (lane == k + 1), 0.0, a) - col0 * new0 - col1 * new1
-        a = jnp.where(sub == k, new0, jnp.where(sub == k + 1, new1, rest))
+    for k in range(0, n, 4):
+        cols = [jnp.broadcast_to(a[:, k + j : k + j + 1], a.shape) for j in range(4)]
+        (p00, p01, p02, p03), (_, p11, p12, p13), (_, _, p22, p23), (_, _, _, p33) = [
+            [cols[j][k + i : k + i + 1] for j in range(4)] for i in range(4)
+        ]
+        inv = 1.0 / (p00 * p11 - p01 * p01)
+        e00, e01, e11 = p11 * inv, -p01 * inv, p00 * inv
+        w00, w01 = e00 * p02 + e01 * p12, e00 * p03 + e01 * p13
+        w10, w11 = e01 * p02 + e11 * p12, e01 * p03 + e11 * p13
+        s00, s01 = p22 - (p02 * w00 + p12 * w10), p23 - (p02 * w01 + p12 * w11)
+        s11 = p33 - (p03 * w01 + p13 * w11)
+        inv = 1.0 / (s00 * s11 - s01 * s01)
+        q22, q23, q33 = s11 * inv, -s01 * inv, s00 * inv
+        v00, v01 = w00 * q22 + w01 * q23, w00 * q23 + w01 * q33
+        v10, v11 = w10 * q22 + w11 * q23, w10 * q23 + w11 * q33
+        q01 = e01 + v00 * w10 + v01 * w11
+        pivot = (
+            (e00 + v00 * w00 + v01 * w01, q01, -v00, -v01),
+            (q01, e11 + v10 * w10 + v11 * w11, -v10, -v11),
+            (-v00, -v10, q22, q23),
+            (-v01, -v11, q23, q33),
+        )
+        rows = [a[k + j : k + j + 1] for j in range(4)]
+        rest = jnp.where((lane >= k) & (lane < k + 4), 0.0, a)
+        fresh = []
+        for i in range(4):
+            q = pivot[i]
+            new = (q[0] * rows[0] + q[1] * rows[1]) + (q[2] * rows[2] + q[3] * rows[3])
+            for j in range(4):
+                new = jnp.where(lane_row == k + j, q[j], new)
+            fresh.append(new)
+        a = rest - ((cols[0] * fresh[0] + cols[1] * fresh[1]) + (cols[2] * fresh[2] + cols[3] * fresh[3]))
+        for i in range(4):
+            a = jnp.where(sub == k + i, fresh[i], a)
     return a * in_col * in_row
 
 
@@ -83,10 +105,12 @@
     return jnp.concatenate([upper, lower], axis=1)
 
 
-def first_product_kernel(prov_ref, month_ref, tiles_ref, kept_ref, c_ref, b_ref, out_ref, late, sems):
+def first_product_kernel(at_ref, month_ref, tiles_ref, kept_ref, c_ref, b_ref, own_ref, other_ref, late, sems):
     copies = tile_copies(tiles_ref, late, sems)
-    out_ref[...] = jnp.zeros_like(out_ref)
+    own_ref[...] = jnp.zeros_like(own_ref)
+    other_ref[...] = jnp.zeros_like(other_ref)
     c = c_ref[...]
+    blocks = own_ref.shape[0]
     zero = jnp.zeros_like(c)
     twice_c = jnp.concatenate([jnp.concatenate([c, zero], axis=1), jnp.concatenate([zero, c], axis=1)], axis=0)
     half, tile_j = tiles_ref.shape[1] // 2, tiles_ref.shape[2]
@@ -94,11 +118,15 @@
     for t, copy in enumerate(copies):
         if copy is not None:
             copy.wait()
+        at = at_ref[t]
         b = b_ref[month_ref[t]][None]
         for start in range(0, half, size):
             product = dot32(both_halves(kept_ref, late, t, start, size), twice_c, ((1,), (0,)), None)
             product = product.reshape(size, tile_j, -1) * b
-            out_ref[prov_ref[t], start : start + size] += jnp.sum(product, axis=1)
+            product = jnp.sum(product, axis=1)
+            rows = pl.ds(start, size)
+            own_ref[at % blocks, rows] += jnp.where(at < blocks, product, 0.0)
+            other_ref[at % blocks, rows] += jnp.where(at < blocks, 0.0, product)
 
 
 def solve_kernel(got_ref, inv_ref, out_ref, own_ref):
@@ -244,18 +272,20 @@
     half = tile_i // 2
     prov_at = jnp.clip(prov_block, 0, PB_DEV - 1)
     month_at = jnp.clip(jnp.concatenate([month_block, month[None]]), 0, MB_DEV - 1)
-    partial_a = pl.pallas_call(
+    swap = [(i, n_month - 1 - i) for i in range(n_month)]
+    block_at = prov_at ^ (month * n_bin)
+    sums = jax.ShapeDtypeStruct((n_bin, half, 2 * rank), jnp.float32)
+    own_half, other_half = pl.pallas_call(
         first_product_kernel,
-        out_shape=jax.ShapeDtypeStruct((PB_DEV, half, 2 * rank), jnp.float32),
+        out_shape=(sums, sums),
         in_specs=[smem, smem, hbm, vmem, vmem, vmem],
-        out_specs=vmem,
+        out_specs=(vmem, vmem),
         scratch_shapes=tile_scratch,
         compiler_params=LARGE,
         name="first_product",
-    )(prov_at, month_at, tile_values, kept, slab_c, slab_b)
-
-    pair_a = lax.all_to_all(partial_a.reshape(n_month, n_bin, half, 2 * rank), "month", 0, 0, tiled=True)
-    pair_a = jnp.sum(pair_a, axis=0)
+    )(block_at, month_at, tile_values, kept, slab_c, slab_b)
+
+    pair_a = own_half + lax.ppermute(other_half, "month", swap)
     twice_b, pairs_c, pair_a = lax.optimization_barrier((twice_b, pairs_c, pair_a))
     own_a = lax.all_to_all(pair_a, BIN, 0, 0, tiled=True)
 
@@ -278,7 +308,7 @@
     )(own_a, inverse)
 
     half_a = lax.all_to_all(spread, BIN, 0, 0, tiled=True)
-    other_a = lax.ppermute(half_a, "month", [(i, n_month - 1 - i) for i in range(n_month)])
+    other_a = lax.ppermute(half_a, "month", swap)
 
     n_out = n_prov * n_month
     out_rows = tile_k // n_out
@@ -293,7 +323,7 @@
         scratch_shapes=tile_scratch + [pltpu.VMEM((tile_k, rank), jnp.float32)],
         compiler_params=LARGE,
         name="last_product",
-    )(prov_at ^ (month * n_bin), month_at, tile_values, kept, half_a, other_a, slab_b)
+    )(block_at, month_at, tile_values, kept, half_a, other_a, slab_b)
 
     sent_gram = jnp.broadcast_to(packed.reshape(1, 1, -1), (n_out, 1, packed.size))
     last = jnp.concatenate([partial_c[:, None, :], sent_gram], axis=2)

time: 116 us -> 115 us (level)
  blocking collectives: 16.8 us -> 12.5 us
  starting transfers between devices: 37.7 us -> 40.2 us
  waiting for transfers between devices: 36.7 us -> 38.4 us
  Pallas kernels: 18 us -> 16.8 us
    all_to_all x1 -> x0, blocking collectives: 4.33 us -> none  [shards(): lax.all_to_all(partial_a.reshape(n_month, n_bin, half, 2 * rank), 'month'...]
    ppermute x1 -> x2, starting transfers between devices: 4.35 us -> 6.82 us  [the longest x1 4.3 us: shards(): other_a = lax.ppermute(half_a, 'month', swap)]
  transfers between devices with their start and end apart: 4 -> 5, of which waited for: 4 -> 5; matrix products, arithmetic and copies ran while one was open for 1% -> 1% of each run, Pallas kernels for 5% -> 4%
where the time goes in v7:
time: 115 us; the launch traced here: 114 us
  starting transfers between devices  40.2 us (35%)
  waiting for transfers between devices  38.4 us (33%)
  Pallas kernels  16.8 us (15%)
  blocking collectives  12.5 us (11%)
  local copies, waits for them, and re-layouts  3.59 us (3%)
  other arithmetic  1.81 us (2%)
    all_to_all x1, starting transfers between devices, shards(): got = lax.all_to_all(sent, PROV + BIN + ('month',), 0, 0, tiled=True)  22.2 us
    all_to_all x1, waiting for transfers between devices, shards(): got = lax.all_to_all(sent, PROV + BIN + ('month',), 0, 0, tiled=True)  15.5 us
    all_to_all x1, waiting for transfers between devices, shards(): last = lax.all_to_all(last, PROV + ('month',), 0, 0, tiled=True)  12.9 us
    all_to_all x1, blocking collectives, shards(): half_a = lax.all_to_all(spread, BIN, 0, 0, tiled=True)  12.5 us
    all_to_all x1, starting transfers between devices, shards(): last = lax.all_to_all(last, PROV + ('month',), 0, 0, tiled=True)  7.81 us
    all_to_all x1, waiting for transfers between devices, shards(): own_a = lax.all_to_all(pair_a, BIN, 0, 0, tiled=True)  7.77 us
    pallas_call x1, Pallas kernels, shards(): pl.pallas_call(last_product_kernel, out_shape=(jax.ShapeDtypeStruct((n_ou...  4.37 us
    ppermute x1, starting transfers between devices, shards(): other_a = lax.ppermute(half_a, 'month', swap)  4.3 us
  transfers between devices with their start and end apart: 5, of which 5 were waited for; matrix products, arithmetic and copies ran while one was open for 1% of the time, Pallas kernels for 4%

profile of v7, /device:TPU:1, one launch (start us, length us, event | category | flops | bytes accessed | tf_op | source)
XLA Modules:
  0.0 114.1 jit_solution(16480666981011594780)
XLA Ops:
  0.7 0.6 copy-done
  1.4 0.7 constant_dynamic-slice_fusion.2
  2.2 0.8 broadcast_in_dim.19
  3.0 22.2 %all-to-all-start = ((bf16[512,2,128]{2,1,0:T(2,128)(2,1)}), bf16[512,2,128]{2,1,0:T(2,128)(2,1)S(1)}, u32[]{:S(2)}, u32[]{:S(2)}) async-start(bf16[512,2,128]{2,1,0:T(2,128)(2,1)} %broadcast_in_dim.19), calls=%async_computation | async-start | bytes 524288 | tf_op jit(solution)/shard_map/all_to_all | solution.py:247
  25.2 1.8 %keep_tiles.1.kept_ref = bf16[5,128,16,128]{3,2,1,0:T(8,128)(2,1)S(1)} custom-call(bf16[8,128,16,128]{3,2,1,0:T(8,128)(2,1)} %tiles_ref.5), custom_call_target="tpu_custom_call" | custom-call | tf_op jit(solution)/shard_map/keep_tiles/pallas_call | solution.py:258
  27.0 15.5 %all-to-all-done = bf16[512,2,128]{2,1,0:T(2,128)(2,1)S(1)} async-done(((bf16[512,2,128]{2,1,0:T(2,128)(2,1)}), bf16[512,2,128]{2,1,0:T(2,128)(2,1)S(1)}, u32[]{:S(2)}, u32[]{:S(2)}) %all-to-all-start) | async-done | bytes 262176 | tf_op jit(solution)/shard_map/all_to_all | solution.py:247
  42.5 0.4 fusion
  43.2 3.3 %first_product.1 = (f32[8,64,128]{2,1,0:T(8,128)S(1)}, f32[8,64,128]{2,1,0:T(8,128)S(1)}) custom-call(s32[8]{0:T(128)S(1)} %clamp_xor_fusion.at_ref, s32[9]{0:T(128)S(1)} %add_clamp_fusion.month_ref, bf16[8,128,16,128]{3,2,1,0:T(8,128)(2,1)} %tiles_ref.5, bf16[5,128,16,128]{3,2,1,0:T(8,128)(2,1)S(1)} %keep_tiles.1.kept_ref, ...), custom_call_target="tpu_custom_call" | custom-call | tf_op jit(solution)/shard_map/first_product/pallas_call | solution.py:278
  46.5 2.5 %collective-permute-start = (f32[8,64,128]{2,1,0:T(8,128)S(1)}, f32[8,64,128]{2,1,0:T(8,128)S(1)}, u32[]{:S(2)}, u32[]{:S(2)}) collective-permute-start(f32[8,64,128]{2,1,0:T(8,128)S(1)} %get-tuple-element.14), channel_id=1, source_target_pairs={{0,8},{8,0},{1,9},{9,1},{2,10},{10,2},{3,11},{11,3},{4,12},{12,4},... | collective-permute-start | bytes 786440 | tf_op jit(solution)/shard_map/ppermute | solution.py:288
  49.0 1.1 collective-permute-done
  50.1 0.7 add.24
  50.9 3.4 %all-to-all-start.1 = ((f32[8,64,128]{2,1,0:T(8,128)}), f32[8,64,128]{2,1,0:T(8,128)S(1)}, u32[]{:S(2)}, u32[]{:S(2)}) async-start(f32[8,64,128]{2,1,0:T(8,128)} %add.24), calls=%async_computation.1 | async-start | bytes 524288 | tf_op jit(solution)/shard_map/all_to_all | solution.py:290
  54.3 3.2 %first_inverse.1 = (f32[64,64]{1,0:T(8,128)S(1)}, f32[64,64]{1,0:T(8,128)S(1)}) custom-call(bf16[256,128]{1,0:T(8,128)(2,1)S(1)} %bitcast.24, bf16[512,128]{1,0:T(8,128)(2,1)S(1)} %bitcast.22), custom_call_target="tpu_custom_call" | custom-call | flops 20000000 | bytes 200000 | tf_op jit(solution)/shard_map/first_inverse/pallas_call | solution.py:293
  57.5 7.8 %all-to-all-done.1.got_ref = f32[8,64,128]{2,1,0:T(8,128)S(1)} async-done(((f32[8,64,128]{2,1,0:T(8,128)}), f32[8,64,128]{2,1,0:T(8,128)S(1)}, u32[]{:S(2)}, u32[]{:S(2)}) %all-to-all-start.1) | async-done | bytes 262176 | tf_op jit(solution)/shard_map/all_to_all | solution.py:290
  65.3 0.3 solve_first.1
  65.6 12.5 %all_to_all.20.a_ref = f32[8,64,128]{2,1,0:T(8,128)S(1)} all-to-all(f32[8,64,128]{2,1,0:T(8,128)S(1)} %get-tuple-element.20), channel_id=1, replica_groups=mesh['zl'=4,'y'=8,'month'=2,'x'=4,'zh'=2] {'x','zh'}, dimensions={0} | all-to-all | bytes 524288 | tf_op jit(solution)/shard_map/all_to_all | solution.py:310
  78.1 4.3 %collective-permute-start.1 = (f32[8,64,128]{2,1,0:T(8,128)S(1)}, f32[8,64,128]{2,1,0:T(8,128)S(1)}, u32[]{:S(2)}, u32[]{:S(2)}) collective-permute-start(f32[8,64,128]{2,1,0:T(8,128)S(1)} %all_to_all.20.a_ref), channel_id=1, source_target_pairs={{0,8},{8,0},{1,9},{9,1},{2,10},{10,2},{3,11},{11,3},{4,12},{12,4},... | collective-permute-start | bytes 786440 | tf_op jit(solution)/shard_map/ppermute | solution.py:311
  82.4 1.1 collective-permute-done.1.other_ref
  83.5 4.4 %last_product.1 = (f32[64,128]{1,0:T(8,128)S(1)}, f32[9,128]{1,0:T(8,128)S(1)}) custom-call(s32[8]{0:T(128)S(1)} %clamp_xor_fusion.at_ref, s32[9]{0:T(128)S(1)} %add_clamp_fusion.month_ref, bf16[8,128,16,128]{3,2,1,0:T(8,128)(2,1)} %tiles_ref.5, bf16[5,128,16,128]{3,2,1,0:T(8,128)(2,1)S(1)} %keep_tiles.1.kept_ref, f32[8,64,128]{2,1,0:T(8,128)S(1)} %all_to_all.20.a_ref, ...), custom_call_target="tpu_custom_call" | custom-call | tf_op jit(solution)/shard_map/last_product/pallas_call | solution.py:315
  87.9 0.9 pad_maximum_fusion
  88.8 7.8 %all-to-all-start.3 = ((f32[64,1,1280]{2,1,0:T(1,128)}), f32[64,1,1280]{2,1,0:T(1,128)S(1)}, u32[]{:S(2)}, u32[]{:S(2)}) async-start(f32[64,1,1280]{2,1,0:T(1,128)} %pad_maximum_fusion), calls=%async_computation.3 | async-start | bytes 655360 | tf_op jit(solution)/shard_map/all_to_all | solution.py:330
  96.6 0.7 copy.19
  97.3 12.9 %all-to-all-done.3 = f32[64,1,1280]{2,1,0:T(1,128)S(1)} async-done(((f32[64,1,1280]{2,1,0:T(1,128)}), f32[64,1,1280]{2,1,0:T(1,128)S(1)}, u32[]{:S(2)}, u32[]{:S(2)}) %all-to-all-start.3) | async-done | bytes 327712 | tf_op jit(solution)/shard_map/all_to_all | solution.py:330
  110.2 3.9 %last_solve.1 = f32[2,64]{1,0:T(2,128)} custom-call(f32[64,1280]{1,0:T(8,128)S(1)} %bitcast.21, f32[64,64]{1,0:T(8,128)S(1)} %get-tuple-element.23.gram_b_ref), custom_call_target="tpu_custom_call" | custom-call | tf_op jit(solution)/shard_map/last_solve/pallas_call | solution.py:331
  (21 shorter events, 0.5 us)
Async XLA Ops:
  0.6 0.7 copy-start
  0.6 26.3 %copy-start.1 = (s32[8]{0:T(128)S(1)}, s32[8]{0:T(128)}, u32[]{:S(2)}) copy-start(s32[8]{0:T(128)} %param.7) | copy-start | bytes 100
  0.7 26.4 %copy-start.2 = (s32[8]{0:T(128)S(1)}, s32[8]{0:T(128)}, u32[]{:S(2)}) copy-start(s32[8]{0:T(128)} %param.6) | copy-start | bytes 100
  3.0 39.5 %all-to-all-start = ((bf16[512,2,128]{2,1,0:T(2,128)(2,1)}), bf16[512,2,128]{2,1,0:T(2,128)(2,1)S(1)}, u32[]{:S(2)}, u32[]{:S(2)}) async-start(bf16[512,2,128]{2,1,0:T(2,128)(2,1)} %broadcast_in_dim.19), calls=%async_computation | async-start | bytes 524288 | tf_op jit(solution)/shard_map/all_to_all | solution.py:247
  46.5 3.7 %collective-permute-start = (f32[8,64,128]{2,1,0:T(8,128)S(1)}, f32[8,64,128]{2,1,0:T(8,128)S(1)}, u32[]{:S(2)}, u32[]{:S(2)}) collective-permute-start(f32[8,64,128]{2,1,0:T(8,128)S(1)} %get-tuple-element.14), channel_id=1, source_target_pairs={{0,8},{8,0},{1,9},{9,1},{2,10},{10,2},{3,11},{11,3},{4,12},{12,4},... | collective-permute-start | bytes 786440 | tf_op jit(solution)/shard_map/ppermute | solution.py:288
  50.9 14.4 %all-to-all-start.1 = ((f32[8,64,128]{2,1,0:T(8,128)}), f32[8,64,128]{2,1,0:T(8,128)S(1)}, u32[]{:S(2)}, u32[]{:S(2)}) async-start(f32[8,64,128]{2,1,0:T(8,128)} %add.24), calls=%async_computation.1 | async-start | bytes 524288 | tf_op jit(solution)/shard_map/all_to_all | solution.py:290
  78.1 5.4 %collective-permute-start.1 = (f32[8,64,128]{2,1,0:T(8,128)S(1)}, f32[8,64,128]{2,1,0:T(8,128)S(1)}, u32[]{:S(2)}, u32[]{:S(2)}) collective-permute-start(f32[8,64,128]{2,1,0:T(8,128)S(1)} %all_to_all.20.a_ref), channel_id=1, source_target_pairs={{0,8},{8,0},{1,9},{9,1},{2,10},{10,2},{3,11},{11,3},{4,12},{12,4},... | collective-permute-start | bytes 786440 | tf_op jit(solution)/shard_map/ppermute | solution.py:311
  88.8 21.4 %all-to-all-start.3 = ((f32[64,1,1280]{2,1,0:T(1,128)}), f32[64,1,1280]{2,1,0:T(1,128)S(1)}, u32[]{:S(2)}, u32[]{:S(2)}) async-start(f32[64,1,1280]{2,1,0:T(1,128)} %pad_maximum_fusion), calls=%async_computation.3 | async-start | bytes 655360 | tf_op jit(solution)/shard_map/all_to_all | solution.py:330

commit v8 on v7

--- a/solution.py
+++ b/solution.py
@@ -83,6 +83,30 @@
     inv_ref[...] = spd_inverse(gram_b * gram_c)
 
 
+def spread_kernel(c_ref, b_ref, out_ref, chunk, sems):
+    month = lax.axis_index("month")
+    bin_at = lax.axis_index("x") * lax.axis_size("zh") + lax.axis_index("zh")
+    c, b = c_ref[...].astype(jnp.float32), b_ref[...].astype(jnp.float32)
+    rows = lax.broadcasted_iota(jnp.int32, c.shape, 0)
+
+    def row(values, at):
+        return jnp.sum(jnp.where(rows == at, values, 0.0), axis=0, keepdims=True)
+
+    c_rows = c.shape[0] // lax.axis_size("month")
+    b_row = row(b, bin_at // (lax.axis_size(BIN) // b.shape[0]))
+    first = jnp.concatenate([row(c, month * c_rows + k) for k in range(c_rows)], axis=1)
+    both = jnp.concatenate([first] + [jnp.concatenate([b_row] * c_rows, axis=1)], axis=0)
+    chunk[...] = jnp.broadcast_to(both.astype(chunk.dtype)[None], chunk.shape)
+    size = chunk.shape[0]
+    copies = [
+        pltpu.make_async_copy(chunk, out_ref.at[pl.ds(k * size, size)], sems.at[k]) for k in range(out_ref.shape[0] // size)
+    ]
+    for copy in copies:
+        copy.start()
+    for copy in copies:
+        copy.wait()
+
+
 def keep_kernel(tiles_ref, kept_ref, sem):
     copy = pltpu.make_async_copy(tiles_ref.at[pl.ds(0, kept_ref.shape[0])], kept_ref, sem)
     copy.start()
@@ -239,11 +263,19 @@
     n_all = n_prov * n_month * n_bin
     c_rows = factor_c.shape[0] // n_month
     b_rep = n_bin // factor_b.shape[0]
-    own_c_rows = lax.dynamic_slice_in_dim(factor_c, month * c_rows, c_rows, 0).reshape(1, c_rows * rank)
-    own_b_row = lax.dynamic_slice_in_dim(factor_b, bin_at // b_rep, 1, 0)
-    own_b_row = jnp.concatenate([own_b_row] * c_rows, axis=1)
-    chunk = jnp.concatenate([own_c_rows, own_b_row], axis=0)
-    sent = jnp.broadcast_to(chunk[None], (n_all,) + chunk.shape)
+    parts = 8
+    sent = pl.pallas_call(
+        spread_kernel,
+        out_shape=jax.ShapeDtypeStruct((n_all, 2, c_rows * rank), factor_c.dtype),
+        in_specs=[pl.BlockSpec(memory_space=pltpu.VMEM)] * 2,
+        out_specs=pl.BlockSpec(memory_space=pl.ANY),
+        scratch_shapes=[
+            pltpu.VMEM((n_all // parts, 2, c_rows * rank), factor_c.dtype),
+            pltpu.SemaphoreType.DMA((parts,)),
+        ],
+        compiler_params=pltpu.CompilerParams(vmem_limit_bytes=60 * 1024 * 1024),
+        name="spread_rows",
+    )(factor_c, factor_b)
     got = lax.all_to_all(sent, PROV + BIN + ("month",), 0, 0, tiled=True)
     pairs_c = got[:, 0, :]
     twice_b = got[:, 1, :].reshape(n_prov, factor_b.shape[0], b_rep, n_month, c_rows * rank)[:, :, 0]

time: 115 us -> 114 us (level)
  local copies, waits for them, and re-layouts: 3.59 us -> 1.34 us
  Pallas kernels: 16.8 us -> 18.4 us
    pallas_call x0 -> x1, Pallas kernels: none -> 1.58 us  [shards(): pl.pallas_call(spread_kernel, out_shape=jax.ShapeDtypeStruct((n_all, 2, c...]
where the time goes in v8:
time: 114 us; the launch traced here: 113 us
  starting transfers between devices  40.2 us (35%)
  waiting for transfers between devices  38.4 us (34%)
  Pallas kernels  18.4 us (16%)
  blocking collectives  12.5 us (11%)
  other arithmetic  1.73 us (2%)
  local copies, waits for them, and re-layouts  1.34 us (1%)
    all_to_all x1, starting transfers between devices, shards(): got = lax.all_to_all(sent, PROV + BIN + ('month',), 0, 0, tiled=True)  22.2 us
    all_to_all x1, waiting for transfers between devices, shards(): got = lax.all_to_all(sent, PROV + BIN + ('month',), 0, 0, tiled=True)  15.5 us
    all_to_all x1, waiting for transfers between devices, shards(): last = lax.all_to_all(last, PROV + ('month',), 0, 0, tiled=True)  12.9 us
    all_to_all x1, blocking collectives, shards(): half_a = lax.all_to_all(spread, BIN, 0, 0, tiled=True)  12.5 us
    all_to_all x1, starting transfers between devices, shards(): last = lax.all_to_all(last, PROV + ('month',), 0, 0, tiled=True)  7.8 us
    all_to_all x1, waiting for transfers between devices, shards(): own_a = lax.all_to_all(pair_a, BIN, 0, 0, tiled=True)  7.71 us
    ppermute x1, starting transfers between devices, shards(): other_a = lax.ppermute(half_a, 'month', swap)  4.36 us
    pallas_call x1, Pallas kernels, shards(): pl.pallas_call(last_product_kernel, out_shape=(jax.ShapeDtypeStruct((n_ou...  4.35 us
  transfers between devices with their start and end apart: 5, of which 5 were waited for; matrix products, arithmetic and copies ran while one was open for 1% of the time, Pallas kernels for 4%

profile of v8, /device:TPU:1, one launch (start us, length us, event | category | flops | bytes accessed | tf_op | source)
XLA Modules:
  0.0 113.3 jit_solution(17496126806871545968)
XLA Ops:
  0.7 1.6 %spread_rows.1 = bf16[512,2,128]{2,1,0:T(2,128)(2,1)} custom-call(bf16[4,64]{1,0:T(4,128)(2,1)} %c_ref.1, bf16[4,64]{1,0:T(4,128)(2,1)} %b_ref.1), custom_call_target="tpu_custom_call" | custom-call | tf_op jit(solution)/shard_map/spread_rows/pallas_call | solution.py:267
  2.2 22.2 %all-to-all-start = ((bf16[512,2,128]{2,1,0:T(2,128)(2,1)}), bf16[512,2,128]{2,1,0:T(2,128)(2,1)S(1)}, u32[]{:S(2)}, u32[]{:S(2)}) async-start(bf16[512,2,128]{2,1,0:T(2,128)(2,1)} %spread_rows.1), calls=%async_computation | async-start | bytes 524288 | tf_op jit(solution)/shard_map/all_to_all | solution.py:279
  24.4 1.8 %keep_tiles.1.kept_ref = bf16[5,128,16,128]{3,2,1,0:T(8,128)(2,1)S(1)} custom-call(bf16[8,128,16,128]{3,2,1,0:T(8,128)(2,1)} %tiles_ref.5), custom_call_target="tpu_custom_call" | custom-call | tf_op jit(solution)/shard_map/keep_tiles/pallas_call | solution.py:290
  26.2 0.1 add_clamp_fusion.month_ref
  26.3 15.5 %all-to-all-done = bf16[512,2,128]{2,1,0:T(2,128)(2,1)S(1)} async-done(((bf16[512,2,128]{2,1,0:T(2,128)(2,1)}), bf16[512,2,128]{2,1,0:T(2,128)(2,1)S(1)}, u32[]{:S(2)}, u32[]{:S(2)}) %all-to-all-start) | async-done | bytes 262176 | tf_op jit(solution)/shard_map/all_to_all | solution.py:279
  41.8 0.4 fusion
  42.4 0.1 reshape.25.c_ref
  42.5 3.3 %first_product.1 = (f32[8,64,128]{2,1,0:T(8,128)S(1)}, f32[8,64,128]{2,1,0:T(8,128)S(1)}) custom-call(s32[8]{0:T(128)S(1)} %clamp_xor_fusion.at_ref, s32[9]{0:T(128)S(1)} %add_clamp_fusion.month_ref, bf16[8,128,16,128]{3,2,1,0:T(8,128)(2,1)} %tiles_ref.5, bf16[5,128,16,128]{3,2,1,0:T(8,128)(2,1)S(1)} %keep_tiles.1.kept_ref, ...), custom_call_target="tpu_custom_call" | custom-call | tf_op jit(solution)/shard_map/first_product/pallas_call | solution.py:310
  45.7 2.5 %collective-permute-start = (f32[8,64,128]{2,1,0:T(8,128)S(1)}, f32[8,64,128]{2,1,0:T(8,128)S(1)}, u32[]{:S(2)}, u32[]{:S(2)}) collective-permute-start(f32[8,64,128]{2,1,0:T(8,128)S(1)} %get-tuple-element.14), channel_id=1, source_target_pairs={{0,8},{8,0},{1,9},{9,1},{2,10},{10,2},{3,11},{11,3},{4,12},{12,4},... | collective-permute-start | bytes 786440 | tf_op jit(solution)/shard_map/ppermute | solution.py:320
  48.2 1.1 collective-permute-done
  49.4 0.7 add.15
  50.1 3.4 %all-to-all-start.1 = ((f32[8,64,128]{2,1,0:T(8,128)}), f32[8,64,128]{2,1,0:T(8,128)S(1)}, u32[]{:S(2)}, u32[]{:S(2)}) async-start(f32[8,64,128]{2,1,0:T(8,128)} %add.15), calls=%async_computation.1 | async-start | bytes 524288 | tf_op jit(solution)/shard_map/all_to_all | solution.py:322
  53.5 3.2 %first_inverse.1 = (f32[64,64]{1,0:T(8,128)S(1)}, f32[64,64]{1,0:T(8,128)S(1)}) custom-call(bf16[256,128]{1,0:T(8,128)(2,1)S(1)} %bitcast.24, bf16[512,128]{1,0:T(8,128)(2,1)S(1)} %bitcast.22), custom_call_target="tpu_custom_call" | custom-call | flops 20000000 | bytes 200000 | tf_op jit(solution)/shard_map/first_inverse/pallas_call | solution.py:325
  56.8 7.7 %all-to-all-done.1.got_ref = f32[8,64,128]{2,1,0:T(8,128)S(1)} async-done(((f32[8,64,128]{2,1,0:T(8,128)}), f32[8,64,128]{2,1,0:T(8,128)S(1)}, u32[]{:S(2)}, u32[]{:S(2)}) %all-to-all-start.1) | async-done | bytes 262176 | tf_op jit(solution)/shard_map/all_to_all | solution.py:322
  64.5 0.3 solve_first.1
  64.8 12.5 %all_to_all.20.a_ref = f32[8,64,128]{2,1,0:T(8,128)S(1)} all-to-all(f32[8,64,128]{2,1,0:T(8,128)S(1)} %get-tuple-element.20), channel_id=1, replica_groups=mesh['zl'=4,'y'=8,'month'=2,'x'=4,'zh'=2] {'x','zh'}, dimensions={0} | all-to-all | bytes 524288 | tf_op jit(solution)/shard_map/all_to_all | solution.py:342
  77.2 4.4 %collective-permute-start.1 = (f32[8,64,128]{2,1,0:T(8,128)S(1)}, f32[8,64,128]{2,1,0:T(8,128)S(1)}, u32[]{:S(2)}, u32[]{:S(2)}) collective-permute-start(f32[8,64,128]{2,1,0:T(8,128)S(1)} %all_to_all.20.a_ref), channel_id=1, source_target_pairs={{0,8},{8,0},{1,9},{9,1},{2,10},{10,2},{3,11},{11,3},{4,12},{12,4},... | collective-permute-start | bytes 786440 | tf_op jit(solution)/shard_map/ppermute | solution.py:343
  81.6 1.1 %collective-permute-done.1.other_ref = f32[8,64,128]{2,1,0:T(8,128)S(1)} collective-permute-done((f32[8,64,128]{2,1,0:T(8,128)S(1)}, f32[8,64,128]{2,1,0:T(8,128)S(1)}, u32[]{:S(2)}, u32[]{:S(2)}) %collective-permute-start.1) | collective-permute-done | bytes 262176 | tf_op jit(solution)/shard_map/ppermute | solution.py:343
  82.8 4.4 %last_product.1 = (f32[64,128]{1,0:T(8,128)S(1)}, f32[9,128]{1,0:T(8,128)S(1)}) custom-call(s32[8]{0:T(128)S(1)} %clamp_xor_fusion.at_ref, s32[9]{0:T(128)S(1)} %add_clamp_fusion.month_ref, bf16[8,128,16,128]{3,2,1,0:T(8,128)(2,1)} %tiles_ref.5, bf16[5,128,16,128]{3,2,1,0:T(8,128)(2,1)S(1)} %keep_tiles.1.kept_ref, f32[8,64,128]{2,1,0:T(8,128)S(1)} %all_to_all.20.a_ref, ...), custom_call_target="tpu_custom_call" | custom-call | tf_op jit(solution)/shard_map/last_product/pallas_call | solution.py:347
  87.1 0.9 pad_maximum_fusion
  88.0 7.8 %all-to-all-start.3 = ((f32[64,1,1280]{2,1,0:T(1,128)}), f32[64,1,1280]{2,1,0:T(1,128)S(1)}, u32[]{:S(2)}, u32[]{:S(2)}) async-start(f32[64,1,1280]{2,1,0:T(1,128)} %pad_maximum_fusion), calls=%async_computation.3 | async-start | bytes 655360 | tf_op jit(solution)/shard_map/all_to_all | solution.py:362
  95.8 0.7 copy.21
  96.5 12.9 %all-to-all-done.3 = f32[64,1,1280]{2,1,0:T(1,128)S(1)} async-done(((f32[64,1,1280]{2,1,0:T(1,128)}), f32[64,1,1280]{2,1,0:T(1,128)S(1)}, u32[]{:S(2)}, u32[]{:S(2)}) %all-to-all-start.3) | async-done | bytes 327712 | tf_op jit(solution)/shard_map/all_to_all | solution.py:362
  109.4 3.9 %last_solve.1 = f32[2,64]{1,0:T(2,128)} custom-call(f32[64,1280]{1,0:T(8,128)S(1)} %bitcast.21, f32[64,64]{1,0:T(8,128)S(1)} %get-tuple-element.23.gram_b_ref), custom_call_target="tpu_custom_call" | custom-call | tf_op jit(solution)/shard_map/last_solve/pallas_call | solution.py:363
  (15 shorter events, 0.2 us)
Async XLA Ops:
  0.6 25.6 %copy-start = (s32[8]{0:T(128)S(1)}, s32[8]{0:T(128)}, u32[]{:S(2)}) copy-start(s32[8]{0:T(128)} %param.7) | copy-start | bytes 100
  0.6 25.6 %copy-start.1 = (s32[8]{0:T(128)S(1)}, s32[8]{0:T(128)}, u32[]{:S(2)}) copy-start(s32[8]{0:T(128)} %param.6) | copy-start | bytes 100
  2.2 39.6 %all-to-all-start = ((bf16[512,2,128]{2,1,0:T(2,128)(2,1)}), bf16[512,2,128]{2,1,0:T(2,128)(2,1)S(1)}, u32[]{:S(2)}, u32[]{:S(2)}) async-start(bf16[512,2,128]{2,1,0:T(2,128)(2,1)} %spread_rows.1), calls=%async_computation | async-start | bytes 524288 | tf_op jit(solution)/shard_map/all_to_all | solution.py:279
  45.7 3.6 %collective-permute-start = (f32[8,64,128]{2,1,0:T(8,128)S(1)}, f32[8,64,128]{2,1,0:T(8,128)S(1)}, u32[]{:S(2)}, u32[]{:S(2)}) collective-permute-start(f32[8,64,128]{2,1,0:T(8,128)S(1)} %get-tuple-element.14), channel_id=1, source_target_pairs={{0,8},{8,0},{1,9},{9,1},{2,10},{10,2},{3,11},{11,3},{4,12},{12,4},... | collective-permute-start | bytes 786440 | tf_op jit(solution)/shard_map/ppermute | solution.py:320
  50.1 14.4 %all-to-all-start.1 = ((f32[8,64,128]{2,1,0:T(8,128)}), f32[8,64,128]{2,1,0:T(8,128)S(1)}, u32[]{:S(2)}, u32[]{:S(2)}) async-start(f32[8,64,128]{2,1,0:T(8,128)} %add.15), calls=%async_computation.1 | async-start | bytes 524288 | tf_op jit(solution)/shard_map/all_to_all | solution.py:322
  77.2 5.5 %collective-permute-start.1 = (f32[8,64,128]{2,1,0:T(8,128)S(1)}, f32[8,64,128]{2,1,0:T(8,128)S(1)}, u32[]{:S(2)}, u32[]{:S(2)}) collective-permute-start(f32[8,64,128]{2,1,0:T(8,128)S(1)} %all_to_all.20.a_ref), channel_id=1, source_target_pairs={{0,8},{8,0},{1,9},{9,1},{2,10},{10,2},{3,11},{11,3},{4,12},{12,4},... | collective-permute-start | bytes 786440 | tf_op jit(solution)/shard_map/ppermute | solution.py:343
  88.0 21.4 %all-to-all-start.3 = ((f32[64,1,1280]{2,1,0:T(1,128)}), f32[64,1,1280]{2,1,0:T(1,128)S(1)}, u32[]{:S(2)}, u32[]{:S(2)}) async-start(f32[64,1,1280]{2,1,0:T(1,128)} %pad_maximum_fusion), calls=%async_computation.3 | async-start | bytes 655360 | tf_op jit(solution)/shard_map/all_to_all | solution.py:362

commit v9 on v8

--- a/solution.py
+++ b/solution.py
@@ -233,17 +233,27 @@
         out_ref[:, row * rank : (row + 1) * rank] = turned[pl.ds(row, tile_k // out_rows, stride=out_rows), :]
 
 
-def last_kernel(got_ref, gram_b_ref, out_ref):
+def fold_kernel(got_ref, keep_ref, send_ref):
+    lead = (got_ref.shape[1] - keep_ref.shape[1]) // (lax.axis_size("month") - 1)
+    got = got_ref[...]
+    total = jnp.sum(got.reshape(got.shape[0] // 8, 8, got.shape[1]), axis=0)
+    total = jnp.sum(total, axis=0, keepdims=True)
+    zero, one, half = total[:, :lead], total[:, lead : 2 * lead], total[:, 2 * lead :]
+    first = lax.axis_index("month") == 0
+    keep_ref[...] = jnp.concatenate([jnp.where(first, zero, one), half], axis=1)
+    send_ref[...] = jnp.concatenate([jnp.where(first, one, zero), half], axis=1)
+
+
+def last_kernel(keep_ref, swapped_ref, gram_b_ref, out_ref):
     rank = gram_b_ref.shape[0]
-    width = got_ref.shape[1]
     lead = out_ref.shape[0] * rank
-    got = got_ref[...]
-    total = jnp.sum(got.reshape(got.shape[0] // 8, 8, width), axis=0)
-    total = (total[0:2] + total[2:4]) + (total[4:6] + total[6:8])
-    rows = total[0:1, :lead] + total[1:2, :lead]
+    keep, swapped = keep_ref[...], swapped_ref[...]
+    rows = keep[:, :lead] + swapped[:, :lead]
     own = jnp.concatenate([rows[:, j * rank : (j + 1) * rank] for j in range(out_ref.shape[0])], axis=0)
     end = lead + rank * rank // 4
-    gram = unpack_gram(total[0:1, lead:end], total[1:2, lead:end], total[1:2, end : end + rank // 2])
+    first = lax.axis_index("month") == 0
+    block, triangles = jnp.where(first, keep, swapped), jnp.where(first, swapped, keep)
+    gram = unpack_gram(block[:, lead:end], triangles[:, lead:end], triangles[:, end : end + rank // 2])
     square_row, square_col = diagonals(gram)
     scale_row = jnp.sqrt(square_row + epsilon)
     scale_col = jnp.sqrt(square_col + epsilon)
@@ -357,15 +367,19 @@
         name="last_product",
     )(block_at, month_at, tile_values, kept, half_a, other_a, slab_b)
 
-    sent_gram = jnp.broadcast_to(packed.reshape(1, 1, -1), (n_out, 1, packed.size))
-    last = jnp.concatenate([partial_c[:, None, :], sent_gram], axis=2)
-    last = lax.all_to_all(last, PROV + ("month",), 0, 0, tiled=True)
+    sent_gram = jnp.broadcast_to(packed.reshape(1, 1, -1), (n_prov, 1, packed.size))
+    last = jnp.concatenate([partial_c.reshape(n_prov, 1, -1), sent_gram], axis=2)
+    last = lax.all_to_all(last, PROV, 0, 0, tiled=True)
+    summed = jax.ShapeDtypeStruct((1, out_rows * rank + packed.size), jnp.float32)
+    keep, send = pl.pallas_call(
+        fold_kernel, out_shape=(summed, summed), compiler_params=SMALL, name="fold_sources"
+    )(last.reshape(n_prov, -1))
     new_c = pl.pallas_call(
         last_kernel,
         out_shape=jax.ShapeDtypeStruct((out_rows, rank), jnp.float32),
         compiler_params=SMALL,
         name="last_solve",
-    )(last.reshape(n_out, -1), gram_b)
+    )(keep, lax.ppermute(send, "month", swap), gram_b)
     return (factor_a, new_c)
 
 

time: 114 us -> 113 us (level)
  blocking collectives: 12.5 us -> 28.7 us
  waiting for transfers between devices: 38.4 us -> 25.6 us
  starting transfers between devices: 40.2 us -> 37 us
    all_to_all x0 -> x1, blocking collectives: none -> 16.3 us  [shards(): last = lax.all_to_all(last, PROV, 0, 0, tiled=True)]
    all_to_all x1 -> x0, waiting for transfers between devices: 12.9 us -> none  [shards(): last = lax.all_to_all(last, PROV + ('month',), 0, 0, tiled=True)]
    all_to_all x1 -> x0, starting transfers between devices: 7.8 us -> none  [shards(): last = lax.all_to_all(last, PROV + ('month',), 0, 0, tiled=True)]
    ppermute x0 -> x1, starting transfers between devices: none -> 4.63 us  [shards(): lax.ppermute(send, 'month', swap)]
where the time goes in v9:
time: 113 us
  starting transfers between devices  37 us (33%)
  blocking collectives  28.7 us (25%)
  waiting for transfers between devices  25.6 us (23%)
  Pallas kernels  18.4 us (16%)
  local copies, waits for them, and re-layouts  1.33 us (1%)
    all_to_all x1, starting transfers between devices, shards(): got = lax.all_to_all(sent, PROV + BIN + ('month',), 0, 0, tiled=True)  22.2 us
    all_to_all x1, blocking collectives, shards(): last = lax.all_to_all(last, PROV, 0, 0, tiled=True)  16.3 us
    all_to_all x1, waiting for transfers between devices, shards(): got = lax.all_to_all(sent, PROV + BIN + ('month',), 0, 0, tiled=True)  15.5 us
    all_to_all x1, blocking collectives, shards(): half_a = lax.all_to_all(spread, BIN, 0, 0, tiled=True)  12.5 us
    all_to_all x1, waiting for transfers between devices, shards(): own_a = lax.all_to_all(pair_a, BIN, 0, 0, tiled=True)  7.71 us
    ppermute x1, starting transfers between devices, shards(): lax.ppermute(send, 'month', swap)  4.63 us
    ppermute x1, starting transfers between devices, shards(): other_a = lax.ppermute(half_a, 'month', swap)  4.36 us
    pallas_call x1, Pallas kernels, shards(): pl.pallas_call(last_product_kernel, out_shape=(jax.ShapeDtypeStruct((n_ou...  4.35 us
  transfers between devices with their start and end apart: 5, of which 5 were waited for; matrix products, arithmetic and copies ran while one was open for 1% of the time, Pallas kernels for 4%

profile of v9, /device:TPU:1, one launch (start us, length us, event | category | flops | bytes accessed | tf_op | source)
XLA Modules:
  0.0 112.9 jit_solution(11488989141862838848)
XLA Ops:
  0.7 1.6 %spread_rows.1 = bf16[512,2,128]{2,1,0:T(2,128)(2,1)} custom-call(bf16[4,64]{1,0:T(4,128)(2,1)} %c_ref.1, bf16[4,64]{1,0:T(4,128)(2,1)} %b_ref.1), custom_call_target="tpu_custom_call" | custom-call | tf_op jit(solution)/shard_map/spread_rows/pallas_call | solution.py:277
  2.2 22.2 %all-to-all-start = ((bf16[512,2,128]{2,1,0:T(2,128)(2,1)}), bf16[512,2,128]{2,1,0:T(2,128)(2,1)S(1)}, u32[]{:S(2)}, u32[]{:S(2)}) async-start(bf16[512,2,128]{2,1,0:T(2,128)(2,1)} %spread_rows.1), calls=%async_computation | async-start | bytes 524288 | tf_op jit(solution)/shard_map/all_to_all | solution.py:289
  24.4 1.8 %keep_tiles.1.kept_ref = bf16[5,128,16,128]{3,2,1,0:T(8,128)(2,1)S(1)} custom-call(bf16[8,128,16,128]{3,2,1,0:T(8,128)(2,1)} %tiles_ref.5), custom_call_target="tpu_custom_call" | custom-call | tf_op jit(solution)/shard_map/keep_tiles/pallas_call | solution.py:300
  26.3 15.5 %all-to-all-done = bf16[512,2,128]{2,1,0:T(2,128)(2,1)S(1)} async-done(((bf16[512,2,128]{2,1,0:T(2,128)(2,1)}), bf16[512,2,128]{2,1,0:T(2,128)(2,1)S(1)}, u32[]{:S(2)}, u32[]{:S(2)}) %all-to-all-start) | async-done | bytes 262176 | tf_op jit(solution)/shard_map/all_to_all | solution.py:289
  41.8 0.4 fusion
  42.4 0.1 reshape.28.c_ref
  42.5 3.3 %first_product.1 = (f32[8,64,128]{2,1,0:T(8,128)S(1)}, f32[8,64,128]{2,1,0:T(8,128)S(1)}) custom-call(s32[8]{0:T(128)S(1)} %clamp_xor_fusion.at_ref, s32[9]{0:T(128)S(1)} %add_clamp_fusion.month_ref, bf16[8,128,16,128]{3,2,1,0:T(8,128)(2,1)} %tiles_ref.5, bf16[5,128,16,128]{3,2,1,0:T(8,128)(2,1)S(1)} %keep_tiles.1.kept_ref, ...), custom_call_target="tpu_custom_call" | custom-call | tf_op jit(solution)/shard_map/first_product/pallas_call | solution.py:320
  45.7 2.5 %collective-permute-start = (f32[8,64,128]{2,1,0:T(8,128)S(1)}, f32[8,64,128]{2,1,0:T(8,128)S(1)}, u32[]{:S(2)}, u32[]{:S(2)}) collective-permute-start(f32[8,64,128]{2,1,0:T(8,128)S(1)} %get-tuple-element.16), channel_id=1, source_target_pairs={{0,8},{8,0},{1,9},{9,1},{2,10},{10,2},{3,11},{11,3},{4,12},{12,4},... | collective-permute-start | bytes 786440 | tf_op jit(solution)/shard_map/ppermute | solution.py:330
  48.2 1.1 collective-permute-done
  49.4 0.7 add.15
  50.1 3.4 %all-to-all-start.1 = ((f32[8,64,128]{2,1,0:T(8,128)}), f32[8,64,128]{2,1,0:T(8,128)S(1)}, u32[]{:S(2)}, u32[]{:S(2)}) async-start(f32[8,64,128]{2,1,0:T(8,128)} %add.15), calls=%async_computation.1 | async-start | bytes 524288 | tf_op jit(solution)/shard_map/all_to_all | solution.py:332
  53.5 3.2 %first_inverse.1 = (f32[64,64]{1,0:T(8,128)S(1)}, f32[64,64]{1,0:T(8,128)S(1)}) custom-call(bf16[256,128]{1,0:T(8,128)(2,1)S(1)} %bitcast.22, bf16[512,128]{1,0:T(8,128)(2,1)S(1)} %bitcast.20), custom_call_target="tpu_custom_call" | custom-call | flops 20000000 | bytes 200000 | tf_op jit(solution)/shard_map/first_inverse/pallas_call | solution.py:335
  56.8 7.7 %all-to-all-done.1.got_ref = f32[8,64,128]{2,1,0:T(8,128)S(1)} async-done(((f32[8,64,128]{2,1,0:T(8,128)}), f32[8,64,128]{2,1,0:T(8,128)S(1)}, u32[]{:S(2)}, u32[]{:S(2)}) %all-to-all-start.1) | async-done | bytes 262176 | tf_op jit(solution)/shard_map/all_to_all | solution.py:332
  64.5 0.3 solve_first.1
  64.8 12.5 %all_to_all.20.a_ref = f32[8,64,128]{2,1,0:T(8,128)S(1)} all-to-all(f32[8,64,128]{2,1,0:T(8,128)S(1)} %get-tuple-element.22), channel_id=1, replica_groups=mesh['zl'=4,'y'=8,'month'=2,'x'=4,'zh'=2] {'x','zh'}, dimensions={0} | all-to-all | bytes 524288 | tf_op jit(solution)/shard_map/all_to_all | solution.py:352
  77.3 4.4 %collective-permute-start.1 = (f32[8,64,128]{2,1,0:T(8,128)S(1)}, f32[8,64,128]{2,1,0:T(8,128)S(1)}, u32[]{:S(2)}, u32[]{:S(2)}) collective-permute-start(f32[8,64,128]{2,1,0:T(8,128)S(1)} %all_to_all.20.a_ref), channel_id=1, source_target_pairs={{0,8},{8,0},{1,9},{9,1},{2,10},{10,2},{3,11},{11,3},{4,12},{12,4},... | collective-permute-start | bytes 786440 | tf_op jit(solution)/shard_map/ppermute | solution.py:353
  81.6 1.1 %collective-permute-done.1.other_ref = f32[8,64,128]{2,1,0:T(8,128)S(1)} collective-permute-done((f32[8,64,128]{2,1,0:T(8,128)S(1)}, f32[8,64,128]{2,1,0:T(8,128)S(1)}, u32[]{:S(2)}, u32[]{:S(2)}) %collective-permute-start.1) | collective-permute-done | bytes 262176 | tf_op jit(solution)/shard_map/ppermute | solution.py:353
  82.8 4.4 %last_product.1 = (f32[64,128]{1,0:T(8,128)S(1)}, f32[9,128]{1,0:T(8,128)S(1)}) custom-call(s32[8]{0:T(128)S(1)} %clamp_xor_fusion.at_ref, s32[9]{0:T(128)S(1)} %add_clamp_fusion.month_ref, bf16[8,128,16,128]{3,2,1,0:T(8,128)(2,1)} %tiles_ref.5, bf16[5,128,16,128]{3,2,1,0:T(8,128)(2,1)S(1)} %keep_tiles.1.kept_ref, f32[8,64,128]{2,1,0:T(8,128)S(1)} %all_to_all.20.a_ref, ...), custom_call_target="tpu_custom_call" | custom-call | tf_op jit(solution)/shard_map/last_product/pallas_call | solution.py:357
  87.1 0.1 pad_maximum_fusion
  87.2 16.3 %all_to_all.21 = f32[32,1,1408]{2,1,0:T(1,128)S(1)} all-to-all(f32[32,1,1408]{2,1,0:T(1,128)S(1)} %pad_maximum_fusion), channel_id=1, replica_groups=mesh['zl'=4,'y'=8,'month'=2,'x'=4,'zh'=2] {'zl','y'}, dimensions={0} | all-to-all | bytes 360448 | tf_op jit(solution)/shard_map/all_to_all | solution.py:372
  103.6 4.6 %collective-permute-start.2 = (f32[1,1280]{1,0:T(1,128)S(1)}, f32[1,1280]{1,0:T(1,128)S(1)}, u32[]{:S(2)}, u32[]{:S(2)}) collective-permute-start(f32[1,1280]{1,0:T(1,128)S(1)} %get-tuple-element.26), channel_id=1, source_target_pairs={{0,8},{8,0},{1,9},{9,1},{2,10},{10,2},{3,11},{11,3},{4,12},{12,4},... | collective-permute-start | bytes 15368 | tf_op jit(solution)/shard_map/ppermute | solution.py:382
  108.2 0.7 copy.21
  108.9 0.1 collective-permute-done.2.swapped_ref
  109.0 3.9 %last_solve.1 = f32[2,64]{1,0:T(2,128)} custom-call(f32[1,1280]{1,0:T(1,128)S(1)} %get-tuple-element.25.keep_ref, f32[1,1280]{1,0:T(1,128)S(1)} %collective-permute-done.2.swapped_ref, f32[64,64]{1,0:T(8,128)S(1)} %get-tuple-element.27.gram_b_ref), custom_call_target="tpu_custom_call" | custom-call | tf_op jit(solution)/shard_map/last_solve/pallas_call | solution.py:377
  (17 shorter events, 0.3 us)
Async XLA Ops:
  0.6 25.6 %copy-start = (s32[8]{0:T(128)S(1)}, s32[8]{0:T(128)}, u32[]{:S(2)}) copy-start(s32[8]{0:T(128)} %param.7) | copy-start | bytes 100
  0.6 25.6 %copy-start.1 = (s32[8]{0:T(128)S(1)}, s32[8]{0:T(128)}, u32[]{:S(2)}) copy-start(s32[8]{0:T(128)} %param.6) | copy-start | bytes 100
  2.2 39.6 %all-to-all-start = ((bf16[512,2,128]{2,1,0:T(2,128)(2,1)}), bf16[512,2,128]{2,1,0:T(2,128)(2,1)S(1)}, u32[]{:S(2)}, u32[]{:S(2)}) async-start(bf16[512,2,128]{2,1,0:T(2,128)(2,1)} %spread_rows.1), calls=%async_computation | async-start | bytes 524288 | tf_op jit(solution)/shard_map/all_to_all | solution.py:289
  45.7 3.6 %collective-permute-start = (f32[8,64,128]{2,1,0:T(8,128)S(1)}, f32[8,64,128]{2,1,0:T(8,128)S(1)}, u32[]{:S(2)}, u32[]{:S(2)}) collective-permute-start(f32[8,64,128]{2,1,0:T(8,128)S(1)} %get-tuple-element.16), channel_id=1, source_target_pairs={{0,8},{8,0},{1,9},{9,1},{2,10},{10,2},{3,11},{11,3},{4,12},{12,4},... | collective-permute-start | bytes 786440 | tf_op jit(solution)/shard_map/ppermute | solution.py:330
  50.1 14.4 %all-to-all-start.1 = ((f32[8,64,128]{2,1,0:T(8,128)}), f32[8,64,128]{2,1,0:T(8,128)S(1)}, u32[]{:S(2)}, u32[]{:S(2)}) async-start(f32[8,64,128]{2,1,0:T(8,128)} %add.15), calls=%async_computation.1 | async-start | bytes 524288 | tf_op jit(solution)/shard_map/all_to_all | solution.py:332
  77.3 5.5 %collective-permute-start.1 = (f32[8,64,128]{2,1,0:T(8,128)S(1)}, f32[8,64,128]{2,1,0:T(8,128)S(1)}, u32[]{:S(2)}, u32[]{:S(2)}) collective-permute-start(f32[8,64,128]{2,1,0:T(8,128)S(1)} %all_to_all.20.a_ref), channel_id=1, source_target_pairs={{0,8},{8,0},{1,9},{9,1},{2,10},{10,2},{3,11},{11,3},{4,12},{12,4},... | collective-permute-start | bytes 786440 | tf_op jit(solution)/shard_map/ppermute | solution.py:353
  103.6 5.4 %collective-permute-start.2 = (f32[1,1280]{1,0:T(1,128)S(1)}, f32[1,1280]{1,0:T(1,128)S(1)}, u32[]{:S(2)}, u32[]{:S(2)}) collective-permute-start(f32[1,1280]{1,0:T(1,128)S(1)} %get-tuple-element.26), channel_id=1, source_target_pairs={{0,8},{8,0},{1,9},{9,1},{2,10},{10,2},{3,11},{11,3},{4,12},{12,4},... | collective-permute-start | bytes 15368 | tf_op jit(solution)/shard_map/ppermute | solution.py:382

commit v10 on v9

--- a/solution.py
+++ b/solution.py
@@ -6,7 +6,7 @@
 from jax.sharding import PartitionSpec as P
 
 MB_DEV = 8
-KEPT = 5
+KEPT = 6
 PB_DEV = 16
 epsilon = 1e-06
 HIGH = lax.Precision.HIGHEST
@@ -327,10 +327,8 @@
         name="first_product",
     )(block_at, month_at, tile_values, kept, slab_c, slab_b)
 
-    pair_a = own_half + lax.ppermute(other_half, "month", swap)
-    twice_b, pairs_c, pair_a = lax.optimization_barrier((twice_b, pairs_c, pair_a))
-    own_a = lax.all_to_all(pair_a, BIN, 0, 0, tiled=True)
-
+    twice_b, pairs_c, own_half, other_half = lax.optimization_barrier((twice_b, pairs_c, own_half, other_half))
+    arrived = lax.ppermute(other_half, "month", swap)
     square = jax.ShapeDtypeStruct((rank, rank), jnp.float32)
     inverse, gram_b = pl.pallas_call(
         first_inverse_kernel,
@@ -339,6 +337,8 @@
         name="first_inverse",
         compiler_params=SMALL,
     )(twice_b, pairs_c)
+    inverse, arrived = lax.optimization_barrier((inverse, arrived))
+    own_a = lax.all_to_all(own_half + arrived, BIN, 0, 0, tiled=True)
     spread, factor_a = pl.pallas_call(
         solve_kernel,
         out_shape=(

time: 113 us -> 115 us (1.018)
  blocking collectives: 28.7 us -> 43.3 us
  waiting for transfers between devices: 25.6 us -> 16.6 us
  starting transfers between devices: 37 us -> 33.6 us
    all_to_all x0 -> x1, blocking collectives: none -> 13.9 us  [shards(): own_a = lax.all_to_all(own_half + arrived, BIN, 0, 0, tiled=True)]
    all_to_all x1 -> x0, waiting for transfers between devices: 7.71 us -> none  [shards(): own_a = lax.all_to_all(pair_a, BIN, 0, 0, tiled=True)]
    all_to_all x1 -> x0, starting transfers between devices: 3.41 us -> none  [shards(): own_a = lax.all_to_all(pair_a, BIN, 0, 0, tiled=True)]
  transfers between devices with their start and end apart: 5 -> 4, of which waited for: 5 -> 3; matrix products, arithmetic and copies ran while one was open for 1% -> 1% of each run, Pallas kernels for 4% -> 5%
where the time goes in v10:
time: 115 us; the launch traced here: 114 us
  blocking collectives  43.3 us (38%)
  starting transfers between devices  33.6 us (29%)
  Pallas kernels  18.2 us (16%)
  waiting for transfers between devices  16.6 us (14%)
  local copies, waits for them, and re-layouts  1.33 us (1%)
    all_to_all x1, starting transfers between devices, shards(): got = lax.all_to_all(sent, PROV + BIN + ('month',), 0, 0, tiled=True)  22.2 us
    all_to_all x1, blocking collectives, shards(): last = lax.all_to_all(last, PROV, 0, 0, tiled=True)  16.9 us
    all_to_all x1, waiting for transfers between devices, shards(): got = lax.all_to_all(sent, PROV + BIN + ('month',), 0, 0, tiled=True)  15.4 us
    all_to_all x1, blocking collectives, shards(): own_a = lax.all_to_all(own_half + arrived, BIN, 0, 0, tiled=True)  13.9 us
    all_to_all x1, blocking collectives, shards(): half_a = lax.all_to_all(spread, BIN, 0, 0, tiled=True)  12.5 us
    ppermute x1, starting transfers between devices, shards(): lax.ppermute(send, 'month', swap)  4.64 us
    ppermute x1, starting transfers between devices, shards(): other_a = lax.ppermute(half_a, 'month', swap)  4.31 us
    pallas_call x1, Pallas kernels, shards(): pl.pallas_call(last_product_kernel, out_shape=(jax.ShapeDtypeStruct((n_ou...  4.11 us
  transfers between devices with their start and end apart: 4, of which 3 were waited for; matrix products, arithmetic and copies ran while one was open for 1% of the time, Pallas kernels for 5%

profile of v10, /device:TPU:1, one launch (start us, length us, event | category | flops | bytes accessed | tf_op | source)
XLA Modules:
  0.0 114.1 jit_solution(2229753703861372295)
XLA Ops:
  0.6 0.0 copy-start
  0.7 1.6 %spread_rows.1 = bf16[512,2,128]{2,1,0:T(2,128)(2,1)} custom-call(bf16[4,64]{1,0:T(4,128)(2,1)} %c_ref.1, bf16[4,64]{1,0:T(4,128)(2,1)} %b_ref.1), custom_call_target="tpu_custom_call" | custom-call | tf_op jit(solution)/shard_map/spread_rows/pallas_call | solution.py:277
  2.2 22.2 %all-to-all-start = ((bf16[512,2,128]{2,1,0:T(2,128)(2,1)}), bf16[512,2,128]{2,1,0:T(2,128)(2,1)S(1)}, u32[]{:S(2)}, u32[]{:S(2)}) async-start(bf16[512,2,128]{2,1,0:T(2,128)(2,1)} %spread_rows.1), calls=%async_computation | async-start | bytes 524288 | tf_op jit(solution)/shard_map/all_to_all | solution.py:289
  24.4 1.9 %keep_tiles.1.kept_ref = bf16[6,128,16,128]{3,2,1,0:T(8,128)(2,1)S(1)} custom-call(bf16[8,128,16,128]{3,2,1,0:T(8,128)(2,1)} %tiles_ref.5), custom_call_target="tpu_custom_call" | custom-call | tf_op jit(solution)/shard_map/keep_tiles/pallas_call | solution.py:300
  26.3 0.1 add_clamp_fusion.month_ref
  26.4 15.4 %all-to-all-done = bf16[512,2,128]{2,1,0:T(2,128)(2,1)S(1)} async-done(((bf16[512,2,128]{2,1,0:T(2,128)(2,1)}), bf16[512,2,128]{2,1,0:T(2,128)(2,1)S(1)}, u32[]{:S(2)}, u32[]{:S(2)}) %all-to-all-start) | async-done | bytes 262176 | tf_op jit(solution)/shard_map/all_to_all | solution.py:289
  41.8 0.4 fusion
  42.4 0.1 reshape.28.c_ref
  42.5 3.1 %first_product.1 = (f32[8,64,128]{2,1,0:T(8,128)S(1)}, f32[8,64,128]{2,1,0:T(8,128)S(1)}) custom-call(s32[8]{0:T(128)S(1)} %clamp_xor_fusion.at_ref, s32[9]{0:T(128)S(1)} %add_clamp_fusion.month_ref, bf16[8,128,16,128]{3,2,1,0:T(8,128)(2,1)} %tiles_ref.5, bf16[6,128,16,128]{3,2,1,0:T(8,128)(2,1)S(1)} %keep_tiles.1.kept_ref, ...), custom_call_target="tpu_custom_call" | custom-call | tf_op jit(solution)/shard_map/first_product/pallas_call | solution.py:320
  45.6 2.5 %collective-permute-start = (f32[8,64,128]{2,1,0:T(8,128)S(1)}, f32[8,64,128]{2,1,0:T(8,128)S(1)}, u32[]{:S(2)}, u32[]{:S(2)}) collective-permute-start(f32[8,64,128]{2,1,0:T(8,128)S(1)} %get-tuple-element.24), channel_id=1, source_target_pairs={{0,8},{8,0},{1,9},{9,1},{2,10},{10,2},{3,11},{11,3},{4,12},{12,4},... | collective-permute-start | bytes 786440 | tf_op jit(solution)/shard_map/ppermute | solution.py:331
  48.1 3.2 %first_inverse.1 = (f32[64,64]{1,0:T(8,128)S(1)}, f32[64,64]{1,0:T(8,128)S(1)}) custom-call(bf16[256,128]{1,0:T(8,128)(2,1)S(1)} %bitcast.22, bf16[512,128]{1,0:T(8,128)(2,1)S(1)} %bitcast.20), custom_call_target="tpu_custom_call" | custom-call | flops 20000000 | bytes 200000 | tf_op jit(solution)/shard_map/first_inverse/pallas_call | solution.py:333
  51.3 0.0 collective-permute-done
  51.4 13.9 %all_to_all.20.got_ref = f32[8,64,128]{2,1,0:T(8,128)S(1)} all-to-all(f32[8,64,128]{2,1,0:T(8,128)S(1)} %add.15), channel_id=1, replica_groups=mesh['zl'=4,'y'=8,'month'=2,'x'=4,'zh'=2] {'x','zh'}, dimensions={0} | all-to-all | bytes 524288 | tf_op jit(solution)/shard_map/all_to_all | solution.py:341
  65.3 0.3 solve_first.1
  65.6 12.5 %all_to_all.21.a_ref = f32[8,64,128]{2,1,0:T(8,128)S(1)} all-to-all(f32[8,64,128]{2,1,0:T(8,128)S(1)} %get-tuple-element.28), channel_id=1, replica_groups=mesh['zl'=4,'y'=8,'month'=2,'x'=4,'zh'=2] {'x','zh'}, dimensions={0} | all-to-all | bytes 524288 | tf_op jit(solution)/shard_map/all_to_all | solution.py:352
  78.1 4.3 %collective-permute-start.1 = (f32[8,64,128]{2,1,0:T(8,128)S(1)}, f32[8,64,128]{2,1,0:T(8,128)S(1)}, u32[]{:S(2)}, u32[]{:S(2)}) collective-permute-start(f32[8,64,128]{2,1,0:T(8,128)S(1)} %all_to_all.21.a_ref), channel_id=1, source_target_pairs={{0,8},{8,0},{1,9},{9,1},{2,10},{10,2},{3,11},{11,3},{4,12},{12,4},... | collective-permute-start | bytes 786440 | tf_op jit(solution)/shard_map/ppermute | solution.py:353
  82.4 1.1 collective-permute-done.1.other_ref
  83.6 4.1 %last_product.1 = (f32[64,128]{1,0:T(8,128)S(1)}, f32[9,128]{1,0:T(8,128)S(1)}) custom-call(s32[8]{0:T(128)S(1)} %clamp_xor_fusion.at_ref, s32[9]{0:T(128)S(1)} %add_clamp_fusion.month_ref, bf16[8,128,16,128]{3,2,1,0:T(8,128)(2,1)} %tiles_ref.5, bf16[6,128,16,128]{3,2,1,0:T(8,128)(2,1)S(1)} %keep_tiles.1.kept_ref, f32[8,64,128]{2,1,0:T(8,128)S(1)} %all_to_all.21.a_ref, ...), custom_call_target="tpu_custom_call" | custom-call | tf_op jit(solution)/shard_map/last_product/pallas_call | solution.py:357
  87.7 0.1 pad_maximum_fusion
  87.8 16.9 %all_to_all.22 = f32[32,1,1408]{2,1,0:T(1,128)S(1)} all-to-all(f32[32,1,1408]{2,1,0:T(1,128)S(1)} %pad_maximum_fusion), channel_id=1, replica_groups=mesh['zl'=4,'y'=8,'month'=2,'x'=4,'zh'=2] {'zl','y'}, dimensions={0} | all-to-all | bytes 360448 | tf_op jit(solution)/shard_map/all_to_all | solution.py:372
  104.8 4.6 %collective-permute-start.2 = (f32[1,1280]{1,0:T(1,128)S(1)}, f32[1,1280]{1,0:T(1,128)S(1)}, u32[]{:S(2)}, u32[]{:S(2)}) collective-permute-start(f32[1,1280]{1,0:T(1,128)S(1)} %get-tuple-element.32), channel_id=1, source_target_pairs={{0,8},{8,0},{1,9},{9,1},{2,10},{10,2},{3,11},{11,3},{4,12},{12,4},... | collective-permute-start | bytes 15368 | tf_op jit(solution)/shard_map/ppermute | solution.py:382
  109.4 0.7 copy.21
  110.1 0.1 collective-permute-done.2.swapped_ref
  110.2 3.9 %last_solve.1 = f32[2,64]{1,0:T(2,128)} custom-call(f32[1,1280]{1,0:T(1,128)S(1)} %get-tuple-element.31.keep_ref, f32[1,1280]{1,0:T(1,128)S(1)} %collective-permute-done.2.swapped_ref, f32[64,64]{1,0:T(8,128)S(1)} %get-tuple-element.33.gram_b_ref), custom_call_target="tpu_custom_call" | custom-call | tf_op jit(solution)/shard_map/last_solve/pallas_call | solution.py:377
  (16 shorter events, 0.3 us)
Async XLA Ops:
  0.6 25.7 %copy-start = (s32[8]{0:T(128)S(1)}, s32[8]{0:T(128)}, u32[]{:S(2)}) copy-start(s32[8]{0:T(128)} %param.7) | copy-start | bytes 100
  0.6 25.8 %copy-start.1 = (s32[8]{0:T(128)S(1)}, s32[8]{0:T(128)}, u32[]{:S(2)}) copy-start(s32[8]{0:T(128)} %param.6) | copy-start | bytes 100
  2.2 39.6 %all-to-all-start = ((bf16[512,2,128]{2,1,0:T(2,128)(2,1)}), bf16[512,2,128]{2,1,0:T(2,128)(2,1)S(1)}, u32[]{:S(2)}, u32[]{:S(2)}) async-start(bf16[512,2,128]{2,1,0:T(2,128)(2,1)} %spread_rows.1), calls=%async_computation | async-start | bytes 524288 | tf_op jit(solution)/shard_map/all_to_all | solution.py:289
  45.6 5.7 %collective-permute-start = (f32[8,64,128]{2,1,0:T(8,128)S(1)}, f32[8,64,128]{2,1,0:T(8,128)S(1)}, u32[]{:S(2)}, u32[]{:S(2)}) collective-permute-start(f32[8,64,128]{2,1,0:T(8,128)S(1)} %get-tuple-element.24), channel_id=1, source_target_pairs={{0,8},{8,0},{1,9},{9,1},{2,10},{10,2},{3,11},{11,3},{4,12},{12,4},... | collective-permute-start | bytes 786440 | tf_op jit(solution)/shard_map/ppermute | solution.py:331
  78.1 5.5 %collective-permute-start.1 = (f32[8,64,128]{2,1,0:T(8,128)S(1)}, f32[8,64,128]{2,1,0:T(8,128)S(1)}, u32[]{:S(2)}, u32[]{:S(2)}) collective-permute-start(f32[8,64,128]{2,1,0:T(8,128)S(1)} %all_to_all.21.a_ref), channel_id=1, source_target_pairs={{0,8},{8,0},{1,9},{9,1},{2,10},{10,2},{3,11},{11,3},{4,12},{12,4},... | collective-permute-start | bytes 786440 | tf_op jit(solution)/shard_map/ppermute | solution.py:353
  104.8 5.4 %collective-permute-start.2 = (f32[1,1280]{1,0:T(1,128)S(1)}, f32[1,1280]{1,0:T(1,128)S(1)}, u32[]{:S(2)}, u32[]{:S(2)}) collective-permute-start(f32[1,1280]{1,0:T(1,128)S(1)} %get-tuple-element.32), channel_id=1, source_target_pairs={{0,8},{8,0},{1,9},{9,1},{2,10},{10,2},{3,11},{11,3},{4,12},{12,4},... | collective-permute-start | bytes 15368 | tf_op jit(solution)/shard_map/ppermute | solution.py:382

commit v11 on v9

--- a/solution.py
+++ b/solution.py
@@ -129,7 +129,7 @@
     return jnp.concatenate([upper, lower], axis=1)
 
 
-def first_product_kernel(at_ref, month_ref, tiles_ref, kept_ref, c_ref, b_ref, own_ref, other_ref, late, sems):
+def first_product_kernel(where_ref, tiles_ref, kept_ref, c_ref, b_ref, own_ref, other_ref, late, sems):
     copies = tile_copies(tiles_ref, late, sems)
     own_ref[...] = jnp.zeros_like(own_ref)
     other_ref[...] = jnp.zeros_like(other_ref)
@@ -142,8 +142,8 @@
     for t, copy in enumerate(copies):
         if copy is not None:
             copy.wait()
-        at = at_ref[t]
-        b = b_ref[month_ref[t]][None]
+        at = where_ref[t]
+        b = b_ref[where_ref[tiles_ref.shape[0] + t]][None]
         for start in range(0, half, size):
             product = dot32(both_halves(kept_ref, late, t, start, size), twice_c, ((1,), (0,)), None)
             product = product.reshape(size, tile_j, -1) * b
@@ -201,22 +201,22 @@
     )
 
 
-def last_product_kernel(at_ref, month_ref, tiles_ref, kept_ref, a_ref, other_ref, b_ref, out_ref, gram_ref, late, sems, turned):
+def last_product_kernel(where_ref, tiles_ref, kept_ref, a_ref, other_ref, b_ref, out_ref, gram_ref, late, sems, turned):
     copies = tile_copies(tiles_ref, late, sems)
     blocks, half, lanes = a_ref.shape
     rank, tile_j, tile_k = lanes // 2, tiles_ref.shape[2], tiles_ref.shape[3]
     size = half // 4
     own, other = (ref[...].reshape(blocks * half, lanes) for ref in (a_ref, other_ref))
     twin = dot32(own, own, ((0,), (0,))) + dot32(other, other, ((0,), (0,)))
-    folded, diagonal = pack_gram(twin[:rank, :rank] + twin[rank:, rank:], month_ref[month_ref.shape[0] - 1])
+    folded, diagonal = pack_gram(twin[:rank, :rank] + twin[rank:, rank:], lax.axis_index("month"))
     gram_ref[: folded.shape[0]] = folded
     gram_ref[folded.shape[0] :] = diagonal
     total = None
     for t, copy in enumerate(copies):
         if copy is not None:
             copy.wait()
-        at = at_ref[t]
-        b = b_ref[month_ref[t]][None]
+        at = where_ref[t]
+        b = b_ref[where_ref[tiles_ref.shape[0] + t]][None]
         for start in range(0, half, size):
             rows = pl.ds(start, size)
             a = jnp.where(at < blocks, a_ref[at % blocks, rows], other_ref[at % blocks, rows])
@@ -313,19 +313,19 @@
     ]
     half = tile_i // 2
     prov_at = jnp.clip(prov_block, 0, PB_DEV - 1)
-    month_at = jnp.clip(jnp.concatenate([month_block, month[None]]), 0, MB_DEV - 1)
+    month_at = jnp.clip(month_block, 0, MB_DEV - 1)
     swap = [(i, n_month - 1 - i) for i in range(n_month)]
-    block_at = prov_at ^ (month * n_bin)
+    where = jnp.concatenate([prov_at ^ (month * n_bin), month_at])
     sums = jax.ShapeDtypeStruct((n_bin, half, 2 * rank), jnp.float32)
     own_half, other_half = pl.pallas_call(
         first_product_kernel,
         out_shape=(sums, sums),
-        in_specs=[smem, smem, hbm, vmem, vmem, vmem],
+        in_specs=[smem, hbm, vmem, vmem, vmem],
         out_specs=(vmem, vmem),
         scratch_shapes=tile_scratch,
         compiler_params=LARGE,
         name="first_product",
-    )(block_at, month_at, tile_values, kept, slab_c, slab_b)
+    )(where, tile_values, kept, slab_c, slab_b)
 
     pair_a = own_half + lax.ppermute(other_half, "month", swap)
     twice_b, pairs_c, pair_a = lax.optimization_barrier((twice_b, pairs_c, pair_a))
@@ -360,12 +360,12 @@
             jax.ShapeDtypeStruct((n_out, out_rows * rank), jnp.float32),
             jax.ShapeDtypeStruct((rank // 8 + 1, 2 * rank), jnp.float32),
         ),
-        in_specs=[smem, smem, hbm, vmem, vmem, vmem, vmem],
+        in_specs=[smem, hbm, vmem, vmem, vmem, vmem],
         out_specs=(vmem, vmem),
         scratch_shapes=tile_scratch + [pltpu.VMEM((tile_k, rank), jnp.float32)],
         compiler_params=LARGE,
         name="last_product",
-    )(block_at, month_at, tile_values, kept, half_a, other_a, slab_b)
+    )(where, tile_values, kept, half_a, other_a, slab_b)
 
     sent_gram = jnp.broadcast_to(packed.reshape(1, 1, -1), (n_prov, 1, packed.size))
     last = jnp.concatenate([partial_c.reshape(n_prov, 1, -1), sent_gram], axis=2)

time: 113 us -> 113 us (level)
  no operation moved by 1% of the time
where the time goes in v11:
time: 113 us
  starting transfers between devices  37.1 us (33%)
  blocking collectives  28.8 us (25%)
  waiting for transfers between devices  25.6 us (23%)
  Pallas kernels  18.4 us (16%)
  local copies, waits for them, and re-layouts  1.33 us (1%)
    all_to_all x1, starting transfers between devices, shards(): got = lax.all_to_all(sent, PROV + BIN + ('month',), 0, 0, tiled=True)  22.2 us
    all_to_all x1, blocking collectives, shards(): last = lax.all_to_all(last, PROV, 0, 0, tiled=True)  16.3 us
    all_to_all x1, waiting for transfers between devices, shards(): got = lax.all_to_all(sent, PROV + BIN + ('month',), 0, 0, tiled=True)  15.5 us
    all_to_all x1, blocking collectives, shards(): half_a = lax.all_to_all(spread, BIN, 0, 0, tiled=True)  12.5 us
    all_to_all x1, waiting for transfers between devices, shards(): own_a = lax.all_to_all(pair_a, BIN, 0, 0, tiled=True)  7.75 us
    ppermute x1, starting transfers between devices, shards(): lax.ppermute(send, 'month', swap)  4.64 us
    pallas_call x1, Pallas kernels, shards(): pl.pallas_call(last_product_kernel, out_shape=(jax.ShapeDtypeStruct((n_ou...  4.36 us
    ppermute x1, starting transfers between devices, shards(): other_a = lax.ppermute(half_a, 'month', swap)  4.32 us
  transfers between devices with their start and end apart: 5, of which 5 were waited for; matrix products, arithmetic and copies ran while one was open for 1% of the time, Pallas kernels for 4%

profile of v11, /device:TPU:1, one launch (start us, length us, event | category | flops | bytes accessed | tf_op | source)
XLA Modules:
  0.0 112.9 jit_solution(1177080189266795518)
XLA Ops:
  0.7 1.6 %spread_rows.1 = bf16[512,2,128]{2,1,0:T(2,128)(2,1)} custom-call(bf16[4,64]{1,0:T(4,128)(2,1)} %c_ref.1, bf16[4,64]{1,0:T(4,128)(2,1)} %b_ref.1), custom_call_target="tpu_custom_call" | custom-call | tf_op jit(solution)/shard_map/spread_rows/pallas_call | solution.py:277
  2.2 22.2 %all-to-all-start = ((bf16[512,2,128]{2,1,0:T(2,128)(2,1)}), bf16[512,2,128]{2,1,0:T(2,128)(2,1)S(1)}, u32[]{:S(2)}, u32[]{:S(2)}) async-start(bf16[512,2,128]{2,1,0:T(2,128)(2,1)} %spread_rows.1), calls=%async_computation | async-start | bytes 524288 | tf_op jit(solution)/shard_map/all_to_all | solution.py:289
  24.4 1.8 %keep_tiles.1.kept_ref = bf16[5,128,16,128]{3,2,1,0:T(8,128)(2,1)S(1)} custom-call(bf16[8,128,16,128]{3,2,1,0:T(8,128)(2,1)} %tiles_ref.5), custom_call_target="tpu_custom_call" | custom-call | tf_op jit(solution)/shard_map/keep_tiles/pallas_call | solution.py:300
  26.3 15.5 %all-to-all-done = bf16[512,2,128]{2,1,0:T(2,128)(2,1)S(1)} async-done(((bf16[512,2,128]{2,1,0:T(2,128)(2,1)}), bf16[512,2,128]{2,1,0:T(2,128)(2,1)S(1)}, u32[]{:S(2)}, u32[]{:S(2)}) %all-to-all-start) | async-done | bytes 262176 | tf_op jit(solution)/shard_map/all_to_all | solution.py:289
  41.8 0.4 fusion
  42.3 0.1 reshape.28.c_ref
  42.4 3.3 %first_product.1 = (f32[8,64,128]{2,1,0:T(8,128)S(1)}, f32[8,64,128]{2,1,0:T(8,128)S(1)}) custom-call(s32[16]{0:T(128)S(1)} %pad_add_fusion.where_ref, bf16[8,128,16,128]{3,2,1,0:T(8,128)(2,1)} %tiles_ref.5, bf16[5,128,16,128]{3,2,1,0:T(8,128)(2,1)S(1)} %keep_tiles.1.kept_ref, bf16[128,64]{1,0:T(8,128)(2,1)S(1)} %reshape.28.c_ref, ...), custom_call_target="tpu_custom_call" | custom-call | tf_op jit(solution)/shard_map/first_product/pallas_call | solution.py:320
  45.7 2.5 %collective-permute-start = (f32[8,64,128]{2,1,0:T(8,128)S(1)}, f32[8,64,128]{2,1,0:T(8,128)S(1)}, u32[]{:S(2)}, u32[]{:S(2)}) collective-permute-start(f32[8,64,128]{2,1,0:T(8,128)S(1)} %get-tuple-element.16), channel_id=1, source_target_pairs={{0,8},{8,0},{1,9},{9,1},{2,10},{10,2},{3,11},{11,3},{4,12},{12,4},... | collective-permute-start | bytes 786440 | tf_op jit(solution)/shard_map/ppermute | solution.py:330
  48.2 1.1 collective-permute-done
  49.3 0.7 add.15
  50.1 3.4 %all-to-all-start.1 = ((f32[8,64,128]{2,1,0:T(8,128)}), f32[8,64,128]{2,1,0:T(8,128)S(1)}, u32[]{:S(2)}, u32[]{:S(2)}) async-start(f32[8,64,128]{2,1,0:T(8,128)} %add.15), calls=%async_computation.1 | async-start | bytes 524288 | tf_op jit(solution)/shard_map/all_to_all | solution.py:332
  53.5 3.2 %first_inverse.1 = (f32[64,64]{1,0:T(8,128)S(1)}, f32[64,64]{1,0:T(8,128)S(1)}) custom-call(bf16[256,128]{1,0:T(8,128)(2,1)S(1)} %bitcast.21, bf16[512,128]{1,0:T(8,128)(2,1)S(1)} %bitcast.19), custom_call_target="tpu_custom_call" | custom-call | flops 20000000 | bytes 200000 | tf_op jit(solution)/shard_map/first_inverse/pallas_call | solution.py:335
  56.7 7.7 %all-to-all-done.1.got_ref = f32[8,64,128]{2,1,0:T(8,128)S(1)} async-done(((f32[8,64,128]{2,1,0:T(8,128)}), f32[8,64,128]{2,1,0:T(8,128)S(1)}, u32[]{:S(2)}, u32[]{:S(2)}) %all-to-all-start.1) | async-done | bytes 262176 | tf_op jit(solution)/shard_map/all_to_all | solution.py:332
  64.5 0.3 solve_first.1
  64.8 12.5 %all_to_all.20.a_ref = f32[8,64,128]{2,1,0:T(8,128)S(1)} all-to-all(f32[8,64,128]{2,1,0:T(8,128)S(1)} %get-tuple-element.22), channel_id=1, replica_groups=mesh['zl'=4,'y'=8,'month'=2,'x'=4,'zh'=2] {'x','zh'}, dimensions={0} | all-to-all | bytes 524288 | tf_op jit(solution)/shard_map/all_to_all | solution.py:352
  77.3 4.3 %collective-permute-start.1 = (f32[8,64,128]{2,1,0:T(8,128)S(1)}, f32[8,64,128]{2,1,0:T(8,128)S(1)}, u32[]{:S(2)}, u32[]{:S(2)}) collective-permute-start(f32[8,64,128]{2,1,0:T(8,128)S(1)} %all_to_all.20.a_ref), channel_id=1, source_target_pairs={{0,8},{8,0},{1,9},{9,1},{2,10},{10,2},{3,11},{11,3},{4,12},{12,4},... | collective-permute-start | bytes 786440 | tf_op jit(solution)/shard_map/ppermute | solution.py:353
  81.6 1.1 %collective-permute-done.1.other_ref = f32[8,64,128]{2,1,0:T(8,128)S(1)} collective-permute-done((f32[8,64,128]{2,1,0:T(8,128)S(1)}, f32[8,64,128]{2,1,0:T(8,128)S(1)}, u32[]{:S(2)}, u32[]{:S(2)}) %collective-permute-start.1) | collective-permute-done | bytes 262176 | tf_op jit(solution)/shard_map/ppermute | solution.py:353
  82.7 4.4 %last_product.1 = (f32[64,128]{1,0:T(8,128)S(1)}, f32[9,128]{1,0:T(8,128)S(1)}) custom-call(s32[16]{0:T(128)S(1)} %pad_add_fusion.where_ref, bf16[8,128,16,128]{3,2,1,0:T(8,128)(2,1)} %tiles_ref.5, bf16[5,128,16,128]{3,2,1,0:T(8,128)(2,1)S(1)} %keep_tiles.1.kept_ref, f32[8,64,128]{2,1,0:T(8,128)S(1)} %all_to_all.20.a_ref, ...), custom_call_target="tpu_custom_call" | custom-call | tf_op jit(solution)/shard_map/last_product/pallas_call | solution.py:357
  87.1 0.1 pad_maximum_fusion
  87.2 16.3 %all_to_all.21 = f32[32,1,1408]{2,1,0:T(1,128)S(1)} all-to-all(f32[32,1,1408]{2,1,0:T(1,128)S(1)} %pad_maximum_fusion), channel_id=1, replica_groups=mesh['zl'=4,'y'=8,'month'=2,'x'=4,'zh'=2] {'zl','y'}, dimensions={0} | all-to-all | bytes 360448 | tf_op jit(solution)/shard_map/all_to_all | solution.py:372
  103.6 4.6 %collective-permute-start.2 = (f32[1,1280]{1,0:T(1,128)S(1)}, f32[1,1280]{1,0:T(1,128)S(1)}, u32[]{:S(2)}, u32[]{:S(2)}) collective-permute-start(f32[1,1280]{1,0:T(1,128)S(1)} %get-tuple-element.26), channel_id=1, source_target_pairs={{0,8},{8,0},{1,9},{9,1},{2,10},{10,2},{3,11},{11,3},{4,12},{12,4},... | collective-permute-start | bytes 15368 | tf_op jit(solution)/shard_map/ppermute | solution.py:382
  108.2 0.7 copy.21
  108.9 0.1 collective-permute-done.2.swapped_ref
  109.0 3.9 %last_solve.1 = f32[2,64]{1,0:T(2,128)} custom-call(f32[1,1280]{1,0:T(1,128)S(1)} %get-tuple-element.25.keep_ref, f32[1,1280]{1,0:T(1,128)S(1)} %collective-permute-done.2.swapped_ref, f32[64,64]{1,0:T(8,128)S(1)} %get-tuple-element.27.gram_b_ref), custom_call_target="tpu_custom_call" | custom-call | tf_op jit(solution)/shard_map/last_solve/pallas_call | solution.py:377
  (17 shorter events, 0.3 us)
Async XLA Ops:
  0.6 25.5 %copy-start.1 = (s32[8]{0:T(128)S(1)}, s32[8]{0:T(128)}, u32[]{:S(2)}) copy-start(s32[8]{0:T(128)} %param.7) | copy-start | bytes 100
  0.6 25.5 %copy-start = (s32[8]{0:T(128)S(1)}, s32[8]{0:T(128)}, u32[]{:S(2)}) copy-start(s32[8]{0:T(128)} %param.6) | copy-start | bytes 100
  2.2 39.5 %all-to-all-start = ((bf16[512,2,128]{2,1,0:T(2,128)(2,1)}), bf16[512,2,128]{2,1,0:T(2,128)(2,1)S(1)}, u32[]{:S(2)}, u32[]{:S(2)}) async-start(bf16[512,2,128]{2,1,0:T(2,128)(2,1)} %spread_rows.1), calls=%async_computation | async-start | bytes 524288 | tf_op jit(solution)/shard_map/all_to_all | solution.py:289
  45.7 3.7 %collective-permute-start = (f32[8,64,128]{2,1,0:T(8,128)S(1)}, f32[8,64,128]{2,1,0:T(8,128)S(1)}, u32[]{:S(2)}, u32[]{:S(2)}) collective-permute-start(f32[8,64,128]{2,1,0:T(8,128)S(1)} %get-tuple-element.16), channel_id=1, source_target_pairs={{0,8},{8,0},{1,9},{9,1},{2,10},{10,2},{3,11},{11,3},{4,12},{12,4},... | collective-permute-start | bytes 786440 | tf_op jit(solution)/shard_map/ppermute | solution.py:330
  50.1 14.4 %all-to-all-start.1 = ((f32[8,64,128]{2,1,0:T(8,128)}), f32[8,64,128]{2,1,0:T(8,128)S(1)}, u32[]{:S(2)}, u32[]{:S(2)}) async-start(f32[8,64,128]{2,1,0:T(8,128)} %add.15), calls=%async_computation.1 | async-start | bytes 524288 | tf_op jit(solution)/shard_map/all_to_all | solution.py:332
  77.3 5.5 %collective-permute-start.1 = (f32[8,64,128]{2,1,0:T(8,128)S(1)}, f32[8,64,128]{2,1,0:T(8,128)S(1)}, u32[]{:S(2)}, u32[]{:S(2)}) collective-permute-start(f32[8,64,128]{2,1,0:T(8,128)S(1)} %all_to_all.20.a_ref), channel_id=1, source_target_pairs={{0,8},{8,0},{1,9},{9,1},{2,10},{10,2},{3,11},{11,3},{4,12},{12,4},... | collective-permute-start | bytes 786440 | tf_op jit(solution)/shard_map/ppermute | solution.py:353
  103.6 5.4 %collective-permute-start.2 = (f32[1,1280]{1,0:T(1,128)S(1)}, f32[1,1280]{1,0:T(1,128)S(1)}, u32[]{:S(2)}, u32[]{:S(2)}) collective-permute-start(f32[1,1280]{1,0:T(1,128)S(1)} %get-tuple-element.26), channel_id=1, source_target_pairs={{0,8},{8,0},{1,9},{9,1},{2,10},{10,2},{3,11},{11,3},{4,12},{12,4},... | collective-permute-start | bytes 15368 | tf_op jit(solution)/shard_map/ppermute | solution.py:382

commit v12 on v11

--- a/solution.py
+++ b/solution.py
@@ -143,7 +143,7 @@
         if copy is not None:
             copy.wait()
         at = where_ref[t]
-        b = b_ref[where_ref[tiles_ref.shape[0] + t]][None]
+        b = b_ref[where_ref[tiles_ref.shape[0] + t]].astype(jnp.float32)[None]
         for start in range(0, half, size):
             product = dot32(both_halves(kept_ref, late, t, start, size), twice_c, ((1,), (0,)), None)
             product = product.reshape(size, tile_j, -1) * b
@@ -216,7 +216,7 @@
         if copy is not None:
             copy.wait()
         at = where_ref[t]
-        b = b_ref[where_ref[tiles_ref.shape[0] + t]][None]
+        b = b_ref[where_ref[tiles_ref.shape[0] + t]].astype(jnp.float32)[None]
         for start in range(0, half, size):
             rows = pl.ds(start, size)
             a = jnp.where(at < blocks, a_ref[at % blocks, rows], other_ref[at % blocks, rows])
@@ -294,7 +294,7 @@
     slab_pairs = lax.dynamic_slice_in_dim(pairs_c, bin_at * (tile_k // c_rows), tile_k // c_rows, 0)
     slab_c = slab_pairs.reshape(tile_k, rank)
     slab_b = lax.dynamic_slice_in_dim(twice_b, month * (MB_DEV * tile_j), MB_DEV * tile_j, 0)
-    slab_b = slab_b.astype(jnp.float32).reshape(MB_DEV, tile_j, c_rows * rank)
+    slab_b = slab_b.reshape(MB_DEV, tile_j, c_rows * rank)
 
     smem, vmem, hbm = (pl.BlockSpec(memory_space=space) for space in (pltpu.SMEM, pltpu.VMEM, pl.ANY))
     kept = pl.pallas_call(

time: 113 us -> 113 us (level)
  no operation moved by 1% of the time
where the time goes in v12:
time: 113 us
  starting transfers between devices  37 us (33%)
  blocking collectives  28.8 us (25%)
  waiting for transfers between devices  25.6 us (23%)
  Pallas kernels  18.4 us (16%)
  local copies, waits for them, and re-layouts  1.32 us (1%)
    all_to_all x1, starting transfers between devices, shards(): got = lax.all_to_all(sent, PROV + BIN + ('month',), 0, 0, tiled=True)  22.2 us
    all_to_all x1, blocking collectives, shards(): last = lax.all_to_all(last, PROV, 0, 0, tiled=True)  16.3 us
    all_to_all x1, waiting for transfers between devices, shards(): got = lax.all_to_all(sent, PROV + BIN + ('month',), 0, 0, tiled=True)  15.5 us
    all_to_all x1, blocking collectives, shards(): half_a = lax.all_to_all(spread, BIN, 0, 0, tiled=True)  12.5 us
    all_to_all x1, waiting for transfers between devices, shards(): own_a = lax.all_to_all(pair_a, BIN, 0, 0, tiled=True)  7.76 us
    ppermute x1, starting transfers between devices, shards(): lax.ppermute(send, 'month', swap)  4.63 us
    pallas_call x1, Pallas kernels, shards(): pl.pallas_call(last_product_kernel, out_shape=(jax.ShapeDtypeStruct((n_ou...  4.35 us
    ppermute x1, starting transfers between devices, shards(): other_a = lax.ppermute(half_a, 'month', swap)  4.31 us
  transfers between devices with their start and end apart: 5, of which 5 were waited for; matrix products, arithmetic and copies ran while one was open for 1% of the time, Pallas kernels for 4%

profile of v12, /device:TPU:1, one launch (start us, length us, event | category | flops | bytes accessed | tf_op | source)
XLA Modules:
  0.0 112.9 jit_solution(2409699746220928947)
XLA Ops:
  0.7 1.6 %spread_rows.1 = bf16[512,2,128]{2,1,0:T(2,128)(2,1)} custom-call(bf16[4,64]{1,0:T(4,128)(2,1)} %c_ref.1, bf16[4,64]{1,0:T(4,128)(2,1)} %b_ref.1), custom_call_target="tpu_custom_call" | custom-call | tf_op jit(solution)/shard_map/spread_rows/pallas_call | solution.py:277
  2.2 22.2 %all-to-all-start = ((bf16[512,2,128]{2,1,0:T(2,128)(2,1)}), bf16[512,2,128]{2,1,0:T(2,128)(2,1)S(1)}, u32[]{:S(2)}, u32[]{:S(2)}) async-start(bf16[512,2,128]{2,1,0:T(2,128)(2,1)} %spread_rows.1), calls=%async_computation | async-start | bytes 524288 | tf_op jit(solution)/shard_map/all_to_all | solution.py:289
  24.4 1.8 %keep_tiles.1.kept_ref = bf16[5,128,16,128]{3,2,1,0:T(8,128)(2,1)S(1)} custom-call(bf16[8,128,16,128]{3,2,1,0:T(8,128)(2,1)} %tiles_ref.5), custom_call_target="tpu_custom_call" | custom-call | tf_op jit(solution)/shard_map/keep_tiles/pallas_call | solution.py:300
  26.3 15.5 %all-to-all-done = bf16[512,2,128]{2,1,0:T(2,128)(2,1)S(1)} async-done(((bf16[512,2,128]{2,1,0:T(2,128)(2,1)}), bf16[512,2,128]{2,1,0:T(2,128)(2,1)S(1)}, u32[]{:S(2)}, u32[]{:S(2)}) %all-to-all-start) | async-done | bytes 262176 | tf_op jit(solution)/shard_map/all_to_all | solution.py:289
  41.8 0.4 fusion
  42.3 0.1 reshape.26.c_ref
  42.4 3.3 %first_product.1 = (f32[8,64,128]{2,1,0:T(8,128)S(1)}, f32[8,64,128]{2,1,0:T(8,128)S(1)}) custom-call(s32[16]{0:T(128)S(1)} %pad_add_fusion.where_ref, bf16[8,128,16,128]{3,2,1,0:T(8,128)(2,1)} %tiles_ref.5, bf16[5,128,16,128]{3,2,1,0:T(8,128)(2,1)S(1)} %keep_tiles.1.kept_ref, bf16[128,64]{1,0:T(8,128)(2,1)S(1)} %reshape.26.c_ref, ...), custom_call_target="tpu_custom_call" | custom-call | tf_op jit(solution)/shard_map/first_product/pallas_call | solution.py:320
  45.6 2.5 %collective-permute-start = (f32[8,64,128]{2,1,0:T(8,128)S(1)}, f32[8,64,128]{2,1,0:T(8,128)S(1)}, u32[]{:S(2)}, u32[]{:S(2)}) collective-permute-start(f32[8,64,128]{2,1,0:T(8,128)S(1)} %get-tuple-element.16), channel_id=1, source_target_pairs={{0,8},{8,0},{1,9},{9,1},{2,10},{10,2},{3,11},{11,3},{4,12},{12,4},... | collective-permute-start | bytes 786440 | tf_op jit(solution)/shard_map/ppermute | solution.py:330
  48.2 1.1 collective-permute-done
  49.3 0.7 add.15
  50.1 3.4 %all-to-all-start.1 = ((f32[8,64,128]{2,1,0:T(8,128)}), f32[8,64,128]{2,1,0:T(8,128)S(1)}, u32[]{:S(2)}, u32[]{:S(2)}) async-start(f32[8,64,128]{2,1,0:T(8,128)} %add.15), calls=%async_computation.1 | async-start | bytes 524288 | tf_op jit(solution)/shard_map/all_to_all | solution.py:332
  53.5 3.2 %first_inverse.1 = (f32[64,64]{1,0:T(8,128)S(1)}, f32[64,64]{1,0:T(8,128)S(1)}) custom-call(bf16[256,128]{1,0:T(8,128)(2,1)S(1)} %bitcast.20, bf16[512,128]{1,0:T(8,128)(2,1)S(1)} %bitcast.18), custom_call_target="tpu_custom_call" | custom-call | flops 20000000 | bytes 200000 | tf_op jit(solution)/shard_map/first_inverse/pallas_call | solution.py:335
  56.7 7.8 %all-to-all-done.1.got_ref = f32[8,64,128]{2,1,0:T(8,128)S(1)} async-done(((f32[8,64,128]{2,1,0:T(8,128)}), f32[8,64,128]{2,1,0:T(8,128)S(1)}, u32[]{:S(2)}, u32[]{:S(2)}) %all-to-all-start.1) | async-done | bytes 262176 | tf_op jit(solution)/shard_map/all_to_all | solution.py:332
  64.5 0.3 solve_first.1
  64.8 12.5 %all_to_all.20.a_ref = f32[8,64,128]{2,1,0:T(8,128)S(1)} all-to-all(f32[8,64,128]{2,1,0:T(8,128)S(1)} %get-tuple-element.22), channel_id=1, replica_groups=mesh['zl'=4,'y'=8,'month'=2,'x'=4,'zh'=2] {'x','zh'}, dimensions={0} | all-to-all | bytes 524288 | tf_op jit(solution)/shard_map/all_to_all | solution.py:352
  77.3 4.3 %collective-permute-start.1 = (f32[8,64,128]{2,1,0:T(8,128)S(1)}, f32[8,64,128]{2,1,0:T(8,128)S(1)}, u32[]{:S(2)}, u32[]{:S(2)}) collective-permute-start(f32[8,64,128]{2,1,0:T(8,128)S(1)} %all_to_all.20.a_ref), channel_id=1, source_target_pairs={{0,8},{8,0},{1,9},{9,1},{2,10},{10,2},{3,11},{11,3},{4,12},{12,4},... | collective-permute-start | bytes 786440 | tf_op jit(solution)/shard_map/ppermute | solution.py:353
  81.6 1.1 %collective-permute-done.1.other_ref = f32[8,64,128]{2,1,0:T(8,128)S(1)} collective-permute-done((f32[8,64,128]{2,1,0:T(8,128)S(1)}, f32[8,64,128]{2,1,0:T(8,128)S(1)}, u32[]{:S(2)}, u32[]{:S(2)}) %collective-permute-start.1) | collective-permute-done | bytes 262176 | tf_op jit(solution)/shard_map/ppermute | solution.py:353
  82.7 4.4 %last_product.1 = (f32[64,128]{1,0:T(8,128)S(1)}, f32[9,128]{1,0:T(8,128)S(1)}) custom-call(s32[16]{0:T(128)S(1)} %pad_add_fusion.where_ref, bf16[8,128,16,128]{3,2,1,0:T(8,128)(2,1)} %tiles_ref.5, bf16[5,128,16,128]{3,2,1,0:T(8,128)(2,1)S(1)} %keep_tiles.1.kept_ref, f32[8,64,128]{2,1,0:T(8,128)S(1)} %all_to_all.20.a_ref, ...), custom_call_target="tpu_custom_call" | custom-call | tf_op jit(solution)/shard_map/last_product/pallas_call | solution.py:357
  87.1 0.1 pad_maximum_fusion
  87.2 16.3 %all_to_all.21 = f32[32,1,1408]{2,1,0:T(1,128)S(1)} all-to-all(f32[32,1,1408]{2,1,0:T(1,128)S(1)} %pad_maximum_fusion), channel_id=1, replica_groups=mesh['zl'=4,'y'=8,'month'=2,'x'=4,'zh'=2] {'zl','y'}, dimensions={0} | all-to-all | bytes 360448 | tf_op jit(solution)/shard_map/all_to_all | solution.py:372
  103.6 4.6 %collective-permute-start.2 = (f32[1,1280]{1,0:T(1,128)S(1)}, f32[1,1280]{1,0:T(1,128)S(1)}, u32[]{:S(2)}, u32[]{:S(2)}) collective-permute-start(f32[1,1280]{1,0:T(1,128)S(1)} %get-tuple-element.26), channel_id=1, source_target_pairs={{0,8},{8,0},{1,9},{9,1},{2,10},{10,2},{3,11},{11,3},{4,12},{12,4},... | collective-permute-start | bytes 15368 | tf_op jit(solution)/shard_map/ppermute | solution.py:382
  108.2 0.7 copy.21
  108.9 0.1 collective-permute-done.2.swapped_ref
  109.0 3.9 %last_solve.1 = f32[2,64]{1,0:T(2,128)} custom-call(f32[1,1280]{1,0:T(1,128)S(1)} %get-tuple-element.25.keep_ref, f32[1,1280]{1,0:T(1,128)S(1)} %collective-permute-done.2.swapped_ref, f32[64,64]{1,0:T(8,128)S(1)} %get-tuple-element.27.gram_b_ref), custom_call_target="tpu_custom_call" | custom-call | tf_op jit(solution)/shard_map/last_solve/pallas_call | solution.py:377
  (16 shorter events, 0.3 us)
Async XLA Ops:
  0.6 25.5 %copy-start.1 = (s32[8]{0:T(128)S(1)}, s32[8]{0:T(128)}, u32[]{:S(2)}) copy-start(s32[8]{0:T(128)} %param.7) | copy-start | bytes 100
  0.6 25.5 %copy-start = (s32[8]{0:T(128)S(1)}, s32[8]{0:T(128)}, u32[]{:S(2)}) copy-start(s32[8]{0:T(128)} %param.6) | copy-start | bytes 100
  2.2 39.5 %all-to-all-start = ((bf16[512,2,128]{2,1,0:T(2,128)(2,1)}), bf16[512,2,128]{2,1,0:T(2,128)(2,1)S(1)}, u32[]{:S(2)}, u32[]{:S(2)}) async-start(bf16[512,2,128]{2,1,0:T(2,128)(2,1)} %spread_rows.1), calls=%async_computation | async-start | bytes 524288 | tf_op jit(solution)/shard_map/all_to_all | solution.py:289
  45.6 3.7 %collective-permute-start = (f32[8,64,128]{2,1,0:T(8,128)S(1)}, f32[8,64,128]{2,1,0:T(8,128)S(1)}, u32[]{:S(2)}, u32[]{:S(2)}) collective-permute-start(f32[8,64,128]{2,1,0:T(8,128)S(1)} %get-tuple-element.16), channel_id=1, source_target_pairs={{0,8},{8,0},{1,9},{9,1},{2,10},{10,2},{3,11},{11,3},{4,12},{12,4},... | collective-permute-start | bytes 786440 | tf_op jit(solution)/shard_map/ppermute | solution.py:330
  50.1 14.4 %all-to-all-start.1 = ((f32[8,64,128]{2,1,0:T(8,128)}), f32[8,64,128]{2,1,0:T(8,128)S(1)}, u32[]{:S(2)}, u32[]{:S(2)}) async-start(f32[8,64,128]{2,1,0:T(8,128)} %add.15), calls=%async_computation.1 | async-start | bytes 524288 | tf_op jit(solution)/shard_map/all_to_all | solution.py:332
  77.3 5.5 %collective-permute-start.1 = (f32[8,64,128]{2,1,0:T(8,128)S(1)}, f32[8,64,128]{2,1,0:T(8,128)S(1)}, u32[]{:S(2)}, u32[]{:S(2)}) collective-permute-start(f32[8,64,128]{2,1,0:T(8,128)S(1)} %all_to_all.20.a_ref), channel_id=1, source_target_pairs={{0,8},{8,0},{1,9},{9,1},{2,10},{10,2},{3,11},{11,3},{4,12},{12,4},... | collective-permute-start | bytes 786440 | tf_op jit(solution)/shard_map/ppermute | solution.py:353
  103.6 5.4 %collective-permute-start.2 = (f32[1,1280]{1,0:T(1,128)S(1)}, f32[1,1280]{1,0:T(1,128)S(1)}, u32[]{:S(2)}, u32[]{:S(2)}) collective-permute-start(f32[1,1280]{1,0:T(1,128)S(1)} %get-tuple-element.26), channel_id=1, source_target_pairs={{0,8},{8,0},{1,9},{9,1},{2,10},{10,2},{3,11},{11,3},{4,12},{12,4},... | collective-permute-start | bytes 15368 | tf_op jit(solution)/shard_map/ppermute | solution.py:382
